TPU v7x, 128 devices: a whole 4x4x4 slice. The times are simulated.
128 devices in a mesh: dp: 8 (over z, core), seq: 16 (over y, x).
Axes of the slice: x: 4, y: 4, z: 4, core: 2. Of those that a mesh axis runs over, the one named last changes fastest.
Arguments:
- video_projected: bfloat16 [8, 3072, 3, 4096], P('dp', 'seq'), may hold values from -6 to 6
- text_projected: bfloat16 [8, 256, 3, 4096], P('dp', 'seq'), may hold values from -6 to 6
- head_live: int32 [32], replicated, may hold values from 0 to 1, as said below
- text_valid: int32 [8, 256], P('dp'), may hold values from 0 to 1, as said below
- text_weight: bfloat16 [4096, 3072], P('seq', 'dp'), may hold values from -0.109375 to 0.109375
- text_cotangent: bfloat16 [8, 256, 3072], P('dp', 'seq'), may hold values from -6 to 6
Outputs:
- video_attended: bfloat16 [8, 3072, 4096], P('dp', 'seq')
- text_output: bfloat16 [8, 256, 3072], P('dp', 'seq')
- weight_gradient: float32 [4096, 3072], P('seq', 'dp')
Inputs may be any that keep to these rules, and one draw needn't show every extreme that they name: `head_live`: exactly 24 entries are 1. `text_valid`: in each window the valid text tokens are a prefix of 64 or more tokens.
All inputs are finite; a program needn't handle non-finite values.
Results may differ from a plain program's by a relative error of at most 0.0057.
Values may be sent and summed in bfloat16 or wider, within the bound.
No kernel may reach another device: no remote copies, remote signals or barrier semaphores. Data moves between devices by JAX's collectives and lax.ppermute only.
A program may use at most 128 MiB of HBM per device.

v0:
```python
import jax
import jax.numpy as jnp
from jax import lax
from jax.sharding import PartitionSpec as P

HD = 128


def head_attend(queries, key_rows, value_rows, key_ok, live):
    scale = 1.0 / HD**0.5
    blocks = queries.reshape(4, queries.shape[0] // 4, queries.shape[1])

    def one_block(block):
        scores = jnp.dot(block, key_rows.T, preferred_element_type=jnp.float32) * scale
        scores = jnp.where(key_ok[None, :], scores, jnp.float32(-1e30))
        highest = jnp.max(scores, axis=1, keepdims=True)
        expos = jnp.exp(scores - highest)
        weights = (expos / jnp.sum(expos, axis=1, keepdims=True)).astype(jnp.bfloat16)
        result = jnp.dot(weights, value_rows, preferred_element_type=jnp.float32)
        return (result * live).astype(jnp.bfloat16)

    return lax.map(one_block, blocks).reshape(queries.shape[0], queries.shape[1])


def on_device(video_projected, text_projected, head_live, text_valid, text_weight, text_cotangent):
    video = video_projected[0]
    text = text_projected[0]
    video_heads, text_heads = (
        lax.all_to_all(video, "seq", split_axis=2, concat_axis=0, tiled=True),
        lax.all_to_all(text, "seq", split_axis=2, concat_axis=0, tiled=True),
    )
    joined = jnp.concatenate([video_heads, text_heads], axis=0)
    length = joined.shape[0]
    video_count = video_heads.shape[0]
    local_heads = joined.shape[2] // HD
    live_local = lax.dynamic_slice_in_dim(
        head_live, lax.axis_index("seq") * local_heads, local_heads
    ).astype(jnp.float32)
    key_ok = jnp.concatenate([jnp.ones((video_count,), bool), text_valid[0] > 0])
    split = joined.reshape(length, 3, local_heads, HD).transpose(1, 2, 0, 3)

    def one_head(args):
        return head_attend(args[0], args[1], args[2], key_ok, args[3])

    heads = lax.map(one_head, (split[0], split[1], split[2], live_local))
    attended = heads.transpose(1, 0, 2).reshape(length, local_heads * HD)
    video_part = attended[:video_count]
    text_part = attended[video_count:]
    weight_cols = lax.all_gather(text_weight, "dp", axis=1, tiled=True)
    video_back, text_back = (
        lax.all_to_all(video_part, "seq", split_axis=0, concat_axis=1, tiled=True),
        lax.all_to_all(text_part, "seq", split_axis=0, concat_axis=1, tiled=True),
    )
    full_weight = lax.all_gather(weight_cols, "seq", axis=0, tiled=True)
    text_output = jnp.dot(text_back, full_weight, preferred_element_type=jnp.float32).astype(
        jnp.bfloat16
    )
    cotangent_all = lax.all_gather(text_cotangent[0], "seq", axis=0, tiled=True)
    gradient_term = lax.dot_general(
        text_part, cotangent_all, (((0,), (0,)), ((), ())), preferred_element_type=jnp.float32
    )
    gradient = lax.psum_scatter(gradient_term, "dp", scatter_dimension=1, tiled=True)
    return (video_back[None], text_output[None], gradient)


def solution(mesh):
    in_specs = (
        P("dp", "seq", None, None),
        P("dp", "seq", None, None),
        P(),
        P("dp", None),
        P("seq", "dp"),
        P("dp", "seq", None),
    )
    out_specs = (P("dp", "seq", None), P("dp", "seq", None), P("seq", "dp"))
    return jax.shard_map(
        on_device, mesh=mesh, in_specs=in_specs, out_specs=out_specs, check_vma=False
    )
```

profile of v0, /device:TPU:1, one launch (start us, length us, event | category | flops | bytes accessed | tf_op | source)
XLA Modules:
  0.0 407.0 jit_solution(4816121795936393613)
XLA Ops:
  8.7 29.5 %all-gather.5.cloned.1.call-done = bf16[256,3072]{1,0:T(8,128)(2,1)} async-done(((bf16[256,384]{1,0:T(8,128)(2,1)}), bf16[256,3072]{1,0:T(8,128)(2,1)}) %all-gather.5.cloned.1.call-update) | async-done | bytes 1572880 | tf_op jit(solution)/shard_map/all_gather | solution.py:49
  38.3 5.8 %copy.30 = bf16[1,16,3,4096]{1,2,3,0:T(4,128)(2,1)} copy(bf16[1,16,3,4096]{3,1,2,0:T(8,128)(2,1)} %param.11) | data formatting | bytes 786432 | tf_op args[1]
  44.0 5.3 %bitcast_bitcast_fusion = bf16[4096,3,16]{2,1,0:T(4,128)(2,1)} fusion(bf16[1,16,3,4096]{1,2,3,0:T(4,128)(2,1)} %copy.30), kind=kLoop, calls=%fused_computation.30 | loop fusion | bytes 786432
  49.4 7.4 %reshape.36 = bf16[16,2,6144]{2,1,0:T(2,128)(2,1)} reshape(bf16[4096,3,16]{2,1,0:T(4,128)(2,1)} %bitcast_bitcast_fusion) | data formatting | bytes 786432
  56.8 6.5 %all-to-all-start.1 = ((bf16[16,2,6144]{2,1,0:T(2,128)(2,1)}), bf16[16,2,6144]{2,1,0:T(2,128)(2,1)S(1)}, u32[]{:S(2)}, u32[]{:S(2)}) async-start(bf16[16,2,6144]{2,1,0:T(2,128)(2,1)} %reshape.36), calls=%async_computation.1 | async-start | bytes 786432 | tf_op jit(solution)/shard_map/all_to_all | solution.py:30
  63.4 12.8 %copy.28 = bf16[1,192,3,4096]{1,2,3,0:T(4,128)(2,1)} copy(bf16[1,192,3,4096]{3,1,2,0:T(8,128)(2,1)} %param.10) | data formatting | bytes 9437184 | tf_op args[0]
  76.1 6.9 %all-to-all-start = ((bf16[192,3,4096]{0,1,2:T(4,128)(2,1)}), bf16[192,3,4096]{0,1,2:T(4,128)(2,1)}, u32[]{:S(2)}, u32[]{:S(2)}) async-start(bf16[192,3,4096]{0,1,2:T(4,128)(2,1)} %bitcast.75), calls=%async_computation | async-start | bytes 16777216 | tf_op jit(solution)/shard_map/all_to_all | solution.py:29
  83.8 5.6 %reshape.37 = bf16[4096,3,16]{2,1,0:T(4,128)(2,1)} reshape(bf16[16,2,6144]{2,1,0:T(2,128)(2,1)S(1)} %all-to-all-done.1) | data formatting | bytes 786432
  89.4 5.3 %copy.31 = bf16[16,3,16,256]{3,0,2,1:T(8,128)(2,1)S(1)} copy(bf16[16,3,16,256]{0,1,3,2:T(4,128)(2,1)} %bitcast.78) | data formatting | bytes 786432 | tf_op jit(solution)/shard_map/all_to_all | solution.py:30
  94.8 133.7 %all-to-all-done = bf16[192,3,4096]{0,1,2:T(4,128)(2,1)} async-done(((bf16[192,3,4096]{0,1,2:T(4,128)(2,1)}), bf16[192,3,4096]{0,1,2:T(4,128)(2,1)}, u32[]{:S(2)}, u32[]{:S(2)}) %all-to-all-start) | async-done | bytes 4718624 | tf_op jit(solution)/shard_map/all_to_all | solution.py:29
  228.5 12.7 %copy.29 = bf16[192,3,16,256]{3,0,2,1:T(8,128)(2,1)} copy(bf16[192,3,16,256]{0,1,3,2:T(4,128)(2,1)} %bitcast.8) | data formatting | bytes 9437184 | tf_op jit(solution)/shard_map/all_to_all | solution.py:29
  241.3 7.8 %concatenate.11 = bf16[3072,3,2,128]{3,2,0,1:T(2,128)(2,1)} reshape(bf16[16,192,3,256]{3,1,0,2:T(8,128)(2,1)} %bitcast.77) | data formatting | bytes 9437184 | tf_op jit(solution)/shard_map/concatenate | solution.py:32
  249.1 13.2 %maximum_bitcast_fusion = bf16[3,2,3328,128]{3,1,2,0:T(2,128)(2,1)S(1)} fusion(bf16[256,3,2,128]{3,2,0,1:T(2,128)(2,1)S(1)} %concatenate.12, bf16[3072,3,2,128]{3,2,0,1:T(2,128)(2,1)} %concatenate.11), kind=kLoop, calls=%fused_computation.20 | loop fusion | flops 2555904 | bytes 10223616 | tf_op jit(solution)/shard_map/transpose | solution.py:40
  262.3 3.6 slice_bitcast_fusion
  270.2 77.6 %while.21 = (s32[]{:T(128)}, bf16[2,3328,128]{1,2,0:T(8,128)(2,1)}, bf16[2,3328,128]{2,1,0:T(8,128)(2,1)}, bf16[2,3328,128]{2,1,0:T(8,128)(2,1)}, bf16[2,3328,12...) while((s32[]{:T(128)}, bf16[2,3328,128]{1,2,0:T(8,128)(2,1)}, ...), condition=%wide.region_5.6_spmd, body=%wide.region_0.5_spmd.sunk | while | flops 1451112832 | bytes 43906356 | solution.py:45
  274.3 33.2 %while.22 = (s32[]{:T(128)}, bf16[4,832,128]{2,1,0:T(8,128)(2,1)S(1)}, pred[3328]{0:T(1024)(128)(4,1)S(1)}, bf16[4,832,128]{2,1,0:T(8,128)(2,1)S(1)}, bf16[3328,...) while((s32[]{:T(128)}, bf16[4,832,128]{2,1,0:T(8,128)(2,1)S(1)}, ...), condition=%wide.region_4.4_spmd, body=%wide.region_1.3_spmd.sunk | while | flops 1451112832 | bytes 35386472 | solution.py:22
  274.3 1.9 fusion.28
  276.2 2.4 fusion.29
  278.7 3.9 fusion.30
  282.6 1.9 fusion.28
  284.5 2.4 fusion.29
  286.9 3.9 fusion.30
  290.9 1.9 fusion.28
  292.8 2.4 fusion.29
  295.2 3.9 fusion.30
  299.1 1.9 fusion.28
  301.1 2.4 fusion.29
  303.5 3.9 fusion.30
  313.0 33.2 %while.22 = (s32[]{:T(128)}, bf16[4,832,128]{2,1,0:T(8,128)(2,1)S(1)}, pred[3328]{0:T(1024)(128)(4,1)S(1)}, bf16[4,832,128]{2,1,0:T(8,128)(2,1)S(1)}, bf16[3328,...) while((s32[]{:T(128)}, bf16[4,832,128]{2,1,0:T(8,128)(2,1)S(1)}, ...), condition=%wide.region_4.4_spmd, body=%wide.region_1.3_spmd.sunk | while | flops 1451112832 | bytes 35386472 | solution.py:22
  314.9 2.4 fusion.29
  317.4 3.9 fusion.30
  321.3 1.9 fusion.28
  323.2 2.5 fusion.29
  325.7 3.9 fusion.30
  329.6 1.9 fusion.28
  331.5 2.4 fusion.29
  334.0 3.9 fusion.30
  337.9 1.9 fusion.28
  339.8 2.4 fusion.29
  342.3 3.9 fusion.30
  348.8 3.7 fusion.14
  353.5 4.6 %all-to-all-start.3 = ((bf16[16,16,256]{2,1,0:T(8,128)(2,1)}), bf16[16,16,256]{2,1,0:T(8,128)(2,1)S(1)}, u32[]{:S(2)}, u32[]{:S(2)}) async-start(bf16[16,16,256]{2,1,0:T(8,128)(2,1)} %all_to_all.57), calls=%async_computation.3 | async-start | bytes 262144 | tf_op jit(solution)/shard_map/all_to_all | solution.py:52
  359.4 2.3 all_to_all.54
  361.7 3.2 all-to-all-done.3
  364.9 3.7 all-to-all-start.2
  368.6 18.4 %all-to-all-done.2 = bf16[16,192,256]{2,1,0:T(8,128)(2,1)S(1)} async-done(((bf16[16,192,256]{2,1,0:T(8,128)(2,1)}), bf16[16,192,256]{2,1,0:T(8,128)(2,1)S(1)}, u32[]{:S(2)}, u32[]{:S(2)}) %all-to-all-start.2) | async-done | bytes 1572896 | tf_op jit(solution)/shard_map/all_to_all | solution.py:51
  387.9 2.1 broadcast_in_dim.34
  390.0 10.5 %fusion.13 = bf16[1,16,3072]{2,1,0:T(8,128)(2,1)} fusion(bf16[16,4096]{1,0:T(8,128)(2,1)S(1)} %bitcast.84, bf16[4096,3072]{1,0:T(8,128)(2,1)} %all-gather.7.cloned.1.call-done), kind=kOutput, calls=%fused_computation.22 | convolution fusion | flops 402702336 | bytes 25395200 | tf_op jit(solution)/shard_map/dot_general | solution.py:55
  (46 shorter events, 24.0 us)
Async XLA Ops:
  7.2 31.1 %all-gather.5.cloned.1.call-start = ((), (), s32[]{:S(2)}) async-start(), calls=%async_computation.5 | async-start | bytes 1769472 | tf_op jit(solution)/shard_map/all_gather | solution.py:49
  7.9 340.9 %all-gather.9.cloned.1.call-start = ((), (), s32[]{:S(2)}) async-start(), calls=%async_computation.8 | async-start | bytes 1671168 | tf_op jit(solution)/shard_map/all_gather | solution.py:58
  8.6 381.3 %all-gather.7.cloned.1.call-start = ((), (), s32[]{:S(2)}) async-start(), calls=%async_computation.6 | async-start | bytes 26738688 | tf_op jit(solution)/shard_map/all_gather | solution.py:54
  56.8 19.3 %all-to-all-start.1 = ((bf16[16,2,6144]{2,1,0:T(2,128)(2,1)}), bf16[16,2,6144]{2,1,0:T(2,128)(2,1)S(1)}, u32[]{:S(2)}, u32[]{:S(2)}) async-start(bf16[16,2,6144]{2,1,0:T(2,128)(2,1)} %reshape.36), calls=%async_computation.1 | async-start | bytes 786432 | tf_op jit(solution)/shard_map/all_to_all | solution.py:30
  76.1 7.0 %copy-start.1 = (s32[1,256]{1,0:T(1,128)S(1)}, s32[1,256]{1,0:T(1,128)}, u32[]{:S(2)}) copy-start(s32[1,256]{1,0:T(1,128)} %param.13) | copy-start | bytes 3076
  76.1 7.0 %copy-start.2 = (s32[32]{0:T(128)S(1)}, s32[32]{0:T(128)}, u32[]{:S(2)}) copy-start(s32[32]{0:T(128)} %param.12) | copy-start | bytes 388
  76.1 152.4 %all-to-all-start = ((bf16[192,3,4096]{0,1,2:T(4,128)(2,1)}), bf16[192,3,4096]{0,1,2:T(4,128)(2,1)}, u32[]{:S(2)}, u32[]{:S(2)}) async-start(bf16[192,3,4096]{0,1,2:T(4,128)(2,1)} %bitcast.75), calls=%async_computation | async-start | bytes 16777216 | tf_op jit(solution)/shard_map/all_to_all | solution.py:29
  83.1 317.4 %reduce-scatter.2.cloned.1.call-start = ((), (), s32[]{:S(2)}) async-start(), calls=%async_computation.7 | async-start | bytes 3538944 | tf_op jit(solution)/shard_map/reduce_scatter | solution.py:62
  347.8 10.2 %copy-start = (bf16[2,3328,128]{1,2,0:T(8,128)(2,1)S(1)}, bf16[2,3328,128]{1,2,0:T(8,128)(2,1)}, u32[]{:S(2)}) copy-start(bf16[2,3328,128]{1,2,0:T(8,128)(2,1)} %get-tuple-element.77) | copy-start | bytes 5111812
  353.5 11.4 %all-to-all-start.3 = ((bf16[16,16,256]{2,1,0:T(8,128)(2,1)}), bf16[16,16,256]{2,1,0:T(8,128)(2,1)S(1)}, u32[]{:S(2)}, u32[]{:S(2)}) async-start(bf16[16,16,256]{2,1,0:T(8,128)(2,1)} %all_to_all.57), calls=%async_computation.3 | async-start | bytes 262144 | tf_op jit(solution)/shard_map/all_to_all | solution.py:52
  364.9 22.1 %all-to-all-start.2 = ((bf16[16,192,256]{2,1,0:T(8,128)(2,1)}), bf16[16,192,256]{2,1,0:T(8,128)(2,1)S(1)}, u32[]{:S(2)}, u32[]{:S(2)}) async-start(bf16[16,192,256]{2,1,0:T(8,128)(2,1)} %all_to_all.54), calls=%async_computation.2 | async-start | bytes 3145728 | tf_op jit(solution)/shard_map/all_to_all | solution.py:51
Sparse Core Ops, SparseCore 0:
  9.7 28.4 all-gather.4
  40.4 42.3 all-gather.8
  84.9 241.2 all-gather.6
  352.7 33.9 reduce-scatter.1
where the time goes:
time: 415 us; the launch traced here: 407 us
  waiting for transfers between devices  186 us (45%)
  local copies, waits for them, and re-layouts  90.6 us (22%)
  matrix products  60.8 us (15%)
  other arithmetic  33.4 us (8%)
  starting transfers between devices  21.9 us (5%)
  between operations  13.9 us (3%)
    all_to_all x1, waiting for transfers between devices, on_device(): lax.all_to_all(video, 'seq', split_axis=2, concat_axis=0, tiled=True)  134 us
    unnamed x11, local copies, waits for them, and re-layouts  37 us
    dot_general x8, matrix products, one_block(): result = jnp.dot(weights, value_rows, preferred_element_type=jnp.float32)  31.1 us
    all_gather x1, waiting for transfers between devices, on_device(): weight_cols = lax.all_gather(text_weight, 'dp', axis=1, tiled=True)  29.5 us
    reduce_sum x8, other arithmetic, one_block(): jnp.sum(expos, axis=1, keepdims=True)  19.6 us
    all_to_all x1, waiting for transfers between devices, on_device(): lax.all_to_all(video_part, 'seq', split_axis=0, concat_axis=1, tiled=True)  18.4 us
    dot_general x8, matrix products, one_block(): jnp.dot(block, key_rows.T, preferred_element_type=jnp.float32) * scale  15.5 us
    transpose x1, other arithmetic, on_device(): split = joined.reshape(length, 3, local_heads, HD).transpose(1, 2, 0, 3)  13.2 us
  transfers between devices with their start and end apart: 8, of which 4 were waited for; matrix products, arithmetic and copies ran while one was open for 45% of the time, Pallas kernels for 0%

commit v1 on v0

v1 whole, which is shorter than its diff:
```python
import functools

import numpy as np

import jax
import jax.numpy as jnp
from jax import lax
from jax.experimental import pallas as pl
from jax.experimental.pallas import tpu as pltpu
from jax.sharding import PartitionSpec as P

HD = 128
LIVE = 24
SLOTS = 32
N = 3328
VID = 3072
TXT = 256
SEQ = 16
VT = 192
TT = 16
HALF = 96
ROWS = VT + TT + HALF + TT
CHUNK = 256
SCALE = float(np.log2(np.e) / HD**0.5)
BF16 = jnp.bfloat16
F32 = jnp.float32
VMEM = pl.BlockSpec(memory_space=pltpu.VMEM)
SMEM = pl.BlockSpec(memory_space=pltpu.SMEM)
ANY = pl.BlockSpec(memory_space=pl.ANY)


def run_all(copies):
    for copy in copies:
        copy.start()
    for copy in copies:
        copy.wait()


def head_columns(slots, rank):
    return pl.ds(pl.multiple_of(slots[rank] * HD, HD), HD)


def give_kernel(slots, core, video, text, give, sem):
    start = pl.multiple_of((1 - core[0]) * HALF, 16)
    copies = []
    for j in range(8):
        cols = head_columns(slots, 16 + j)
        copies.append(pltpu.make_async_copy(
            video.at[:, pl.ds(start, HALF), cols], give.at[j, :, pl.ds(0, HALF), :], sem.at[0]))
        copies.append(pltpu.make_async_copy(
            text.at[:, :, cols], give.at[j, :, pl.ds(HALF, TT), :], sem.at[1]))
    run_all(copies)


def pack_kernel(slots, core, video, text, buf, sem):
    start = pl.multiple_of(core[0] * HALF, 16)
    copies = []
    for r in range(16):
        cols = head_columns(slots, r)
        copies.append(pltpu.make_async_copy(
            video.at[:, :, cols], buf.at[r, :, pl.ds(0, VT), :], sem.at[0]))
        copies.append(pltpu.make_async_copy(
            text.at[:, :, cols], buf.at[r, :, pl.ds(VT, TT), :], sem.at[1]))
    for j in range(8):
        cols = head_columns(slots, 16 + j)
        to = 2 * j + core[0]
        copies.append(pltpu.make_async_copy(
            video.at[:, pl.ds(start, HALF), cols], buf.at[to, :, pl.ds(VT + TT, HALF), :], sem.at[2]))
        copies.append(pltpu.make_async_copy(
            text.at[:, :, cols], buf.at[to, :, pl.ds(VT + TT + HALF, TT), :], sem.at[3]))
    run_all(copies)


def fill_kernel(core, got, _, buf, sem):
    copies = []
    for j in range(8):
        to = 2 * j + 1 - core[0]
        copies.append(pltpu.make_async_copy(
            got.at[j], buf.at[to, :, pl.ds(VT + TT, HALF + TT), :], sem.at[0]))
    run_all(copies)


def rows_dot(a, b):
    return lax.dot_general(a, b, (((1,), (1,)), ((), ())), preferred_element_type=F32)


def lay_a(recv, keys, values):
    for s in range(SEQ):
        keys[s * VT:(s + 1) * VT, :] = recv[s, 1, 0:VT, :]
        values[s * VT:(s + 1) * VT, 0:HD] = recv[s, 2, 0:VT, :]
        keys[VID + s * TT:VID + (s + 1) * TT, :] = recv[s, 1, VT:VT + TT, :]
        values[VID + s * TT:VID + (s + 1) * TT, 0:HD] = recv[s, 2, VT:VT + TT, :]
    values[:, HD:] = jnp.ones((N, HD), BF16)


def lay_c(recv, other, keys, values):
    first, tail = VT + TT, VT + TT + HALF
    for s in range(SEQ):
        at, far = s * HALF, VID // 2 + s * HALF
        keys[at:at + HALF, :] = recv[s, 1, first:tail, :]
        values[at:at + HALF, 0:HD] = recv[s, 2, first:tail, :]
        keys[far:far + HALF, :] = other[s, 0]
        values[far:far + HALF, 0:HD] = other[s, 1]
        keys[VID + s * TT:VID + (s + 1) * TT, :] = recv[s, 1, tail:ROWS, :]
        values[VID + s * TT:VID + (s + 1) * TT, 0:HD] = recv[s, 2, tail:ROWS, :]
    values[:, HD:] = jnp.ones((N, HD), BF16)


def score_chunk(query, keys, bias, scores, slot, c, top):
    rows = query.shape[0]
    s = rows_dot(query, keys[c:c + CHUNK, :])
    if c >= VID:
        s = s + bias[:, c - VID:c - VID + CHUNK]
    scores[slot, 0:rows, c:c + CHUNK] = s
    for t in range(0, CHUNK, HD):
        x = s[:, t:t + HD]
        top = x if top is None else jnp.maximum(top, x)
    return top


def keep_top(tops, slot, top):
    rows = top.shape[0]
    highest = jnp.max(top, axis=1, keepdims=True) * SCALE
    tops[slot, 0:rows, :] = jnp.broadcast_to(highest, (rows, HD))


def score_block(query, keys, bias, scores, tops, slot):
    top = None
    for c in range(0, N, CHUNK):
        top = score_chunk(query, keys, bias, scores, slot, c, top)
    keep_top(tops, slot, top)


def attend_block(rows, values, scores, tops, slot, following=None):
    highest = jnp.concatenate([tops[slot, 0:rows, :]] * (CHUNK // HD), axis=1)
    top, total = None, None
    for c in range(0, N, CHUNK):
        if following is not None:
            query, keys, bias = following
            top = score_chunk(query, keys, bias, scores, 1 - slot, c, top)
        p = jnp.exp2(scores[slot, 0:rows, c:c + CHUNK] * SCALE - highest)
        part = jnp.dot(p.astype(BF16), values[c:c + CHUNK, :], preferred_element_type=F32)
        total = part if total is None else total + part
    if following is not None:
        keep_top(tops, 1 - slot, top)
    return (total[:, 0:HD] / total[:, HD:]).astype(BF16)


def text_kernel(bias_a, bias_c, recv, other, _w, _c, out, scores, tops, keys_a, values_a, keys_c, values_c):
    lay_a(recv, keys_a, values_a)
    ba, bc = bias_a[...], bias_c[...]
    score_block(recv[:, 0, VT:VT + TT, :].reshape(TXT, HD), keys_a, ba, scores, tops, 0)
    lay_c(recv, other, keys_c, values_c)
    query = recv[:, 0, VT + TT + HALF:ROWS, :].reshape(TXT, HD)
    got = attend_block(TXT, values_a, scores, tops, 0, (query, keys_c, bc))
    out[:, 0:TT, :] = got.reshape(SEQ, TT, HD)
    got = attend_block(TXT, values_c, scores, tops, 1)
    out[:, TT:2 * TT, :] = got.reshape(SEQ, TT, HD)


def video_blocks(count, rows, load, store, keys, values, bias, scores, tops):
    def step(i, slot, more):
        following = (load(i + 1), keys, bias) if more else None
        store(i, attend_block(rows, values, scores, tops, slot, following))

    score_block(load(0), keys, bias, scores, tops, 0)

    def body(j, carry):
        step(2 * j, 0, True)
        step(2 * j + 1, 1, True)
        return carry

    lax.fori_loop(0, count // 2 - 1, body, 0)
    step(count - 2, 0, True)
    step(count - 1, 1, False)


def a_kernel(bias_a, recv, out, scores, tops, keys, values):
    lay_a(recv, keys, values)

    def load(i):
        return recv[pl.ds(2 * i, 2), 0, 0:VT, :].reshape(2 * VT, HD)

    def store(i, got):
        out[pl.ds(2 * i, 2)] = got.reshape(2, VT, HD)

    video_blocks(8, 2 * VT, load, store, keys, values, bias_a[...], scores, tops)


def c_kernel(bias_c, recv, other, out_a, out, scores, tops, keys, values):
    lay_c(recv, other, keys, values)
    out[:, 0:VT, :] = out_a[...]

    def load(i):
        return recv[pl.ds(4 * i, 4), 0, VT + TT:VT + TT + HALF, :].reshape(4 * HALF, HD)

    def store(i, got):
        out[pl.ds(4 * i, 4), VT:VT + HALF, :] = got.reshape(4, HALF, HD)

    video_blocks(4, 4 * HALF, load, store, keys, values, bias_c[...], scores, tops)


def slot_text_kernel(ranks, core, seat, got, _, out):
    for h in range(SLOTS):
        rank = ranks[h]
        group = (h // 8) ^ (seat[0] // 4)
        pair = ((h // 2) % 4) ^ (seat[0] % 4)
        cols = pl.ds(pl.multiple_of((pair * 2 + h % 2) * HD, HD), HD)

        @pl.when(rank < 0)
        def _():
            out[group, :, cols] = jnp.zeros((TT, HD), BF16)

        @pl.when((rank >= 0) & (rank < 16))
        def _():
            out[group, :, cols] = got[jnp.clip(rank, 0, 15), 0:TT, :]

        @pl.when(rank >= 16)
        def _():
            out[group, :, cols] = got[2 * jnp.clip(rank - 16, 0, 7) + core[0], TT:2 * TT, :]


def project_kernel(rows, weight, cot, p0, p1, p2, p3, g0, g1, g2, g3):
    part = jnp.dot(rows[...], weight[...], preferred_element_type=F32).reshape(8, 4, TT, 384)
    for j, ref in enumerate((p0, p1, p2, p3)):
        ref[...] = part[:, j].astype(ref.dtype)
    for j, ref in enumerate((g0, g1, g2, g3)):
        term = lax.dot_general(
            rows[:, j * 256:(j + 1) * 256], cot[...], (((0,), (0,)), ((), ())),
            preferred_element_type=F32)
        ref[...] = term.astype(ref.dtype)


def slot_video_kernel(ranks, core, got, other, out):
    mine = pl.multiple_of(core[0] * HALF, 16)
    far = pl.multiple_of((1 - core[0]) * HALF, 16)
    for h in range(SLOTS):
        rank = ranks[h]
        cols = pl.ds(h * HD, HD)

        @pl.when(rank < 0)
        def _():
            out[:, cols] = jnp.zeros((VT, HD), BF16)

        @pl.when((rank >= 0) & (rank < 16))
        def _():
            out[:, cols] = got[jnp.clip(rank, 0, 15), 0:VT, :]

        @pl.when(rank >= 16)
        def _():
            j = jnp.clip(rank - 16, 0, 7)
            out[pl.ds(mine, HALF), cols] = got[2 * j + core[0], VT:VT + HALF, :]
            out[pl.ds(far, HALF), cols] = other[j]


def shape(*dims, dtype=BF16):
    return jax.ShapeDtypeStruct(dims, dtype)


def cost(rows):
    return pl.CostEstimate(
        flops=4 * rows * N * HD, bytes_accessed=8 << 20, transcendentals=rows * N)


def attention_call(kernel, name, rows, block, heads, out_shape, specs):
    scratch = [pltpu.VMEM((2, block, N), F32), pltpu.VMEM((2, block, HD), F32)]
    for _ in range(heads):
        scratch += [pltpu.VMEM((N, HD), BF16), pltpu.VMEM((N, 2 * HD), BF16)]
    return pl.pallas_call(
        kernel, out_shape=out_shape, in_specs=specs, out_specs=VMEM, scratch_shapes=scratch,
        cost_estimate=cost(rows), name=name,
        compiler_params=pltpu.CompilerParams(vmem_limit_bytes=40 << 20))


def trade(x, axis, mask):
    count = 8 if axis == "dp" else SEQ
    return lax.ppermute(x, axis, [(i, i ^ mask) for i in range(count)])


def swap(x):
    return trade(x, "dp", 1)


def by_xor(x, index):
    count, rest = x.shape[0], x.shape[1:]
    bits = count.bit_length() - 1
    for b in range(bits):
        parts = x.reshape((count >> (b + 1), 2, 1 << b) + rest)
        x = jnp.where((index >> b) & 1 > 0, parts[:, ::-1], parts).reshape((count,) + rest)
    return x


def gather4(x, axis, low):
    near, far = trade(x, axis, low), trade(x, axis, 3 * low)
    half = x.shape[0] // 2
    opposite = jnp.concatenate(
        [trade(near[:half], axis, 3 * low), trade(far[half:], axis, low)], axis=0)
    return jnp.stack([x, near, opposite, far])


def gather_dp(x):
    along = gather4(x, "dp", 2)
    return jnp.stack([along, swap(along)], axis=1).reshape((8,) + x.shape)


def exchange_dp(x):
    rest = x.shape[1:]
    for b in (2, 1, 0):
        parts = x.reshape((8 >> (b + 1), 2, 1 << b) + rest)
        got = trade(parts[:, 1], "dp", 1 << b)
        x = jnp.stack([parts[:, 0], got], axis=1).reshape((8,) + rest)
    return x


def on_device(video_projected, text_projected, head_live, text_valid, text_weight, text_cotangent):
    video = video_projected[0].transpose(1, 0, 2)
    text = text_projected[0].transpose(1, 0, 2)
    seq = lax.axis_index("seq")
    dp = lax.axis_index("dp")
    core_bit = dp % 2
    core = core_bit.astype(jnp.int32).reshape(1)
    seat = seq.astype(jnp.int32).reshape(1)

    heads = jnp.arange(SLOTS, dtype=jnp.int32)
    live = head_live > 0
    place = jnp.sum(jnp.where(heads[None, :] < heads[:, None], head_live[None, :], 0), axis=1)
    ranks = jnp.where(live, place, -1).astype(jnp.int32)
    slots = jnp.sum(
        jnp.where(ranks[None, :] == jnp.arange(LIVE, dtype=jnp.int32)[:, None], heads[None, :], 0),
        axis=1).astype(jnp.int32)

    give = pl.pallas_call(
        give_kernel, out_shape=shape(8, 3, HALF + TT, HD), in_specs=[SMEM, SMEM, ANY, ANY],
        out_specs=VMEM, scratch_shapes=[pltpu.SemaphoreType.DMA((2,))], name="give",
        cost_estimate=pl.CostEstimate(flops=0, bytes_accessed=2 << 20, transcendentals=0),
    )(slots, core, video, text)
    got = swap(give)
    valid_other = swap(text_valid)
    buf = pl.pallas_call(
        pack_kernel, out_shape=shape(SEQ, 3, ROWS, HD), in_specs=[SMEM, SMEM, ANY, ANY],
        out_specs=VMEM, scratch_shapes=[pltpu.SemaphoreType.DMA((4,))], name="pack",
        cost_estimate=pl.CostEstimate(flops=0, bytes_accessed=7 << 20, transcendentals=0),
    )(slots, core, video, text)
    buf = pl.pallas_call(
        fill_kernel, out_shape=shape(SEQ, 3, ROWS, HD), in_specs=[SMEM, VMEM, ANY],
        out_specs=ANY, scratch_shapes=[pltpu.SemaphoreType.DMA((1,))], name="fill",
        input_output_aliases={2: 0},
    )(core, got, buf)
    buf, weight, cot = lax.optimization_barrier((buf, text_weight, text_cotangent[0]))
    weight_x = gather4(weight, "seq", 1).reshape(4 * 256, 384)
    cot = by_xor(cot.reshape(TT, 8, 384).transpose(1, 0, 2), dp)
    cot = gather4(exchange_dp(cot).reshape(8 * TT, 384), "seq", 4)
    cot_y = cot.reshape(4, 8, TT, 384).transpose(1, 0, 2, 3).reshape(8 * 4 * TT, 384)
    recv = lax.all_to_all(buf, "seq", split_axis=0, concat_axis=0, tiled=True)
    other = swap(recv[:, 1:3, VT + TT:VT + TT + HALF, :])

    bias_a = jnp.where(text_valid > 0, 0.0, -1e30).astype(F32)
    bias_far = jnp.where(valid_other > 0, 0.0, -1e30).astype(F32)
    bias_c = jnp.where(seq % 2 == core_bit, bias_a, bias_far)

    text_out = attention_call(
        text_kernel, "text_attention", 2 * TXT, TXT, 2, shape(SEQ, 2 * TT, HD), [VMEM] * 4 + [ANY] * 2,
    )(bias_a, bias_c, recv, other, weight_x, cot_y)
    text_got = lax.all_to_all(text_out, "seq", split_axis=0, concat_axis=0, tiled=True)
    out_a = attention_call(
        a_kernel, "video_attention_a", VID, 2 * VT, 1, shape(SEQ, VT, HD), [VMEM] * 2,
    )(bias_a, recv)
    out_all = attention_call(
        c_kernel, "video_attention_c", VID // 2, 4 * HALF, 1, shape(SEQ, VT + HALF, HD), [VMEM] * 4,
    )(bias_c, recv, other, out_a)
    back = lax.all_to_all(out_all, "seq", split_axis=0, concat_axis=0, tiled=True)
    halves = back.reshape(8, 2, VT + HALF, HD)[:, :, VT:, :]
    halves = swap(lax.dynamic_index_in_dim(halves, 1 - core_bit, 1, keepdims=False))
    video_attended = pl.pallas_call(
        slot_video_kernel, out_shape=shape(VT, SLOTS * HD), in_specs=[SMEM, SMEM, VMEM, VMEM],
        out_specs=VMEM, name="slot_video")(ranks, core, back, halves)

    text_slots = pl.pallas_call(
        slot_text_kernel, out_shape=shape(4, TT, 8 * HD),
        in_specs=[SMEM, SMEM, SMEM, VMEM, ANY], out_specs=VMEM, name="slot_text",
    )(ranks, core, seat, text_got, out_all)
    rows = [text_slots[0]] + [trade(text_slots[j], "seq", 4 * j) for j in (1, 2, 3)]
    rows_all = gather_dp(jnp.concatenate(rows)).reshape(8 * 4 * TT, 8 * HD)
    sums = pl.pallas_call(
        project_kernel,
        out_shape=[shape(8, TT, 384, dtype=F32)] + [shape(8, TT, 384)] * 3
        + [shape(256, 384, dtype=F32)] + [shape(256, 384)] * 3,
        in_specs=[VMEM] * 3, out_specs=[VMEM] * 8, name="project",
        compiler_params=pltpu.CompilerParams(vmem_limit_bytes=20 << 20),
    )(rows_all, weight_x, cot_y)
    projected = sums[0]
    for j in (1, 2, 3):
        projected = projected + trade(sums[j], "seq", 4 * j).astype(F32)
    gradient = sums[4]
    for j in (1, 2, 3):
        gradient = gradient + trade(sums[4 + j], "seq", j).astype(F32)
    projected = by_xor(exchange_dp(projected.astype(BF16)), dp)
    text_output = projected.transpose(1, 0, 2).reshape(TT, 8 * 384)
    return (video_attended[None], text_output[None], gradient)


def solution(mesh):
    in_specs = (
        P("dp", "seq", None, None),
        P("dp", "seq", None, None),
        P(),
        P("dp", None),
        P("seq", "dp"),
        P("dp", "seq", None),
    )
    out_specs = (P("dp", "seq", None), P("dp", "seq", None), P("seq", "dp"))
    return jax.shard_map(
        on_device, mesh=mesh, in_specs=in_specs, out_specs=out_specs, check_vma=False
    )
```

time: 415 us -> 200 us (0.48); the launches traced: 407 us -> 199 us
  waiting for transfers between devices: 186 us -> 67 us
  local copies, waits for them, and re-layouts: 90.6 us -> 5.18 us
  matrix products: 60.8 us -> 0 us
  starting transfers between devices: 21.9 us -> 75.6 us
  Pallas kernels: 0 us -> 46.9 us
  other arithmetic: 33.4 us -> 3.6 us
  between operations: 13.9 us -> 1.12 us
    all_to_all x4 -> x3, waiting for transfers between devices: 155 us -> 0.01 us  [the longest x1 0.01 us: on_device(): recv = lax.all_to_all(buf, 'seq', split_axis=0, concat_axis=0, tiled=True)]
    ppermute x0 -> x32, waiting for transfers between devices: none -> 67 us  [trade(): return lax.ppermute(x, axis, [(i, i ^ mask) for i in range(count)])]
    dot_general x18 -> x0, matrix products: 60.8 us -> none  [the longest x8 31.1 us: one_block(): result = jnp.dot(weights, value_rows, preferred_element_type=jnp.float32)]
    ppermute x0 -> x32, starting transfers between devices: none -> 59.2 us  [trade(): return lax.ppermute(x, axis, [(i, i ^ mask) for i in range(count)])]
    pallas_call x0 -> x9, Pallas kernels: none -> 46.9 us  [the longest x1 15.1 us: on_device(): attention_call(a_kernel, 'video_attention_a', VID, 2 * VT, 1, shape(SEQ,...]
    unnamed x11 -> x16, local copies, waits for them, and re-layouts: 37 us -> 2.2 us
    all_gather x3 -> x0, waiting for transfers between devices: 29.6 us -> none  [the longest x1 29.5 us: on_device(): weight_cols = lax.all_gather(text_weight, 'dp', axis=1, tiled=True)]
    all_to_all x6 -> x0, local copies, waits for them, and re-layouts: 22 us -> none  [the longest x1 12.7 us: on_device(): lax.all_to_all(video, 'seq', split_axis=2, concat_axis=0, tiled=True)]
  transfers between devices with their start and end apart: 8 -> 35, of which waited for: 4 -> 16; matrix products, arithmetic and copies ran while one was open for 45% -> 2% of each run, Pallas kernels for 0% -> 15%
where the time goes in v1:
time: 200 us; the launch traced here: 199 us
  starting transfers between devices  75.6 us (38%)
  waiting for transfers between devices  67 us (34%)
  Pallas kernels  46.9 us (23%)
  local copies, waits for them, and re-layouts  5.18 us (3%)
  other arithmetic  3.6 us (2%)
    ppermute x32, waiting for transfers between devices, trade(): return lax.ppermute(x, axis, [(i, i ^ mask) for i in range(count)])  67 us
    ppermute x32, starting transfers between devices, trade(): return lax.ppermute(x, axis, [(i, i ^ mask) for i in range(count)])  59.2 us
    pallas_call x1, Pallas kernels, on_device(): attention_call(a_kernel, 'video_attention_a', VID, 2 * VT, 1, shape(SEQ,...  15.1 us
    pallas_call x1, Pallas kernels, on_device(): attention_call(c_kernel, 'video_attention_c', VID // 2, 4 * HALF, 1, shap...  9.97 us
    all_to_all x1, starting transfers between devices, on_device(): recv = lax.all_to_all(buf, 'seq', split_axis=0, concat_axis=0, tiled=True)  7.03 us
    pallas_call x1, Pallas kernels, on_device(): attention_call(text_kernel, 'text_attention', 2 * TXT, TXT, 2, shape(SEQ,...  5.51 us
    all_to_all x1, starting transfers between devices, on_device(): lax.all_to_all(out_all, 'seq', split_axis=0, concat_axis=0, tiled=True)  4.92 us
    pallas_call x1, Pallas kernels, on_device(): pl.pallas_call(pack_kernel, out_shape=shape(SEQ, 3, ROWS, HD), in_specs=[...  4.76 us
  transfers between devices with their start and end apart: 35, of which 16 were waited for; matrix products, arithmetic and copies ran while one was open for 2% of the time, Pallas kernels for 15%

profile of v1, /device:TPU:1, one launch (start us, length us, event | category | flops | bytes accessed | tf_op | source)
XLA Modules:
  0.0 199.4 jit_solution(15229559536920712140)
XLA Ops:
  2.7 2.8 %give.1 = bf16[8,3,112,128]{3,2,1,0:T(8,128)(2,1)} custom-call(s32[24]{0:T(128)} %select_reduce_fusion.1.slots, s32[1]{0:T(128)} %bitcast.core, bf16[3,192,4096]{2,1,0:T(8,128)(2,1)} %bitcast.102, bf16[3,16,4096]{2,1,0:T(8,128)(2,1)} %bitcast.105), custom_call_target="tpu_custom_call" | custom-call | bytes 2097152 | tf_op jit(solution)/shard_map/give/pallas_call | solution.py:332
  5.5 1.5 collective-permute-start.1
  7.0 4.8 %pack.1._ = bf16[16,3,320,128]{3,2,1,0:T(8,128)(2,1)} custom-call(s32[24]{0:T(128)} %select_reduce_fusion.1.slots, s32[1]{0:T(128)} %bitcast.core, bf16[3,192,4096]{2,1,0:T(8,128)(2,1)} %bitcast.103, bf16[3,16,4096]{2,1,0:T(8,128)(2,1)} %bitcast.106), custom_call_target="tpu_custom_call" | custom-call | bytes 7340032 | tf_op jit(solution)/shard_map/pack/pallas_call | solution.py:339
  11.8 0.8 copy-done.1
  12.6 2.0 fill.1
  14.7 7.0 %all-to-all-start = ((bf16[16,3,320,128]{3,2,1,0:T(8,128)(2,1)}), bf16[16,3,320,128]{3,2,1,0:T(8,128)(2,1)}, u32[]{:S(2)}, u32[]{:S(2)}) async-start(bf16[16,3,320,128]{3,2,1,0:T(8,128)(2,1)} %fill.1), calls=%async_computation | async-start | bytes 7864320 | tf_op jit(solution)/shard_map/all_to_all | solution.py:354
  21.8 3.7 %collective-permute-start.8 = (bf16[1,4,16,384]{3,2,1,0:T(8,128)(2,1)S(1)}, bf16[1,4,16,384]{3,2,1,0:T(8,128)(2,1)S(1)}, u32[]{:S(2)}, u32[]{:S(2)}) collective-permute-start(bf16[1,4,16,384]{3,2,1,0:T(8,128)(2,1)S(1)} %get-tuple-element.44), channel_id=1, source_target_pairs={{0,64},{16,80},{32,96},{48,112},{64,0},{80,16},{96,32},{112,48},{1... | collective-permute-start | bytes 147464 | tf_op jit(solution)/shard_map/ppermute | solution.py:277
  25.5 1.9 collective-permute-done.8
  27.4 1.1 collective-permute-start.9
  28.5 2.5 %collective-permute-start.6 = (bf16[256,384]{1,0:T(8,128)(2,1)S(1)}, bf16[256,384]{1,0:T(8,128)(2,1)S(1)}, u32[]{:S(2)}, u32[]{:S(2)}) collective-permute-start(bf16[256,384]{1,0:T(8,128)(2,1)S(1)} %copy-done.3), channel_id=1, source_target_pairs={{0,3},{1,2},{2,1},{3,0},{4,7},{5,6},{6,5},{7,4},{8,11},{9,10},{10,... | collective-permute-start | bytes 589832 | tf_op jit(solution)/shard_map/ppermute | solution.py:277
  31.1 2.2 %collective-permute-start.10 = (bf16[4,1,16,384]{3,2,0,1:T(8,128)(2,1)S(1)}, bf16[4,1,16,384]{3,2,0,1:T(8,128)(2,1)S(1)}, u32[]{:S(2)}, u32[]{:S(2)}) collective-permute-start(bf16[4,1,16,384]{3,2,0,1:T(8,128)(2,1)S(1)} %get-tuple-element.40), channel_id=1, source_target_pairs={{0,16},{16,0},{32,48},{48,32},{64,80},{80,64},{96,112},{112,96},{1... | collective-permute-start | bytes 147464 | tf_op jit(solution)/shard_map/ppermute | solution.py:277
  34.2 2.5 %collective-permute-start.13 = (bf16[128,384]{1,0:T(8,128)(2,1)S(1)}, bf16[128,384]{1,0:T(8,128)(2,1)S(1)}, u32[]{:S(2)}, u32[]{:S(2)}) collective-permute-start(bf16[128,384]{1,0:T(8,128)(2,1)S(1)} %bitcast.111), channel_id=1, source_target_pairs={{0,12},{1,13},{2,14},{3,15},{4,8},{5,9},{6,10},{7,11},{8,4},{9,5},... | collective-permute-start | bytes 294920 | tf_op jit(solution)/shard_map/ppermute | solution.py:277
  36.7 36.5 %collective-permute-done.6 = bf16[256,384]{1,0:T(8,128)(2,1)S(1)} collective-permute-done((bf16[256,384]{1,0:T(8,128)(2,1)S(1)}, bf16[256,384]{1,0:T(8,128)(2,1)S(1)}, u32[]{:S(2)}, u32[]{:S(2)}) %collective-permute-start.6) | collective-permute-done | bytes 196640 | tf_op jit(solution)/shard_map/ppermute | solution.py:277
  73.2 7.6 %collective-permute-start.7 = (bf16[128,384]{1,0:T(8,128)(2,1)S(1)}, bf16[128,384]{1,0:T(8,128)(2,1)S(1)}, u32[]{:S(2)}, u32[]{:S(2)}) collective-permute-start(bf16[128,384]{1,0:T(8,128)(2,1)S(1)} %slice.99), channel_id=1, source_target_pairs={{0,1},{1,0},{2,3},{3,2},{4,5},{5,4},{6,7},{7,6},{8,9},{9,8},{10,11... | collective-permute-start | bytes 294920 | tf_op jit(solution)/shard_map/ppermute | solution.py:277
  80.8 3.1 %collective-permute-done.4 = bf16[256,384]{1,0:T(8,128)(2,1)S(1)} collective-permute-done((bf16[256,384]{1,0:T(8,128)(2,1)S(1)}, bf16[256,384]{1,0:T(8,128)(2,1)S(1)}, u32[]{:S(2)}, u32[]{:S(2)}) %collective-permute-start.4) | collective-permute-done | bytes 196640 | tf_op jit(solution)/shard_map/ppermute | solution.py:277
  83.9 0.9 collective-permute-start.5
  85.0 2.9 %collective-permute-start.12 = (bf16[64,384]{1,0:T(8,128)(2,1)S(1)}, bf16[64,384]{1,0:T(8,128)(2,1)S(1)}, u32[]{:S(2)}, u32[]{:S(2)}) collective-permute-start(bf16[64,384]{1,0:T(8,128)(2,1)S(1)} %slice.106), channel_id=1, source_target_pairs={{0,12},{1,13},{2,14},{3,15},{4,8},{5,9},{6,10},{7,11},{8,4},{9,5},... | collective-permute-start | bytes 147464 | tf_op jit(solution)/shard_map/ppermute | solution.py:277
  88.7 1.2 slice.96
  89.9 3.3 %collective-permute-start.2 = (bf16[16,2,96,128]{3,2,1,0:T(8,128)(2,1)S(1)}, bf16[16,2,96,128]{3,2,1,0:T(8,128)(2,1)S(1)}, u32[]{:S(2)}, u32[]{:S(2)}) collective-permute-start(bf16[16,2,96,128]{3,2,1,0:T(8,128)(2,1)S(1)} %slice.96), channel_id=1, source_target_pairs={{0,16},{16,0},{32,48},{48,32},{64,80},{80,64},{96,112},{112,96},{1... | collective-permute-start | bytes 2359304 | tf_op jit(solution)/shard_map/ppermute | solution.py:277
  93.5 15.1 %video_attention_a.1.out_a = bf16[16,192,128]{2,1,0:T(8,128)(2,1)S(1)} custom-call(f32[1,256]{1,0:T(1,128)S(1)} %get-tuple-element.45.bias_a, bf16[16,3,320,128]{3,2,1,0:T(8,128)(2,1)} %all-to-all-done.recv), custom_call_target="tpu_custom_call" | custom-call | flops 5234491392 | bytes 8388608 | tf_op jit(solution)/shard_map/video_attention_a/pallas_call | solution.py:365
  108.5 5.5 %text_attention.1 = bf16[16,32,128]{2,1,0:T(8,128)(2,1)} custom-call(f32[1,256]{1,0:T(1,128)S(1)} %get-tuple-element.45.bias_a, f32[1,256]{1,0:T(1,128)S(1)} %get-tuple-element.46.bias_c, bf16[16,3,320,128]{3,2,1,0:T(8,128)(2,1)} %all-to-all-done.recv, bf16[16,2,96,128]{3,2,1,0:T(8,128)(2,1)S(1)} %collective-permute-done.2.other, ...), custom_call_target="tpu_custom_call" | custom-call | flops 872415232 | bytes 8388608 | tf_op jit(solution)/shard_map/text_attention/pallas_call | solution.py:361
  114.0 4.5 %all-to-all-start.2 = ((bf16[16,32,128]{2,1,0:T(8,128)(2,1)}), bf16[16,32,128]{2,1,0:T(8,128)(2,1)S(1)}, u32[]{:S(2)}, u32[]{:S(2)}) async-start(bf16[16,32,128]{2,1,0:T(8,128)(2,1)} %text_attention.1), calls=%async_computation.2 | async-start | bytes 262144 | tf_op jit(solution)/shard_map/all_to_all | solution.py:364
  118.5 10.0 %video_attention_c.1._ = bf16[16,288,128]{2,1,0:T(8,128)(2,1)} custom-call(f32[1,256]{1,0:T(1,128)S(1)} %get-tuple-element.46.bias_c, bf16[16,3,320,128]{3,2,1,0:T(8,128)(2,1)} %all-to-all-done.recv, bf16[16,2,96,128]{3,2,1,0:T(8,128)(2,1)S(1)} %collective-permute-done.2.other, bf16[16,192,128]{2,1,0:T(8,128)(2,1)S(1)} %video_attention_a.1.out_a), custom_call_target="tpu_custom_call" | custom-call | flops 2617245696 | bytes 8388608 | tf_op jit(solution)/shard_map/video_attention_c/pallas_call | solution.py:368
  129.2 2.3 %slot_text.1 = bf16[4,16,1024]{2,1,0:T(8,128)(2,1)} custom-call(s32[32]{0:T(128)} %copy-done.6, s32[1]{0:T(128)} %bitcast.core, s32[1]{0:T(128)} %bitcast.11.seat, bf16[16,32,128]{2,1,0:T(8,128)(2,1)} %copy-done.2, bf16[16,288,128]{2,1,0:T(8,128)(2,1)} %video_attention_c.1._), custom_call_target="tpu_custom_call" | custom-call | tf_op jit(solution)/shard_map/slot_text/pallas_call | solution.py:378
  131.5 0.8 slice_bitcast_fusion.8
  132.3 2.7 %collective-permute-start.17 = (bf16[16,1024]{1,0:T(8,128)(2,1)S(1)}, bf16[16,1024]{1,0:T(8,128)(2,1)S(1)}, u32[]{:S(2)}, u32[]{:S(2)}) collective-permute-start(bf16[16,1024]{1,0:T(8,128)(2,1)S(1)} %get-tuple-element.30), channel_id=1, source_target_pairs={{0,12},{1,13},{2,14},{3,15},{4,8},{5,9},{6,10},{7,11},{8,4},{9,5},... | collective-permute-start | bytes 98312 | tf_op jit(solution)/shard_map/ppermute | solution.py:277
  136.3 2.9 %collective-permute-done.16 = bf16[16,1024]{1,0:T(8,128)(2,1)S(1)} collective-permute-done((bf16[16,1024]{1,0:T(8,128)(2,1)S(1)}, bf16[16,1024]{1,0:T(8,128)(2,1)S(1)}, u32[]{:S(2)}, u32[]{:S(2)}) %collective-permute-start.16) | collective-permute-done | bytes 32800 | tf_op jit(solution)/shard_map/ppermute | solution.py:277
  139.2 1.7 collective-permute-start.18
  140.9 2.3 %collective-permute-start.20 = (bf16[64,1024]{1,0:T(8,128)(2,1)S(1)}, bf16[64,1024]{1,0:T(8,128)(2,1)S(1)}, u32[]{:S(2)}, u32[]{:S(2)}) collective-permute-start(bf16[64,1024]{1,0:T(8,128)(2,1)S(1)} %get-tuple-element.28), channel_id=1, source_target_pairs={{0,96},{16,112},{32,64},{48,80},{64,32},{80,48},{96,0},{112,16},{1... | collective-permute-start | bytes 393224 | tf_op jit(solution)/shard_map/ppermute | solution.py:277
  143.3 3.6 %collective-permute-start.19 = (bf16[32,1024]{1,0:T(8,128)(2,1)S(1)}, bf16[32,1024]{1,0:T(8,128)(2,1)S(1)}, u32[]{:S(2)}, u32[]{:S(2)}) collective-permute-start(bf16[32,1024]{1,0:T(8,128)(2,1)S(1)} %slice.112), channel_id=1, source_target_pairs={{0,96},{16,112},{32,64},{48,80},{64,32},{80,48},{96,0},{112,16},{1... | collective-permute-start | bytes 196616 | tf_op jit(solution)/shard_map/ppermute | solution.py:277
  147.0 2.2 %collective-permute-done.19 = bf16[32,1024]{1,0:T(8,128)(2,1)S(1)} collective-permute-done((bf16[32,1024]{1,0:T(8,128)(2,1)S(1)}, bf16[32,1024]{1,0:T(8,128)(2,1)S(1)}, u32[]{:S(2)}, u32[]{:S(2)}) %collective-permute-start.19) | collective-permute-done | bytes 65568 | tf_op jit(solution)/shard_map/ppermute | solution.py:277
  149.2 1.0 collective-permute-done.21
  150.4 5.4 %collective-permute-start.22 = (bf16[4,64,1024]{2,1,0:T(8,128)(2,1)S(1)}, bf16[4,64,1024]{2,1,0:T(8,128)(2,1)S(1)}, u32[]{:S(2)}, u32[]{:S(2)}) collective-permute-start(bf16[4,64,1024]{2,1,0:T(8,128)(2,1)S(1)} %get-tuple-element.26), channel_id=1, source_target_pairs={{0,16},{16,0},{32,48},{48,32},{64,80},{80,64},{96,112},{112,96},{1... | collective-permute-start | bytes 1572872 | tf_op jit(solution)/shard_map/ppermute | solution.py:277
  155.7 1.5 collective-permute-done.22
  157.5 1.3 project.1
  158.8 2.3 %collective-permute-start.24 = (bf16[8,16,384]{2,1,0:T(8,128)(2,1)S(1)}, bf16[8,16,384]{2,1,0:T(8,128)(2,1)S(1)}, u32[]{:S(2)}, u32[]{:S(2)}) collective-permute-start(bf16[8,16,384]{2,1,0:T(8,128)(2,1)S(1)} %get-tuple-element.19), channel_id=1, source_target_pairs={{0,8},{1,9},{2,10},{3,11},{4,12},{5,13},{6,14},{7,15},{8,0},{9,1},... | collective-permute-start | bytes 294920 | tf_op jit(solution)/shard_map/ppermute | solution.py:277
  161.1 1.5 collective-permute-start.25
  162.7 4.9 %all-to-all-start.1 = ((bf16[16,288,128]{2,1,0:T(8,128)(2,1)}), bf16[16,288,128]{2,1,0:T(8,128)(2,1)S(1)}, u32[]{:S(2)}, u32[]{:S(2)}) async-start(bf16[16,288,128]{2,1,0:T(8,128)(2,1)} %video_attention_c.1._), calls=%async_computation.1 | async-start | bytes 2359296 | tf_op jit(solution)/shard_map/all_to_all | solution.py:371
  168.4 1.3 collective-permute-start.26
  169.7 3.2 %collective-permute-done.26 = bf16[1,4,16,384]{3,2,1,0:T(8,128)(2,1)S(1)} collective-permute-done((bf16[1,4,16,384]{3,2,1,0:T(8,128)(2,1)S(1)}, bf16[1,4,16,384]{3,2,1,0:T(8,128)(2,1)S(1)}, u32[]{:S(2)}, u32[]{:S(2)}) %collective-permute-start.26) | collective-permute-done | bytes 49184 | tf_op jit(solution)/shard_map/ppermute | solution.py:277
  173.1 1.3 collective-permute-start.29
  174.3 2.4 %collective-permute-start.30 = (bf16[256,384]{1,0:T(8,128)(2,1)S(1)}, bf16[256,384]{1,0:T(8,128)(2,1)S(1)}, u32[]{:S(2)}, u32[]{:S(2)}) collective-permute-start(bf16[256,384]{1,0:T(8,128)(2,1)S(1)} %get-tuple-element.23), channel_id=1, source_target_pairs={{0,2},{1,3},{2,0},{3,1},{4,6},{5,7},{6,4},{7,5},{8,10},{9,11},{10,... | collective-permute-start | bytes 589832 | tf_op jit(solution)/shard_map/ppermute | solution.py:277
  177.0 2.8 %collective-permute-start.28 = (bf16[4,1,16,384]{3,2,0,1:T(8,128)(2,1)S(1)}, bf16[4,1,16,384]{3,2,0,1:T(8,128)(2,1)S(1)}, u32[]{:S(2)}, u32[]{:S(2)}) collective-permute-start(bf16[4,1,16,384]{3,2,0,1:T(8,128)(2,1)S(1)} %get-tuple-element.34), channel_id=1, source_target_pairs={{0,16},{16,0},{32,48},{48,32},{64,80},{80,64},{96,112},{112,96},{1... | collective-permute-start | bytes 147464 | tf_op jit(solution)/shard_map/ppermute | solution.py:277
  179.9 5.4 %collective-permute-done.29 = bf16[256,384]{1,0:T(8,128)(2,1)S(1)} collective-permute-done((bf16[256,384]{1,0:T(8,128)(2,1)S(1)}, bf16[256,384]{1,0:T(8,128)(2,1)S(1)}, u32[]{:S(2)}, u32[]{:S(2)}) %collective-permute-start.29) | collective-permute-done | bytes 196640 | tf_op jit(solution)/shard_map/ppermute | solution.py:277
  185.3 5.7 %collective-permute-done.30 = bf16[256,384]{1,0:T(8,128)(2,1)S(1)} collective-permute-done((bf16[256,384]{1,0:T(8,128)(2,1)S(1)}, bf16[256,384]{1,0:T(8,128)(2,1)S(1)}, u32[]{:S(2)}, u32[]{:S(2)}) %collective-permute-start.30) | collective-permute-done | bytes 196640 | tf_op jit(solution)/shard_map/ppermute | solution.py:277
  191.0 0.8 convert_add_fusion
  191.9 2.5 %collective-permute-start.3 = (bf16[8,96,128]{2,1,0:T(8,128)(2,1)S(1)}, bf16[8,96,128]{2,1,0:T(8,128)(2,1)S(1)}, u32[]{:S(2)}, u32[]{:S(2)}) collective-permute-start(bf16[8,96,128]{2,1,0:T(8,128)(2,1)S(1)} %dynamic-slice_bitcast_fusion), channel_id=1, source_target_pairs={{0,16},{16,0},{32,48},{48,32},{64,80},{80,64},{96,112},{112,96},{1... | collective-permute-start | bytes 589832 | tf_op jit(solution)/shard_map/ppermute | solution.py:277
  196.2 3.3 %slot_video.1 = bf16[192,4096]{1,0:T(8,128)(2,1)} custom-call(s32[32]{0:T(128)} %copy-done.6, s32[1]{0:T(128)} %bitcast.core, bf16[16,288,128]{2,1,0:T(8,128)(2,1)} %copy-done, bf16[8,96,128]{2,1,0:T(8,128)(2,1)} %copy-done.4), custom_call_target="tpu_custom_call" | custom-call | tf_op jit(solution)/shard_map/slot_video/pallas_call | solution.py:374
  (91 shorter events, 10.0 us)
Async XLA Ops:
  2.1 9.7 %copy-start.6 = (s32[32]{0:T(128)}, s32[32]{0:T(128)S(1)}, u32[]{:S(2)}) copy-start(s32[32]{0:T(128)S(1)} %compare_select_fusion.2.ranks) | copy-start | bytes 388
  5.5 6.3 %collective-permute-start.1 = (bf16[8,3,112,128]{3,2,1,0:T(8,128)(2,1)}, bf16[8,3,112,128]{3,2,1,0:T(8,128)(2,1)S(1)}, u32[]{:S(2)}, u32[]{:S(2)}) collective-permute-start(bf16[8,3,112,128]{3,2,1,0:T(8,128)(2,1)} %give.1), channel_id=1, source_target_pairs={{0,16},{16,0},{32,48},{48,32},{64,80},{80,64},{96,112},{112,96},{1... | collective-permute-start | bytes 2064392 | tf_op jit(solution)/shard_map/ppermute | solution.py:277
  11.8 0.8 copy-start.1
  14.6 7.1 %copy-start.5 = (bf16[1,16,3072]{2,1,0:T(8,128)(2,1)S(1)}, bf16[1,16,3072]{2,1,0:T(8,128)(2,1)}, u32[]{:S(2)}) copy-start(bf16[1,16,3072]{2,1,0:T(8,128)(2,1)} %param.11) | copy-start | bytes 294916
  14.6 13.9 %copy-start.3 = (bf16[256,384]{1,0:T(8,128)(2,1)S(1)}, bf16[256,384]{1,0:T(8,128)(2,1)}, u32[]{:S(2)}) copy-start(bf16[256,384]{1,0:T(8,128)(2,1)} %param.10) | copy-start | bytes 589828
  14.6 18.7 %copy-start.7 = (s32[1,256]{1,0:T(1,128)S(1)}, s32[1,256]{1,0:T(1,128)}, u32[]{:S(2)}) copy-start(s32[1,256]{1,0:T(1,128)} %param.9) | copy-start | bytes 3076
  14.7 74.1 %all-to-all-start = ((bf16[16,3,320,128]{3,2,1,0:T(8,128)(2,1)}), bf16[16,3,320,128]{3,2,1,0:T(8,128)(2,1)}, u32[]{:S(2)}, u32[]{:S(2)}) async-start(bf16[16,3,320,128]{3,2,1,0:T(8,128)(2,1)} %fill.1), calls=%async_computation | async-start | bytes 7864320 | tf_op jit(solution)/shard_map/all_to_all | solution.py:354
  21.8 5.6 %collective-permute-start.8 = (bf16[1,4,16,384]{3,2,1,0:T(8,128)(2,1)S(1)}, bf16[1,4,16,384]{3,2,1,0:T(8,128)(2,1)S(1)}, u32[]{:S(2)}, u32[]{:S(2)}) collective-permute-start(bf16[1,4,16,384]{3,2,1,0:T(8,128)(2,1)S(1)} %get-tuple-element.44), channel_id=1, source_target_pairs={{0,64},{16,80},{32,96},{48,112},{64,0},{80,16},{96,32},{112,48},{1... | collective-permute-start | bytes 147464 | tf_op jit(solution)/shard_map/ppermute | solution.py:277
  27.4 3.6 %collective-permute-start.9 = (bf16[2,2,16,384]{3,2,0,1:T(8,128)(2,1)S(1)}, bf16[2,2,16,384]{3,2,0,1:T(8,128)(2,1)S(1)}, u32[]{:S(2)}, u32[]{:S(2)}) collective-permute-start(bf16[2,2,16,384]{3,2,0,1:T(8,128)(2,1)S(1)} %get-tuple-element.42), channel_id=1, source_target_pairs={{0,32},{16,48},{32,0},{48,16},{64,96},{80,112},{96,64},{112,80},{1... | collective-permute-start | bytes 147464 | tf_op jit(solution)/shard_map/ppermute | solution.py:277
  28.5 44.7 %collective-permute-start.6 = (bf16[256,384]{1,0:T(8,128)(2,1)S(1)}, bf16[256,384]{1,0:T(8,128)(2,1)S(1)}, u32[]{:S(2)}, u32[]{:S(2)}) collective-permute-start(bf16[256,384]{1,0:T(8,128)(2,1)S(1)} %copy-done.3), channel_id=1, source_target_pairs={{0,3},{1,2},{2,1},{3,0},{4,7},{5,6},{6,5},{7,4},{8,11},{9,10},{10,... | collective-permute-start | bytes 589832 | tf_op jit(solution)/shard_map/ppermute | solution.py:277
  31.0 52.9 %collective-permute-start.4 = (bf16[256,384]{1,0:T(8,128)(2,1)S(1)}, bf16[256,384]{1,0:T(8,128)(2,1)S(1)}, u32[]{:S(2)}, u32[]{:S(2)}) collective-permute-start(bf16[256,384]{1,0:T(8,128)(2,1)S(1)} %copy-done.3), channel_id=1, source_target_pairs={{0,1},{1,0},{2,3},{3,2},{4,5},{5,4},{6,7},{7,6},{8,9},{9,8},{10,11... | collective-permute-start | bytes 589832 | tf_op jit(solution)/shard_map/ppermute | solution.py:277
  31.1 3.1 %collective-permute-start.10 = (bf16[4,1,16,384]{3,2,0,1:T(8,128)(2,1)S(1)}, bf16[4,1,16,384]{3,2,0,1:T(8,128)(2,1)S(1)}, u32[]{:S(2)}, u32[]{:S(2)}) collective-permute-start(bf16[4,1,16,384]{3,2,0,1:T(8,128)(2,1)S(1)} %get-tuple-element.40), channel_id=1, source_target_pairs={{0,16},{16,0},{32,48},{48,32},{64,80},{80,64},{96,112},{112,96},{1... | collective-permute-start | bytes 147464 | tf_op jit(solution)/shard_map/ppermute | solution.py:277
  33.3 51.6 %collective-permute-start = (s32[1,256]{1,0:T(1,128)S(1)}, s32[1,256]{1,0:T(1,128)S(1)}, u32[]{:S(2)}, u32[]{:S(2)}) collective-permute-start(s32[1,256]{1,0:T(1,128)S(1)} %copy-done.7), channel_id=1, source_target_pairs={{0,16},{16,0},{32,48},{48,32},{64,80},{80,64},{96,112},{112,96},{1... | collective-permute-start | bytes 3080 | tf_op jit(solution)/shard_map/ppermute | solution.py:277
  34.2 50.7 %collective-permute-start.13 = (bf16[128,384]{1,0:T(8,128)(2,1)S(1)}, bf16[128,384]{1,0:T(8,128)(2,1)S(1)}, u32[]{:S(2)}, u32[]{:S(2)}) collective-permute-start(bf16[128,384]{1,0:T(8,128)(2,1)S(1)} %bitcast.111), channel_id=1, source_target_pairs={{0,12},{1,13},{2,14},{3,15},{4,8},{5,9},{6,10},{7,11},{8,4},{9,5},... | collective-permute-start | bytes 294920 | tf_op jit(solution)/shard_map/ppermute | solution.py:277
  36.7 48.3 %collective-permute-start.11 = (bf16[128,384]{1,0:T(8,128)(2,1)S(1)}, bf16[128,384]{1,0:T(8,128)(2,1)S(1)}, u32[]{:S(2)}, u32[]{:S(2)}) collective-permute-start(bf16[128,384]{1,0:T(8,128)(2,1)S(1)} %bitcast.112), channel_id=1, source_target_pairs={{0,4},{1,5},{2,6},{3,7},{4,0},{5,1},{6,2},{7,3},{8,12},{9,13},{10,... | collective-permute-start | bytes 294920 | tf_op jit(solution)/shard_map/ppermute | solution.py:277
  73.2 14.7 %collective-permute-start.7 = (bf16[128,384]{1,0:T(8,128)(2,1)S(1)}, bf16[128,384]{1,0:T(8,128)(2,1)S(1)}, u32[]{:S(2)}, u32[]{:S(2)}) collective-permute-start(bf16[128,384]{1,0:T(8,128)(2,1)S(1)} %slice.99), channel_id=1, source_target_pairs={{0,1},{1,0},{2,3},{3,2},{4,5},{5,4},{6,7},{7,6},{8,9},{9,8},{10,11... | collective-permute-start | bytes 294920 | tf_op jit(solution)/shard_map/ppermute | solution.py:277
  83.9 4.8 %collective-permute-start.5 = (bf16[128,384]{1,0:T(8,128)(2,1)S(1)}, bf16[128,384]{1,0:T(8,128)(2,1)S(1)}, u32[]{:S(2)}, u32[]{:S(2)}) collective-permute-start(bf16[128,384]{1,0:T(8,128)(2,1)S(1)} %slice.98), channel_id=1, source_target_pairs={{0,3},{1,2},{2,1},{3,0},{4,7},{5,6},{6,5},{7,4},{8,11},{9,10},{10,... | collective-permute-start | bytes 294920 | tf_op jit(solution)/shard_map/ppermute | solution.py:277
  84.9 8.5 %collective-permute-start.14 = (bf16[64,384]{1,0:T(8,128)(2,1)S(1)}, bf16[64,384]{1,0:T(8,128)(2,1)S(1)}, u32[]{:S(2)}, u32[]{:S(2)}) collective-permute-start(bf16[64,384]{1,0:T(8,128)(2,1)S(1)} %slice.107), channel_id=1, source_target_pairs={{0,4},{1,5},{2,6},{3,7},{4,0},{5,1},{6,2},{7,3},{8,12},{9,13},{10,... | collective-permute-start | bytes 147464 | tf_op jit(solution)/shard_map/ppermute | solution.py:277
  85.0 8.4 %collective-permute-start.12 = (bf16[64,384]{1,0:T(8,128)(2,1)S(1)}, bf16[64,384]{1,0:T(8,128)(2,1)S(1)}, u32[]{:S(2)}, u32[]{:S(2)}) collective-permute-start(bf16[64,384]{1,0:T(8,128)(2,1)S(1)} %slice.106), channel_id=1, source_target_pairs={{0,12},{1,13},{2,14},{3,15},{4,8},{5,9},{6,10},{7,11},{8,4},{9,5},... | collective-permute-start | bytes 147464 | tf_op jit(solution)/shard_map/ppermute | solution.py:277
  89.9 18.6 %collective-permute-start.2 = (bf16[16,2,96,128]{3,2,1,0:T(8,128)(2,1)S(1)}, bf16[16,2,96,128]{3,2,1,0:T(8,128)(2,1)S(1)}, u32[]{:S(2)}, u32[]{:S(2)}) collective-permute-start(bf16[16,2,96,128]{3,2,1,0:T(8,128)(2,1)S(1)} %slice.96), channel_id=1, source_target_pairs={{0,16},{16,0},{32,48},{48,32},{64,80},{80,64},{96,112},{112,96},{1... | collective-permute-start | bytes 2359304 | tf_op jit(solution)/shard_map/ppermute | solution.py:277
  114.0 14.5 %all-to-all-start.2 = ((bf16[16,32,128]{2,1,0:T(8,128)(2,1)}), bf16[16,32,128]{2,1,0:T(8,128)(2,1)S(1)}, u32[]{:S(2)}, u32[]{:S(2)}) async-start(bf16[16,32,128]{2,1,0:T(8,128)(2,1)} %text_attention.1), calls=%async_computation.2 | async-start | bytes 262144 | tf_op jit(solution)/shard_map/all_to_all | solution.py:364
  128.5 0.7 copy-start.2
  132.3 4.1 %collective-permute-start.17 = (bf16[16,1024]{1,0:T(8,128)(2,1)S(1)}, bf16[16,1024]{1,0:T(8,128)(2,1)S(1)}, u32[]{:S(2)}, u32[]{:S(2)}) collective-permute-start(bf16[16,1024]{1,0:T(8,128)(2,1)S(1)} %get-tuple-element.30), channel_id=1, source_target_pairs={{0,12},{1,13},{2,14},{3,15},{4,8},{5,9},{6,10},{7,11},{8,4},{9,5},... | collective-permute-start | bytes 98312 | tf_op jit(solution)/shard_map/ppermute | solution.py:277
  134.9 4.3 %collective-permute-start.16 = (bf16[16,1024]{1,0:T(8,128)(2,1)S(1)}, bf16[16,1024]{1,0:T(8,128)(2,1)S(1)}, u32[]{:S(2)}, u32[]{:S(2)}) collective-permute-start(bf16[16,1024]{1,0:T(8,128)(2,1)S(1)} %get-tuple-element.31), channel_id=1, source_target_pairs={{0,8},{1,9},{2,10},{3,11},{4,12},{5,13},{6,14},{7,15},{8,0},{9,1},... | collective-permute-start | bytes 98312 | tf_op jit(solution)/shard_map/ppermute | solution.py:277
  135.5 3.7 %collective-permute-start.15 = (bf16[16,1024]{1,0:T(8,128)(2,1)S(1)}, bf16[16,1024]{1,0:T(8,128)(2,1)S(1)}, u32[]{:S(2)}, u32[]{:S(2)}) collective-permute-start(bf16[16,1024]{1,0:T(8,128)(2,1)S(1)} %get-tuple-element.32), channel_id=1, source_target_pairs={{0,4},{1,5},{2,6},{3,7},{4,0},{5,1},{6,2},{7,3},{8,12},{9,13},{10,... | collective-permute-start | bytes 98312 | tf_op jit(solution)/shard_map/ppermute | solution.py:277
  139.2 4.1 %collective-permute-start.18 = (bf16[64,1024]{1,0:T(8,128)(2,1)S(1)}, bf16[64,1024]{1,0:T(8,128)(2,1)S(1)}, u32[]{:S(2)}, u32[]{:S(2)}) collective-permute-start(bf16[64,1024]{1,0:T(8,128)(2,1)S(1)} %get-tuple-element.28), channel_id=1, source_target_pairs={{0,32},{16,48},{32,0},{48,16},{64,96},{80,112},{96,64},{112,80},{1... | collective-permute-start | bytes 393224 | tf_op jit(solution)/shard_map/ppermute | solution.py:277
  140.9 6.0 %collective-permute-start.20 = (bf16[64,1024]{1,0:T(8,128)(2,1)S(1)}, bf16[64,1024]{1,0:T(8,128)(2,1)S(1)}, u32[]{:S(2)}, u32[]{:S(2)}) collective-permute-start(bf16[64,1024]{1,0:T(8,128)(2,1)S(1)} %get-tuple-element.28), channel_id=1, source_target_pairs={{0,96},{16,112},{32,64},{48,80},{64,32},{80,48},{96,0},{112,16},{1... | collective-permute-start | bytes 393224 | tf_op jit(solution)/shard_map/ppermute | solution.py:277
  143.3 5.9 %collective-permute-start.19 = (bf16[32,1024]{1,0:T(8,128)(2,1)S(1)}, bf16[32,1024]{1,0:T(8,128)(2,1)S(1)}, u32[]{:S(2)}, u32[]{:S(2)}) collective-permute-start(bf16[32,1024]{1,0:T(8,128)(2,1)S(1)} %slice.112), channel_id=1, source_target_pairs={{0,96},{16,112},{32,64},{48,80},{64,32},{80,48},{96,0},{112,16},{1... | collective-permute-start | bytes 196616 | tf_op jit(solution)/shard_map/ppermute | solution.py:277
  146.9 3.3 %collective-permute-start.21 = (bf16[32,1024]{1,0:T(8,128)(2,1)S(1)}, bf16[32,1024]{1,0:T(8,128)(2,1)S(1)}, u32[]{:S(2)}, u32[]{:S(2)}) collective-permute-start(bf16[32,1024]{1,0:T(8,128)(2,1)S(1)} %slice.113), channel_id=1, source_target_pairs={{0,32},{16,48},{32,0},{48,16},{64,96},{80,112},{96,64},{112,80},{1... | collective-permute-start | bytes 196616 | tf_op jit(solution)/shard_map/ppermute | solution.py:277
  150.4 6.9 %collective-permute-start.22 = (bf16[4,64,1024]{2,1,0:T(8,128)(2,1)S(1)}, bf16[4,64,1024]{2,1,0:T(8,128)(2,1)S(1)}, u32[]{:S(2)}, u32[]{:S(2)}) collective-permute-start(bf16[4,64,1024]{2,1,0:T(8,128)(2,1)S(1)} %get-tuple-element.26), channel_id=1, source_target_pairs={{0,16},{16,0},{32,48},{48,32},{64,80},{80,64},{96,112},{112,96},{1... | collective-permute-start | bytes 1572872 | tf_op jit(solution)/shard_map/ppermute | solution.py:277
  158.7 8.9 %collective-permute-start.23 = (bf16[8,16,384]{2,1,0:T(8,128)(2,1)S(1)}, bf16[8,16,384]{2,1,0:T(8,128)(2,1)S(1)}, u32[]{:S(2)}, u32[]{:S(2)}) collective-permute-start(bf16[8,16,384]{2,1,0:T(8,128)(2,1)S(1)} %get-tuple-element.18), channel_id=1, source_target_pairs={{0,4},{1,5},{2,6},{3,7},{4,0},{5,1},{6,2},{7,3},{8,12},{9,13},{10,... | collective-permute-start | bytes 294920 | tf_op jit(solution)/shard_map/ppermute | solution.py:277
  158.8 8.8 %collective-permute-start.24 = (bf16[8,16,384]{2,1,0:T(8,128)(2,1)S(1)}, bf16[8,16,384]{2,1,0:T(8,128)(2,1)S(1)}, u32[]{:S(2)}, u32[]{:S(2)}) collective-permute-start(bf16[8,16,384]{2,1,0:T(8,128)(2,1)S(1)} %get-tuple-element.19), channel_id=1, source_target_pairs={{0,8},{1,9},{2,10},{3,11},{4,12},{5,13},{6,14},{7,15},{8,0},{9,1},... | collective-permute-start | bytes 294920 | tf_op jit(solution)/shard_map/ppermute | solution.py:277
  161.1 7.2 %collective-permute-start.25 = (bf16[8,16,384]{2,1,0:T(8,128)(2,1)S(1)}, bf16[8,16,384]{2,1,0:T(8,128)(2,1)S(1)}, u32[]{:S(2)}, u32[]{:S(2)}) collective-permute-start(bf16[8,16,384]{2,1,0:T(8,128)(2,1)S(1)} %get-tuple-element.20), channel_id=1, source_target_pairs={{0,12},{1,13},{2,14},{3,15},{4,8},{5,9},{6,10},{7,11},{8,4},{9,5},... | collective-permute-start | bytes 294920 | tf_op jit(solution)/shard_map/ppermute | solution.py:277
  162.7 29.2 %all-to-all-start.1 = ((bf16[16,288,128]{2,1,0:T(8,128)(2,1)}), bf16[16,288,128]{2,1,0:T(8,128)(2,1)S(1)}, u32[]{:S(2)}, u32[]{:S(2)}) async-start(bf16[16,288,128]{2,1,0:T(8,128)(2,1)} %video_attention_c.1._), calls=%async_computation.1 | async-start | bytes 2359296 | tf_op jit(solution)/shard_map/all_to_all | solution.py:371
  168.4 4.5 %collective-permute-start.26 = (bf16[1,4,16,384]{3,2,1,0:T(8,128)(2,1)S(1)}, bf16[1,4,16,384]{3,2,1,0:T(8,128)(2,1)S(1)}, u32[]{:S(2)}, u32[]{:S(2)}) collective-permute-start(bf16[1,4,16,384]{3,2,1,0:T(8,128)(2,1)S(1)} %get-tuple-element.38), channel_id=1, source_target_pairs={{0,64},{16,80},{32,96},{48,112},{64,0},{80,16},{96,32},{112,48},{1... | collective-permute-start | bytes 147464 | tf_op jit(solution)/shard_map/ppermute | solution.py:277
  173.0 4.0 %collective-permute-start.27 = (bf16[2,2,16,384]{3,2,1,0:T(8,128)(2,1)S(1)}, bf16[2,2,16,384]{3,2,1,0:T(8,128)(2,1)S(1)}, u32[]{:S(2)}, u32[]{:S(2)}) collective-permute-start(bf16[2,2,16,384]{3,2,1,0:T(8,128)(2,1)S(1)} %get-tuple-element.36), channel_id=1, source_target_pairs={{0,32},{16,48},{32,0},{48,16},{64,96},{80,112},{96,64},{112,80},{1... | collective-permute-start | bytes 147464 | tf_op jit(solution)/shard_map/ppermute | solution.py:277
  173.1 12.3 %collective-permute-start.29 = (bf16[256,384]{1,0:T(8,128)(2,1)S(1)}, bf16[256,384]{1,0:T(8,128)(2,1)S(1)}, u32[]{:S(2)}, u32[]{:S(2)}) collective-permute-start(bf16[256,384]{1,0:T(8,128)(2,1)S(1)} %get-tuple-element.22), channel_id=1, source_target_pairs={{0,1},{1,0},{2,3},{3,2},{4,5},{5,4},{6,7},{7,6},{8,9},{9,8},{10,11... | collective-permute-start | bytes 589832 | tf_op jit(solution)/shard_map/ppermute | solution.py:277
  174.3 16.7 %collective-permute-start.30 = (bf16[256,384]{1,0:T(8,128)(2,1)S(1)}, bf16[256,384]{1,0:T(8,128)(2,1)S(1)}, u32[]{:S(2)}, u32[]{:S(2)}) collective-permute-start(bf16[256,384]{1,0:T(8,128)(2,1)S(1)} %get-tuple-element.23), channel_id=1, source_target_pairs={{0,2},{1,3},{2,0},{3,1},{4,6},{5,7},{6,4},{7,5},{8,10},{9,11},{10,... | collective-permute-start | bytes 589832 | tf_op jit(solution)/shard_map/ppermute | solution.py:277
  176.7 14.3 %collective-permute-start.31 = (bf16[256,384]{1,0:T(8,128)(2,1)S(1)}, bf16[256,384]{1,0:T(8,128)(2,1)S(1)}, u32[]{:S(2)}, u32[]{:S(2)}) collective-permute-start(bf16[256,384]{1,0:T(8,128)(2,1)S(1)} %get-tuple-element.24), channel_id=1, source_target_pairs={{0,3},{1,2},{2,1},{3,0},{4,7},{5,6},{6,5},{7,4},{8,11},{9,10},{10,... | collective-permute-start | bytes 589832 | tf_op jit(solution)/shard_map/ppermute | solution.py:277
  177.0 17.4 %collective-permute-start.28 = (bf16[4,1,16,384]{3,2,0,1:T(8,128)(2,1)S(1)}, bf16[4,1,16,384]{3,2,0,1:T(8,128)(2,1)S(1)}, u32[]{:S(2)}, u32[]{:S(2)}) collective-permute-start(bf16[4,1,16,384]{3,2,0,1:T(8,128)(2,1)S(1)} %get-tuple-element.34), channel_id=1, source_target_pairs={{0,16},{16,0},{32,48},{48,32},{64,80},{80,64},{96,112},{112,96},{1... | collective-permute-start | bytes 147464 | tf_op jit(solution)/shard_map/ppermute | solution.py:277
  191.9 3.6 %copy-start = (bf16[16,288,128]{2,1,0:T(8,128)(2,1)}, bf16[16,288,128]{2,1,0:T(8,128)(2,1)S(1)}, u32[]{:S(2)}) copy-start(bf16[16,288,128]{2,1,0:T(8,128)(2,1)S(1)} %all-to-all-done.1.got) | copy-start | bytes 3538948
  191.9 3.5 %collective-permute-start.3 = (bf16[8,96,128]{2,1,0:T(8,128)(2,1)S(1)}, bf16[8,96,128]{2,1,0:T(8,128)(2,1)S(1)}, u32[]{:S(2)}, u32[]{:S(2)}) collective-permute-start(bf16[8,96,128]{2,1,0:T(8,128)(2,1)S(1)} %dynamic-slice_bitcast_fusion), channel_id=1, source_target_pairs={{0,16},{16,0},{32,48},{48,32},{64,80},{80,64},{96,112},{112,96},{1... | collective-permute-start | bytes 589832 | tf_op jit(solution)/shard_map/ppermute | solution.py:277
  195.5 0.7 copy-start.4

commit v2 on v1

--- a/solution.py
+++ b/solution.py
@@ -36,11 +36,23 @@
         copy.wait()
 
 
+def list_live(live, slots):
+    def body(h, counts):
+        alive = live[h] > 0
+        at = jnp.where(alive, counts[0], LIVE + counts[1])
+        slots[jnp.clip(at, 0, SLOTS - 1)] = h
+        one = jnp.where(alive, 1, 0)
+        return counts[0] + one, counts[1] + 1 - one
+
+    lax.fori_loop(0, SLOTS, body, (jnp.int32(0), jnp.int32(0)))
+
+
 def head_columns(slots, rank):
     return pl.ds(pl.multiple_of(slots[rank] * HD, HD), HD)
 
 
-def give_kernel(slots, core, video, text, give, sem):
+def give_kernel(live, core, video, text, give, slots, sem):
+    list_live(live, slots)
     start = pl.multiple_of((1 - core[0]) * HALF, 16)
     copies = []
     for j in range(8):
@@ -52,7 +64,8 @@
     run_all(copies)
 
 
-def pack_kernel(slots, core, video, text, buf, sem):
+def pack_kernel(live, core, video, text, buf, slots, sem):
+    list_live(live, slots)
     start = pl.multiple_of(core[0] * HALF, 16)
     copies = []
     for r in range(16):
@@ -76,7 +89,7 @@
     for j in range(8):
         to = 2 * j + 1 - core[0]
         copies.append(pltpu.make_async_copy(
-            got.at[j], buf.at[to, :, pl.ds(VT + TT, HALF + TT), :], sem.at[0]))
+            got.at[j], buf.at[to, :, pl.ds(VT + TT, HALF + TT), :], sem))
     run_all(copies)
 
 
@@ -146,16 +159,23 @@
     return (total[:, 0:HD] / total[:, HD:]).astype(BF16)
 
 
-def text_kernel(bias_a, bias_c, recv, other, _w, _c, out, scores, tops, keys_a, values_a, keys_c, values_c):
+def put_text(out, at, got):
+    got = got.reshape(4, 4, TT, HD)
+    for s in range(SEQ):
+        for y in range(4):
+            out[s, at + y * TT:at + (y + 1) * TT, :] = got[y, s % 4]
+
+
+def text_kernel(bias_a, bias_c, recv, other, out, token, scores, tops, keys_a, values_a, keys_c, values_c):
     lay_a(recv, keys_a, values_a)
     ba, bc = bias_a[...], bias_c[...]
     score_block(recv[:, 0, VT:VT + TT, :].reshape(TXT, HD), keys_a, ba, scores, tops, 0)
     lay_c(recv, other, keys_c, values_c)
     query = recv[:, 0, VT + TT + HALF:ROWS, :].reshape(TXT, HD)
     got = attend_block(TXT, values_a, scores, tops, 0, (query, keys_c, bc))
-    out[:, 0:TT, :] = got.reshape(SEQ, TT, HD)
-    got = attend_block(TXT, values_c, scores, tops, 1)
-    out[:, TT:2 * TT, :] = got.reshape(SEQ, TT, HD)
+    put_text(out, 0, got)
+    put_text(out, 4 * TT, attend_block(TXT, values_c, scores, tops, 1))
+    token[...] = jnp.zeros_like(token)
 
 
 def video_blocks(count, rows, load, store, keys, values, bias, scores, tops):
@@ -175,7 +195,7 @@
     step(count - 1, 1, False)
 
 
-def a_kernel(bias_a, recv, out, scores, tops, keys, values):
+def a_kernel(bias_a, recv, _, out, token, scores, tops, keys, values):
     lay_a(recv, keys, values)
 
     def load(i):
@@ -185,39 +205,34 @@
         out[pl.ds(2 * i, 2)] = got.reshape(2, VT, HD)
 
     video_blocks(8, 2 * VT, load, store, keys, values, bias_a[...], scores, tops)
-
-
-def c_kernel(bias_c, recv, other, out_a, out, scores, tops, keys, values):
+    token[...] = jnp.zeros_like(token)
+
+
+def c_kernel(bias_c, recv, other, out_a, _, out, token, scores, tops, keys, values):
+    out[:, 0:VT, :] = out_a[...]
+    token[...] = jnp.zeros_like(token)
     lay_c(recv, other, keys, values)
-    out[:, 0:VT, :] = out_a[...]
 
     def load(i):
         return recv[pl.ds(4 * i, 4), 0, VT + TT:VT + TT + HALF, :].reshape(4 * HALF, HD)
 
     def store(i, got):
-        out[pl.ds(4 * i, 4), VT:VT + HALF, :] = got.reshape(4, HALF, HD)
+        out[pl.ds(4 * i, 4), VT:, :] = got.reshape(4, HALF, HD)
 
     video_blocks(4, 4 * HALF, load, store, keys, values, bias_c[...], scores, tops)
 
 
-def slot_text_kernel(ranks, core, seat, got, _, out):
-    for h in range(SLOTS):
-        rank = ranks[h]
-        group = (h // 8) ^ (seat[0] // 4)
-        pair = ((h // 2) % 4) ^ (seat[0] % 4)
-        cols = pl.ds(pl.multiple_of((pair * 2 + h % 2) * HD, HD), HD)
-
-        @pl.when(rank < 0)
-        def _():
-            out[group, :, cols] = jnp.zeros((TT, HD), BF16)
-
-        @pl.when((rank >= 0) & (rank < 16))
-        def _():
-            out[group, :, cols] = got[jnp.clip(rank, 0, 15), 0:TT, :]
-
-        @pl.when(rank >= 16)
-        def _():
-            out[group, :, cols] = got[2 * jnp.clip(rank - 16, 0, 7) + core[0], TT:2 * TT, :]
+def slot_text_kernel(ranks, core, seat, got, _t, _w, _c, out, token):
+    token[...] = jnp.zeros_like(token)
+    y, x = seat[0] // 4, seat[0] % 4
+    for k in range(8):
+        rank = ranks[8 * y + k]
+        cols = pl.ds(pl.multiple_of((((k // 2) ^ x) * 2 + k % 2) * HD, HD), HD)
+        source = jnp.where(rank < 16, jnp.clip(rank, 0, 15), 2 * jnp.clip(rank - 16, 0, 7) + core[0])
+        base = jnp.where(rank < 16, 0, 4 * TT)
+        for j in range(4):
+            block = got[source, pl.ds(pl.multiple_of(base + (j ^ y) * TT, TT), TT), :]
+            out[j * TT:(j + 1) * TT, cols] = jnp.where(rank >= 0, block, jnp.zeros_like(block))
 
 
 def project_kernel(rows, weight, cot, p0, p1, p2, p3, g0, g1, g2, g3):
@@ -231,26 +246,17 @@
         ref[...] = term.astype(ref.dtype)
 
 
-def slot_video_kernel(ranks, core, got, other, out):
+def slot_video_kernel(live, core, got, other, out, slots):
+    list_live(live, slots)
     mine = pl.multiple_of(core[0] * HALF, 16)
     far = pl.multiple_of((1 - core[0]) * HALF, 16)
-    for h in range(SLOTS):
-        rank = ranks[h]
-        cols = pl.ds(h * HD, HD)
-
-        @pl.when(rank < 0)
-        def _():
-            out[:, cols] = jnp.zeros((VT, HD), BF16)
-
-        @pl.when((rank >= 0) & (rank < 16))
-        def _():
-            out[:, cols] = got[jnp.clip(rank, 0, 15), 0:VT, :]
-
-        @pl.when(rank >= 16)
-        def _():
-            j = jnp.clip(rank - 16, 0, 7)
-            out[pl.ds(mine, HALF), cols] = got[2 * j + core[0], VT:VT + HALF, :]
-            out[pl.ds(far, HALF), cols] = other[j]
+    for r in range(16):
+        out[:, head_columns(slots, r)] = got[r, 0:VT, :]
+    for j in range(8):
+        cols = head_columns(slots, 16 + j)
+        out[pl.ds(mine, HALF), cols] = got[2 * j + core[0], VT:, :]
+        out[pl.ds(far, HALF), cols] = other[j]
+        out[:, head_columns(slots, LIVE + j)] = jnp.zeros((VT, HD), BF16)
 
 
 def shape(*dims, dtype=BF16):
@@ -267,9 +273,10 @@
     for _ in range(heads):
         scratch += [pltpu.VMEM((N, HD), BF16), pltpu.VMEM((N, 2 * HD), BF16)]
     return pl.pallas_call(
-        kernel, out_shape=out_shape, in_specs=specs, out_specs=VMEM, scratch_shapes=scratch,
+        kernel, out_shape=[out_shape, shape(8, HD, dtype=F32)], in_specs=specs,
+        out_specs=[VMEM, VMEM], scratch_shapes=scratch,
         cost_estimate=cost(rows), name=name,
-        compiler_params=pltpu.CompilerParams(vmem_limit_bytes=40 << 20))
+        compiler_params=pltpu.CompilerParams(vmem_limit_bytes=22 << 20))
 
 
 def trade(x, axis, mask):
@@ -290,25 +297,20 @@
     return x
 
 
-def gather4(x, axis, low):
-    near, far = trade(x, axis, low), trade(x, axis, 3 * low)
-    half = x.shape[0] // 2
-    opposite = jnp.concatenate(
-        [trade(near[:half], axis, 3 * low), trade(far[half:], axis, low)], axis=0)
-    return jnp.stack([x, near, opposite, far])
-
-
-def gather_dp(x):
-    along = gather4(x, "dp", 2)
-    return jnp.stack([along, swap(along)], axis=1).reshape((8,) + x.shape)
+def direct4(x, axis, low):
+    return jnp.stack([x] + [trade(x, axis, j * low) for j in (1, 2, 3)])
+
+
+def exchange_round(x, b):
+    rest = x.shape[1:]
+    parts = x.reshape((8 >> (b + 1), 2, 1 << b) + rest)
+    got = trade(parts[:, 1], "dp", 1 << b)
+    return jnp.stack([parts[:, 0], got], axis=1).reshape((8,) + rest)
 
 
 def exchange_dp(x):
-    rest = x.shape[1:]
     for b in (2, 1, 0):
-        parts = x.reshape((8 >> (b + 1), 2, 1 << b) + rest)
-        got = trade(parts[:, 1], "dp", 1 << b)
-        x = jnp.stack([parts[:, 0], got], axis=1).reshape((8,) + rest)
+        x = exchange_round(x, b)
     return x
 
 
@@ -322,35 +324,30 @@
     seat = seq.astype(jnp.int32).reshape(1)
 
     heads = jnp.arange(SLOTS, dtype=jnp.int32)
-    live = head_live > 0
-    place = jnp.sum(jnp.where(heads[None, :] < heads[:, None], head_live[None, :], 0), axis=1)
-    ranks = jnp.where(live, place, -1).astype(jnp.int32)
-    slots = jnp.sum(
-        jnp.where(ranks[None, :] == jnp.arange(LIVE, dtype=jnp.int32)[:, None], heads[None, :], 0),
-        axis=1).astype(jnp.int32)
-
+    before = jnp.sum(jnp.where(heads[None, :] < heads[:, None], head_live[None, :], 0), axis=1)
+    ranks = jnp.where(head_live > 0, before, -1).astype(jnp.int32)
+
+    slots_scratch = pltpu.SMEM((SLOTS,), jnp.int32)
     give = pl.pallas_call(
         give_kernel, out_shape=shape(8, 3, HALF + TT, HD), in_specs=[SMEM, SMEM, ANY, ANY],
-        out_specs=VMEM, scratch_shapes=[pltpu.SemaphoreType.DMA((2,))], name="give",
+        out_specs=VMEM, scratch_shapes=[slots_scratch, pltpu.SemaphoreType.DMA((2,))], name="give",
         cost_estimate=pl.CostEstimate(flops=0, bytes_accessed=2 << 20, transcendentals=0),
-    )(slots, core, video, text)
+    )(head_live, core, video, text)
     got = swap(give)
     valid_other = swap(text_valid)
     buf = pl.pallas_call(
         pack_kernel, out_shape=shape(SEQ, 3, ROWS, HD), in_specs=[SMEM, SMEM, ANY, ANY],
-        out_specs=VMEM, scratch_shapes=[pltpu.SemaphoreType.DMA((4,))], name="pack",
+        out_specs=VMEM, scratch_shapes=[slots_scratch, pltpu.SemaphoreType.DMA((4,))], name="pack",
         cost_estimate=pl.CostEstimate(flops=0, bytes_accessed=7 << 20, transcendentals=0),
-    )(slots, core, video, text)
+    )(head_live, core, video, text)
     buf = pl.pallas_call(
         fill_kernel, out_shape=shape(SEQ, 3, ROWS, HD), in_specs=[SMEM, VMEM, ANY],
-        out_specs=ANY, scratch_shapes=[pltpu.SemaphoreType.DMA((1,))], name="fill",
+        out_specs=ANY, scratch_shapes=[pltpu.SemaphoreType.DMA], name="fill",
         input_output_aliases={2: 0},
     )(core, got, buf)
-    buf, weight, cot = lax.optimization_barrier((buf, text_weight, text_cotangent[0]))
-    weight_x = gather4(weight, "seq", 1).reshape(4 * 256, 384)
-    cot = by_xor(cot.reshape(TT, 8, 384).transpose(1, 0, 2), dp)
-    cot = gather4(exchange_dp(cot).reshape(8 * TT, 384), "seq", 4)
-    cot_y = cot.reshape(4, 8, TT, 384).transpose(1, 0, 2, 3).reshape(8 * 4 * TT, 384)
+    cot = by_xor(text_cotangent[0].reshape(TT, 8, 384).transpose(1, 0, 2), dp)
+    cot = exchange_dp(cot).reshape(8 * TT, 384)
+    buf, valid_other, cot = lax.optimization_barrier((buf, valid_other, cot))
     recv = lax.all_to_all(buf, "seq", split_axis=0, concat_axis=0, tiled=True)
     other = swap(recv[:, 1:3, VT + TT:VT + TT + HALF, :])
 
@@ -358,29 +355,32 @@
     bias_far = jnp.where(valid_other > 0, 0.0, -1e30).astype(F32)
     bias_c = jnp.where(seq % 2 == core_bit, bias_a, bias_far)
 
-    text_out = attention_call(
-        text_kernel, "text_attention", 2 * TXT, TXT, 2, shape(SEQ, 2 * TT, HD), [VMEM] * 4 + [ANY] * 2,
-    )(bias_a, bias_c, recv, other, weight_x, cot_y)
+    text_out, token = attention_call(
+        text_kernel, "text_attention", 2 * TXT, TXT, 2, shape(SEQ, 8 * TT, HD), [VMEM] * 4,
+    )(bias_a, bias_c, recv, other)
+    text_out, weight, cot = lax.optimization_barrier((text_out, text_weight, cot))
+    weight_x = direct4(weight, "seq", 1).reshape(4 * 256, 384)
+    cot = direct4(cot, "seq", 4)
+    cot_y = cot.reshape(4, 8, TT, 384).transpose(1, 0, 2, 3).reshape(8 * 4 * TT, 384)
     text_got = lax.all_to_all(text_out, "seq", split_axis=0, concat_axis=0, tiled=True)
-    out_a = attention_call(
-        a_kernel, "video_attention_a", VID, 2 * VT, 1, shape(SEQ, VT, HD), [VMEM] * 2,
-    )(bias_a, recv)
-    out_all = attention_call(
-        c_kernel, "video_attention_c", VID // 2, 4 * HALF, 1, shape(SEQ, VT + HALF, HD), [VMEM] * 4,
-    )(bias_c, recv, other, out_a)
-    back = lax.all_to_all(out_all, "seq", split_axis=0, concat_axis=0, tiled=True)
-    halves = back.reshape(8, 2, VT + HALF, HD)[:, :, VT:, :]
-    halves = swap(lax.dynamic_index_in_dim(halves, 1 - core_bit, 1, keepdims=False))
-    video_attended = pl.pallas_call(
-        slot_video_kernel, out_shape=shape(VT, SLOTS * HD), in_specs=[SMEM, SMEM, VMEM, VMEM],
-        out_specs=VMEM, name="slot_video")(ranks, core, back, halves)
-
-    text_slots = pl.pallas_call(
-        slot_text_kernel, out_shape=shape(4, TT, 8 * HD),
-        in_specs=[SMEM, SMEM, SMEM, VMEM, ANY], out_specs=VMEM, name="slot_text",
-    )(ranks, core, seat, text_got, out_all)
-    rows = [text_slots[0]] + [trade(text_slots[j], "seq", 4 * j) for j in (1, 2, 3)]
-    rows_all = gather_dp(jnp.concatenate(rows)).reshape(8 * 4 * TT, 8 * HD)
+
+    out_a, token = attention_call(
+        a_kernel, "video_attention_a", VID, 2 * VT, 1, shape(SEQ, VT, HD), [VMEM] * 3,
+    )(bias_a, recv, token)
+    text_rows, token = pl.pallas_call(
+        slot_text_kernel, out_shape=[shape(4 * TT, 8 * HD), shape(8, HD, dtype=F32)],
+        in_specs=[SMEM, SMEM, SMEM, VMEM, VMEM, ANY, ANY], out_specs=[VMEM, VMEM],
+        name="slot_text",
+    )(ranks, core, seat, text_got, token, weight_x, cot_y)
+    out_c, _ = attention_call(
+        c_kernel, "video_attention_c", VID // 2, 4 * HALF, 1, shape(SEQ, VT + HALF, HD),
+        [VMEM] * 5,
+    )(bias_c, recv, other, out_a, token)
+    rows_near = direct4(text_rows, "dp", 2)
+    out_c, rows_near = lax.optimization_barrier((out_c, rows_near))
+    back = lax.all_to_all(out_c, "seq", split_axis=0, concat_axis=0, tiled=True)
+    rows_far = swap(rows_near)
+    rows_all = jnp.stack([rows_near, rows_far], axis=1).reshape(8 * 4 * TT, 8 * HD)
     sums = pl.pallas_call(
         project_kernel,
         out_shape=[shape(8, TT, 384, dtype=F32)] + [shape(8, TT, 384)] * 3
@@ -394,7 +394,15 @@
     gradient = sums[4]
     for j in (1, 2, 3):
         gradient = gradient + trade(sums[4 + j], "seq", j).astype(F32)
-    projected = by_xor(exchange_dp(projected.astype(BF16)), dp)
+    projected, back = lax.optimization_barrier((projected.astype(BF16), back))
+    halves = swap(lax.dynamic_index_in_dim(
+        back.reshape(8, 2, VT + HALF, HD)[:, :, VT:], 1 - core_bit, 1, keepdims=False))
+    video_attended = pl.pallas_call(
+        slot_video_kernel, out_shape=shape(VT, SLOTS * HD), in_specs=[SMEM, SMEM] + [VMEM] * 2,
+        out_specs=VMEM, scratch_shapes=[slots_scratch], name="slot_video",
+    )(head_live, core, back, halves)
+
+    projected = by_xor(exchange_dp(projected), dp)
     text_output = projected.transpose(1, 0, 2).reshape(TT, 8 * 384)
     return (video_attended[None], text_output[None], gradient)
 

time: 200 us -> 179 us (0.90)
  blocking collectives: 0 us -> 54.2 us
  waiting for transfers between devices: 67 us -> 17.1 us
  starting transfers between devices: 75.6 us -> 47.9 us
  local copies, waits for them, and re-layouts: 5.18 us -> 13.7 us
  Pallas kernels: 46.9 us -> 41.1 us
    all_to_all x0 -> x1, blocking collectives: none -> 54.2 us  [on_device(): recv = lax.all_to_all(buf, 'seq', split_axis=0, concat_axis=0, tiled=True)]
    ppermute x32 -> x26, waiting for transfers between devices: 67 us -> 17.1 us  [trade(): return lax.ppermute(x, axis, [(i, i ^ mask) for i in range(count)])]
    ppermute x32 -> x26, starting transfers between devices: 59.2 us -> 39.5 us  [trade(): return lax.ppermute(x, axis, [(i, i ^ mask) for i in range(count)])]
    unnamed x16 -> x33, local copies, waits for them, and re-layouts: 2.2 us -> 12.7 us
    all_to_all x2 -> x1, starting transfers between devices: 11.9 us -> 4.5 us  [on_device(): back = lax.all_to_all(out_c, 'seq', split_axis=0, concat_axis=0, tiled=True)]
    pallas_call x1, Pallas kernels: 15.1 us -> 12.9 us  [on_device(): attention_call(a_kernel, 'video_attention_a', VID, 2 * VT, 1, shape(SEQ,...]
    pallas_call x1, Pallas kernels: 9.97 us -> 7.88 us  [on_device(): attention_call(c_kernel, 'video_attention_c', VID // 2, 4 * HALF, 1, shap...]
  transfers between devices with their start and end apart: 35 -> 28, of which waited for: 16 -> 10; matrix products, arithmetic and copies ran while one was open for 2% -> 2% of each run, Pallas kernels for 15% -> 18%
where the time goes in v2:
time: 179 us
  blocking collectives  54.2 us (30%)
  starting transfers between devices  47.9 us (27%)
  Pallas kernels  41.1 us (23%)
  waiting for transfers between devices  17.1 us (10%)
  local copies, waits for them, and re-layouts  13.7 us (8%)
  other arithmetic  3.72 us (2%)
    all_to_all x1, blocking collectives, on_device(): recv = lax.all_to_all(buf, 'seq', split_axis=0, concat_axis=0, tiled=True)  54.2 us
    ppermute x26, starting transfers between devices, trade(): return lax.ppermute(x, axis, [(i, i ^ mask) for i in range(count)])  39.5 us
    ppermute x26, waiting for transfers between devices, trade(): return lax.ppermute(x, axis, [(i, i ^ mask) for i in range(count)])  17.1 us
    pallas_call x1, Pallas kernels, on_device(): attention_call(a_kernel, 'video_attention_a', VID, 2 * VT, 1, shape(SEQ,...  12.9 us
    unnamed x33, local copies, waits for them, and re-layouts  12.7 us
    pallas_call x1, Pallas kernels, on_device(): attention_call(c_kernel, 'video_attention_c', VID // 2, 4 * HALF, 1, shap...  7.88 us
    pallas_call x1, Pallas kernels, on_device(): pl.pallas_call(pack_kernel, out_shape=shape(SEQ, 3, ROWS, HD), in_specs=[...  5.18 us
    all_to_all x1, starting transfers between devices, on_device(): back = lax.all_to_all(out_c, 'seq', split_axis=0, concat_axis=0, tiled=True)  4.5 us
  transfers between devices with their start and end apart: 28, of which 10 were waited for; matrix products, arithmetic and copies ran while one was open for 2% of the time, Pallas kernels for 18%

profile of v2, /device:TPU:1, one launch (start us, length us, event | category | flops | bytes accessed | tf_op | source)
XLA Modules:
  0.0 178.7 jit_solution(4890891156785580066)
XLA Ops:
  0.6 0.9 copy.39
  1.7 4.5 %collective-permute-start.2 = (bf16[1,4,16,384]{3,2,1,0:T(8,128)(2,1)S(1)}, bf16[1,4,16,384]{3,2,1,0:T(8,128)(2,1)S(1)}, u32[]{:S(2)}, u32[]{:S(2)}) collective-permute-start(bf16[1,4,16,384]{3,2,1,0:T(8,128)(2,1)S(1)} %get-tuple-element.64), channel_id=1, source_target_pairs={{0,64},{16,80},{32,96},{48,112},{64,0},{80,16},{96,32},{112,48},{1... | collective-permute-start | bytes 147464 | tf_op jit(solution)/shard_map/ppermute | solution.py:284
  6.2 3.2 %give.1 = bf16[8,3,112,128]{3,2,1,0:T(8,128)(2,1)} custom-call(s32[32]{0:T(128)} %live.5, s32[1]{0:T(128)} %bitcast.core, bf16[3,192,4096]{2,1,0:T(8,128)(2,1)} %bitcast.84, bf16[3,16,4096]{2,1,0:T(8,128)(2,1)} %bitcast.88), custom_call_target="tpu_custom_call" | custom-call | bytes 2097152 | tf_op jit(solution)/shard_map/give/pallas_call | solution.py:331
  9.4 1.0 collective-permute-start
  10.5 0.8 collective-permute-start.3
  11.3 2.6 %collective-permute-done.3 = bf16[2,2,16,384]{3,2,1,0:T(8,128)(2,1)S(1)} collective-permute-done((bf16[2,2,16,384]{3,2,1,0:T(8,128)(2,1)S(1)}, bf16[2,2,16,384]{3,2,1,0:T(8,128)(2,1)S(1)}, u32[]{:S(2)}, u32[]{:S(2)}) %collective-permute-start.3) | collective-permute-done | bytes 49184 | tf_op jit(solution)/shard_map/ppermute | solution.py:284
  14.0 0.9 collective-permute-start.4
  15.0 5.2 %pack.1._ = bf16[16,3,320,128]{3,2,1,0:T(8,128)(2,1)} custom-call(s32[32]{0:T(128)} %live.5, s32[1]{0:T(128)} %bitcast.core, bf16[3,192,4096]{2,1,0:T(8,128)(2,1)} %bitcast.85, bf16[3,16,4096]{2,1,0:T(8,128)(2,1)} %bitcast.89), custom_call_target="tpu_custom_call" | custom-call | bytes 7340032 | tf_op jit(solution)/shard_map/pack/pallas_call | solution.py:338
  20.2 0.8 copy-done.10
  21.0 2.0 %fill.1 = bf16[16,3,320,128]{3,2,1,0:T(8,128)(2,1)} custom-call(s32[1]{0:T(128)} %bitcast.core, bf16[8,3,112,128]{3,2,1,0:T(8,128)(2,1)} %copy-done.10, bf16[16,3,320,128]{3,2,1,0:T(8,128)(2,1)} %pack.1._), custom_call_target="tpu_custom_call", output_to_operand_aliasing={{}: (2, {})} | custom-call | tf_op jit(solution)/shard_map/fill/pallas_call | solution.py:343
  23.0 54.2 %all_to_all.15.recv = bf16[16,3,320,128]{3,2,1,0:T(8,128)(2,1)S(1)} all-to-all(bf16[16,3,320,128]{3,2,1,0:T(8,128)(2,1)} %fill.1), channel_id=1, replica_groups=mesh['dp'=8,'seq'=16] {'seq'}, dimensions={0} | all-to-all | bytes 7864320 | tf_op jit(solution)/shard_map/all_to_all | solution.py:351
  77.3 1.9 %copy-done = bf16[16,3,320,128]{3,2,1,0:T(8,128)(2,1)} copy-done((bf16[16,3,320,128]{3,2,1,0:T(8,128)(2,1)}, bf16[16,3,320,128]{3,2,1,0:T(8,128)(2,1)S(1)}, u32[]{:S(2)}) %copy-start) | copy-done | bytes 3932184
  79.2 1.6 collective-permute-start.5
  80.9 1.8 %collective-permute-done.5.other = bf16[16,2,96,128]{3,2,1,0:T(8,128)(2,1)S(1)} collective-permute-done((bf16[16,2,96,128]{3,2,1,0:T(8,128)(2,1)S(1)}, bf16[16,2,96,128]{3,2,1,0:T(8,128)(2,1)S(1)}, u32[]{:S(2)}, u32[]{:S(2)}) %collective-permute-start.5) | collective-permute-done | bytes 786464 | tf_op jit(solution)/shard_map/ppermute | solution.py:284
  82.7 2.1 %copy-done.1 = bf16[16,3,320,128]{3,2,1,0:T(8,128)(2,1)S(1)} copy-done((bf16[16,3,320,128]{3,2,1,0:T(8,128)(2,1)S(1)}, bf16[16,3,320,128]{3,2,1,0:T(8,128)(2,1)}, u32[]{:S(2)}) %copy-start.1) | copy-done | bytes 3932184
  84.8 3.5 %text_attention.1 = (bf16[16,128,128]{2,1,0:T(8,128)(2,1)}, f32[8,128]{1,0:T(8,128)S(1)}) custom-call(f32[1,256]{1,0:T(1,128)S(1)} %get-tuple-element.65.bias_a, f32[1,256]{1,0:T(1,128)S(1)} %get-tuple-element.66.bias_c, bf16[16,3,320,128]{3,2,1,0:T(8,128)(2,1)S(1)} %copy-done.1, bf16[16,2,96,128]{3,2,1,0:T(8,128)(2,1)S(1)} %collective-permute-done.5.other), custom_call_target="tpu_custom_call" | custom-call | flops 872415232 | bytes 8388608 | tf_op jit(solution)/shard_map/text_attention/pallas_call | solution.py:358
  88.8 1.8 collective-permute-start.10
  90.6 2.1 %collective-permute-start.11 = (bf16[128,384]{1,0:T(8,128)(2,1)S(1)}, bf16[128,384]{1,0:T(8,128)(2,1)S(1)}, u32[]{:S(2)}, u32[]{:S(2)}) collective-permute-start(bf16[128,384]{1,0:T(8,128)(2,1)S(1)} %bitcast.94), channel_id=1, source_target_pairs={{0,12},{1,13},{2,14},{3,15},{4,8},{5,9},{6,10},{7,11},{8,4},{9,5},... | collective-permute-start | bytes 294920 | tf_op jit(solution)/shard_map/ppermute | solution.py:284
  93.0 1.3 collective-permute-start.7
  94.3 3.9 %all-to-all-start.1 = ((bf16[16,128,128]{2,1,0:T(8,128)(2,1)}), bf16[16,128,128]{2,1,0:T(8,128)(2,1)S(1)}, u32[]{:S(2)}, u32[]{:S(2)}) async-start(bf16[16,128,128]{2,1,0:T(8,128)(2,1)} %get-tuple-element.34), calls=%async_computation.1 | async-start | bytes 1048576 | tf_op jit(solution)/shard_map/all_to_all | solution.py:365
  98.2 2.8 %collective-permute-start.8 = (bf16[256,384]{1,0:T(8,128)(2,1)S(1)}, bf16[256,384]{1,0:T(8,128)(2,1)S(1)}, u32[]{:S(2)}, u32[]{:S(2)}) collective-permute-start(bf16[256,384]{1,0:T(8,128)(2,1)S(1)} %copy-done.11), channel_id=1, source_target_pairs={{0,3},{1,2},{2,1},{3,0},{4,7},{5,6},{6,5},{7,4},{8,11},{9,10},{10,... | collective-permute-start | bytes 589832 | tf_op jit(solution)/shard_map/ppermute | solution.py:284
  101.1 2.1 %copy-done.2 = bf16[16,3,320,128]{3,2,1,0:T(8,128)(2,1)S(1)} copy-done((bf16[16,3,320,128]{3,2,1,0:T(8,128)(2,1)S(1)}, bf16[16,3,320,128]{3,2,1,0:T(8,128)(2,1)}, u32[]{:S(2)}) %copy-start.2) | copy-done | bytes 3932184
  103.2 12.9 %video_attention_a.1 = (bf16[16,192,128]{2,1,0:T(8,128)(2,1)S(1)}, f32[8,128]{1,0:T(8,128)S(1)}) custom-call(f32[1,256]{1,0:T(1,128)S(1)} %get-tuple-element.65.bias_a, bf16[16,3,320,128]{3,2,1,0:T(8,128)(2,1)S(1)} %copy-done.2, f32[8,128]{1,0:T(8,128)S(1)} %get-tuple-element.30._), custom_call_target="tpu_custom_call" | custom-call | flops 5234491392 | bytes 8388608 | tf_op jit(solution)/shard_map/video_attention_a/pallas_call | solution.py:367
  116.7 0.8 pad_maximum_fusion.3
  117.5 1.0 pad_maximum_fusion.1
  119.4 1.8 %slot_text.1 = (bf16[64,1024]{1,0:T(8,128)(2,1)}, f32[8,128]{1,0:T(8,128)}) custom-call(s32[32]{0:T(128)} %compare_select_fusion.2.ranks, s32[1]{0:T(128)} %bitcast.core, s32[1]{0:T(128)} %bitcast.21.seat, bf16[16,128,128]{2,1,0:T(8,128)(2,1)} %copy-done.9, f32[8,128]{1,0:T(8,128)} %copy-done.6, bf16[1024,384]{1,0:T(8,128)(2,1)} %bitcast.79, ...), custom_call_target="tpu_custom_call" | custom-call | tf_op jit(solution)/shard_map/slot_text/pallas_call | solution.py:370
  122.0 2.5 %collective-permute-start.13 = (bf16[64,1024]{1,0:T(8,128)(2,1)}, bf16[64,1024]{1,0:T(8,128)(2,1)S(1)}, u32[]{:S(2)}, u32[]{:S(2)}) collective-permute-start(bf16[64,1024]{1,0:T(8,128)(2,1)} %get-tuple-element.40), channel_id=1, source_target_pairs={{0,64},{16,80},{32,96},{48,112},{64,0},{80,16},{96,32},{112,48},{1... | collective-permute-start | bytes 393224 | tf_op jit(solution)/shard_map/ppermute | solution.py:284
  125.1 2.1 %copy-done.3 = bf16[16,3,320,128]{3,2,1,0:T(8,128)(2,1)S(1)} copy-done((bf16[16,3,320,128]{3,2,1,0:T(8,128)(2,1)S(1)}, bf16[16,3,320,128]{3,2,1,0:T(8,128)(2,1)}, u32[]{:S(2)}) %copy-start.3) | copy-done | bytes 3932184
  127.9 7.9 %video_attention_c.1 = (bf16[16,288,128]{2,1,0:T(8,128)(2,1)}, f32[8,128]{1,0:T(8,128)}) custom-call(f32[1,256]{1,0:T(1,128)S(1)} %get-tuple-element.66.bias_c, bf16[16,3,320,128]{3,2,1,0:T(8,128)(2,1)S(1)} %copy-done.3, bf16[16,2,96,128]{3,2,1,0:T(8,128)(2,1)S(1)} %collective-permute-done.5.other, bf16[16,192,128]{2,1,0:T(8,128)(2,1)S(1)} %get-tuple-element.31.out_a, ...), custom_call_target="tpu_custom_call" | custom-call | flops 2617245696 | bytes 8388608 | tf_op jit(solution)/shard_map/video_attention_c/pallas_call | solution.py:375
  135.9 4.5 %all-to-all-start.2 = ((bf16[16,288,128]{2,1,0:T(8,128)(2,1)}), bf16[16,288,128]{2,1,0:T(8,128)(2,1)S(1)}, u32[]{:S(2)}, u32[]{:S(2)}) async-start(bf16[16,288,128]{2,1,0:T(8,128)(2,1)} %get-tuple-element.46), calls=%async_computation.2 | async-start | bytes 2359296 | tf_op jit(solution)/shard_map/all_to_all | solution.py:381
  140.4 3.8 %collective-permute-start.15 = (bf16[4,64,1024]{2,1,0:T(8,128)(2,1)S(1)}, bf16[4,64,1024]{2,1,0:T(8,128)(2,1)S(1)}, u32[]{:S(2)}, u32[]{:S(2)}) collective-permute-start(bf16[4,64,1024]{2,1,0:T(8,128)(2,1)S(1)} %pad_maximum_fusion.2), channel_id=1, source_target_pairs={{0,16},{16,0},{32,48},{48,32},{64,80},{80,64},{96,112},{112,96},{1... | collective-permute-start | bytes 1572872 | tf_op jit(solution)/shard_map/ppermute | solution.py:284
  144.2 1.5 collective-permute-done.15
  146.0 1.3 project.1
  147.2 1.6 collective-permute-start.16
  148.9 2.4 %collective-permute-start.17 = (bf16[8,16,384]{2,1,0:T(8,128)(2,1)S(1)}, bf16[8,16,384]{2,1,0:T(8,128)(2,1)S(1)}, u32[]{:S(2)}, u32[]{:S(2)}) collective-permute-start(bf16[8,16,384]{2,1,0:T(8,128)(2,1)S(1)} %get-tuple-element.44), channel_id=1, source_target_pairs={{0,8},{1,9},{2,10},{3,11},{4,12},{5,13},{6,14},{7,15},{8,0},{9,1},... | collective-permute-start | bytes 294920 | tf_op jit(solution)/shard_map/ppermute | solution.py:284
  151.4 1.4 collective-permute-start.23
  152.7 2.4 %collective-permute-start.24 = (bf16[256,384]{1,0:T(8,128)(2,1)S(1)}, bf16[256,384]{1,0:T(8,128)(2,1)S(1)}, u32[]{:S(2)}, u32[]{:S(2)}) collective-permute-start(bf16[256,384]{1,0:T(8,128)(2,1)S(1)} %get-tuple-element.51), channel_id=1, source_target_pairs={{0,2},{1,3},{2,0},{3,1},{4,6},{5,7},{6,4},{7,5},{8,10},{9,11},{10,... | collective-permute-start | bytes 589832 | tf_op jit(solution)/shard_map/ppermute | solution.py:284
  155.1 2.3 %collective-permute-done.16 = bf16[8,16,384]{2,1,0:T(8,128)(2,1)S(1)} collective-permute-done((bf16[8,16,384]{2,1,0:T(8,128)(2,1)S(1)}, bf16[8,16,384]{2,1,0:T(8,128)(2,1)S(1)}, u32[]{:S(2)}, u32[]{:S(2)}) %collective-permute-start.16) | collective-permute-done | bytes 98336 | tf_op jit(solution)/shard_map/ppermute | solution.py:284
  157.4 2.4 %collective-permute-start.25 = (bf16[256,384]{1,0:T(8,128)(2,1)S(1)}, bf16[256,384]{1,0:T(8,128)(2,1)S(1)}, u32[]{:S(2)}, u32[]{:S(2)}) collective-permute-start(bf16[256,384]{1,0:T(8,128)(2,1)S(1)} %get-tuple-element.52), channel_id=1, source_target_pairs={{0,3},{1,2},{2,1},{3,0},{4,7},{5,6},{6,5},{7,4},{8,11},{9,10},{10,... | collective-permute-start | bytes 589832 | tf_op jit(solution)/shard_map/ppermute | solution.py:284
  159.8 0.8 collective-permute-done.17
  160.6 1.6 collective-permute-done.18
  162.3 0.8 collective-permute-start.20
  163.1 3.7 %collective-permute-done.20 = bf16[1,4,16,384]{3,2,1,0:T(8,128)(2,1)S(1)} collective-permute-done((bf16[1,4,16,384]{3,2,1,0:T(8,128)(2,1)S(1)}, bf16[1,4,16,384]{3,2,1,0:T(8,128)(2,1)S(1)}, u32[]{:S(2)}, u32[]{:S(2)}) %collective-permute-start.20) | collective-permute-done | bytes 49184 | tf_op jit(solution)/shard_map/ppermute | solution.py:284
  167.0 0.9 collective-permute-done.25
  167.9 0.8 convert_add_fusion
  168.8 1.0 collective-permute-done.21
  169.9 3.1 %collective-permute-start.22 = (bf16[4,1,16,384]{3,2,0,1:T(8,128)(2,1)S(1)}, bf16[4,1,16,384]{3,2,0,1:T(8,128)(2,1)S(1)}, u32[]{:S(2)}, u32[]{:S(2)}) collective-permute-start(bf16[4,1,16,384]{3,2,0,1:T(8,128)(2,1)S(1)} %get-tuple-element.54), channel_id=1, source_target_pairs={{0,16},{16,0},{32,48},{48,32},{64,80},{80,64},{96,112},{112,96},{1... | collective-permute-start | bytes 147464 | tf_op jit(solution)/shard_map/ppermute | solution.py:284
  175.4 3.3 %slot_video.1 = bf16[192,4096]{1,0:T(8,128)(2,1)} custom-call(s32[32]{0:T(128)} %live.5, s32[1]{0:T(128)} %bitcast.core, bf16[16,288,128]{2,1,0:T(8,128)(2,1)} %copy-done.8, bf16[8,96,128]{2,1,0:T(8,128)(2,1)} %copy-done.12), custom_call_target="tpu_custom_call" | custom-call | tf_op jit(solution)/shard_map/slot_video/pallas_call | solution.py:400
  (84 shorter events, 7.7 us)
Async XLA Ops:
  0.6 14.2 %copy-start.15 = (s32[1,256]{1,0:T(1,128)S(1)}, s32[1,256]{1,0:T(1,128)}, u32[]{:S(2)}) copy-start(s32[1,256]{1,0:T(1,128)} %param.9) | copy-start | bytes 3076
  1.7 8.8 %collective-permute-start.2 = (bf16[1,4,16,384]{3,2,1,0:T(8,128)(2,1)S(1)}, bf16[1,4,16,384]{3,2,1,0:T(8,128)(2,1)S(1)}, u32[]{:S(2)}, u32[]{:S(2)}) collective-permute-start(bf16[1,4,16,384]{3,2,1,0:T(8,128)(2,1)S(1)} %get-tuple-element.64), channel_id=1, source_target_pairs={{0,64},{16,80},{32,96},{48,112},{64,0},{80,16},{96,32},{112,48},{1... | collective-permute-start | bytes 147464 | tf_op jit(solution)/shard_map/ppermute | solution.py:284
  9.4 10.8 %collective-permute-start = (bf16[8,3,112,128]{3,2,1,0:T(8,128)(2,1)}, bf16[8,3,112,128]{3,2,1,0:T(8,128)(2,1)S(1)}, u32[]{:S(2)}, u32[]{:S(2)}) collective-permute-start(bf16[8,3,112,128]{3,2,1,0:T(8,128)(2,1)} %give.1), channel_id=1, source_target_pairs={{0,16},{16,0},{32,48},{48,32},{64,80},{80,64},{96,112},{112,96},{1... | collective-permute-start | bytes 2064392 | tf_op jit(solution)/shard_map/ppermute | solution.py:284
  10.5 3.4 %collective-permute-start.3 = (bf16[2,2,16,384]{3,2,1,0:T(8,128)(2,1)S(1)}, bf16[2,2,16,384]{3,2,1,0:T(8,128)(2,1)S(1)}, u32[]{:S(2)}, u32[]{:S(2)}) collective-permute-start(bf16[2,2,16,384]{3,2,1,0:T(8,128)(2,1)S(1)} %get-tuple-element.62), channel_id=1, source_target_pairs={{0,32},{16,48},{32,0},{48,16},{64,96},{80,112},{96,64},{112,80},{1... | collective-permute-start | bytes 147464 | tf_op jit(solution)/shard_map/ppermute | solution.py:284
  14.0 6.2 %collective-permute-start.4 = (bf16[4,1,16,384]{3,2,0,1:T(8,128)(2,1)S(1)}, bf16[4,1,16,384]{3,2,0,1:T(8,128)(2,1)S(1)}, u32[]{:S(2)}, u32[]{:S(2)}) collective-permute-start(bf16[4,1,16,384]{3,2,0,1:T(8,128)(2,1)S(1)} %get-tuple-element.60), channel_id=1, source_target_pairs={{0,16},{16,0},{32,48},{48,32},{64,80},{80,64},{96,112},{112,96},{1... | collective-permute-start | bytes 147464 | tf_op jit(solution)/shard_map/ppermute | solution.py:284
  14.9 8.2 %collective-permute-start.1 = (s32[1,256]{1,0:T(1,128)S(1)}, s32[1,256]{1,0:T(1,128)S(1)}, u32[]{:S(2)}, u32[]{:S(2)}) collective-permute-start(s32[1,256]{1,0:T(1,128)S(1)} %copy-done.15), channel_id=1, source_target_pairs={{0,16},{16,0},{32,48},{48,32},{64,80},{80,64},{96,112},{112,96},{1... | collective-permute-start | bytes 3080 | tf_op jit(solution)/shard_map/ppermute | solution.py:284
  20.2 0.8 copy-start.10
  23.0 57.7 %copy-start.14 = (s32[32]{0:T(128)S(1)}, s32[32]{0:T(128)}, u32[]{:S(2)}) copy-start(s32[32]{0:T(128)} %live.5) | copy-start | bytes 388
  77.2 15.5 %copy-start.11 = (bf16[256,384]{1,0:T(8,128)(2,1)S(1)}, bf16[256,384]{1,0:T(8,128)(2,1)}, u32[]{:S(2)}) copy-start(bf16[256,384]{1,0:T(8,128)(2,1)} %param.10) | copy-start | bytes 589828
  77.3 1.9 %copy-start = (bf16[16,3,320,128]{3,2,1,0:T(8,128)(2,1)}, bf16[16,3,320,128]{3,2,1,0:T(8,128)(2,1)S(1)}, u32[]{:S(2)}) copy-start(bf16[16,3,320,128]{3,2,1,0:T(8,128)(2,1)S(1)} %all_to_all.15.recv) | copy-start | bytes 11796484
  79.2 3.5 %collective-permute-start.5 = (bf16[16,2,96,128]{3,2,1,0:T(8,128)(2,1)S(1)}, bf16[16,2,96,128]{3,2,1,0:T(8,128)(2,1)S(1)}, u32[]{:S(2)}, u32[]{:S(2)}) collective-permute-start(bf16[16,2,96,128]{3,2,1,0:T(8,128)(2,1)S(1)} %slice.62), channel_id=1, source_target_pairs={{0,16},{16,0},{32,48},{48,32},{64,80},{80,64},{96,112},{112,96},{1... | collective-permute-start | bytes 2359304 | tf_op jit(solution)/shard_map/ppermute | solution.py:284
  82.7 2.1 %copy-start.1 = (bf16[16,3,320,128]{3,2,1,0:T(8,128)(2,1)S(1)}, bf16[16,3,320,128]{3,2,1,0:T(8,128)(2,1)}, u32[]{:S(2)}) copy-start(bf16[16,3,320,128]{3,2,1,0:T(8,128)(2,1)} %copy-done) | copy-start | bytes 11796484
  88.3 9.9 %collective-permute-start.9 = (bf16[128,384]{1,0:T(8,128)(2,1)S(1)}, bf16[128,384]{1,0:T(8,128)(2,1)S(1)}, u32[]{:S(2)}, u32[]{:S(2)}) collective-permute-start(bf16[128,384]{1,0:T(8,128)(2,1)S(1)} %bitcast.92), channel_id=1, source_target_pairs={{0,4},{1,5},{2,6},{3,7},{4,0},{5,1},{6,2},{7,3},{8,12},{9,13},{10,... | collective-permute-start | bytes 294920 | tf_op jit(solution)/shard_map/ppermute | solution.py:284
  88.8 27.9 %collective-permute-start.10 = (bf16[128,384]{1,0:T(8,128)(2,1)S(1)}, bf16[128,384]{1,0:T(8,128)(2,1)S(1)}, u32[]{:S(2)}, u32[]{:S(2)}) collective-permute-start(bf16[128,384]{1,0:T(8,128)(2,1)S(1)} %bitcast.93), channel_id=1, source_target_pairs={{0,8},{1,9},{2,10},{3,11},{4,12},{5,13},{6,14},{7,15},{8,0},{9,1},... | collective-permute-start | bytes 294920 | tf_op jit(solution)/shard_map/ppermute | solution.py:284
  90.6 26.2 %collective-permute-start.11 = (bf16[128,384]{1,0:T(8,128)(2,1)S(1)}, bf16[128,384]{1,0:T(8,128)(2,1)S(1)}, u32[]{:S(2)}, u32[]{:S(2)}) collective-permute-start(bf16[128,384]{1,0:T(8,128)(2,1)S(1)} %bitcast.94), channel_id=1, source_target_pairs={{0,12},{1,13},{2,14},{3,15},{4,8},{5,9},{6,10},{7,11},{8,4},{9,5},... | collective-permute-start | bytes 294920 | tf_op jit(solution)/shard_map/ppermute | solution.py:284
  92.7 24.9 %collective-permute-start.6 = (bf16[256,384]{1,0:T(8,128)(2,1)S(1)}, bf16[256,384]{1,0:T(8,128)(2,1)S(1)}, u32[]{:S(2)}, u32[]{:S(2)}) collective-permute-start(bf16[256,384]{1,0:T(8,128)(2,1)S(1)} %copy-done.11), channel_id=1, source_target_pairs={{0,1},{1,0},{2,3},{3,2},{4,5},{5,4},{6,7},{7,6},{8,9},{9,8},{10,11... | collective-permute-start | bytes 589832 | tf_op jit(solution)/shard_map/ppermute | solution.py:284
  93.0 24.6 %collective-permute-start.7 = (bf16[256,384]{1,0:T(8,128)(2,1)S(1)}, bf16[256,384]{1,0:T(8,128)(2,1)S(1)}, u32[]{:S(2)}, u32[]{:S(2)}) collective-permute-start(bf16[256,384]{1,0:T(8,128)(2,1)S(1)} %copy-done.11), channel_id=1, source_target_pairs={{0,2},{1,3},{2,0},{3,1},{4,6},{5,7},{6,4},{7,5},{8,10},{9,11},{10,... | collective-permute-start | bytes 589832 | tf_op jit(solution)/shard_map/ppermute | solution.py:284
  94.3 24.3 %all-to-all-start.1 = ((bf16[16,128,128]{2,1,0:T(8,128)(2,1)}), bf16[16,128,128]{2,1,0:T(8,128)(2,1)S(1)}, u32[]{:S(2)}, u32[]{:S(2)}) async-start(bf16[16,128,128]{2,1,0:T(8,128)(2,1)} %get-tuple-element.34), calls=%async_computation.1 | async-start | bytes 1048576 | tf_op jit(solution)/shard_map/all_to_all | solution.py:365
  98.2 19.3 %collective-permute-start.8 = (bf16[256,384]{1,0:T(8,128)(2,1)S(1)}, bf16[256,384]{1,0:T(8,128)(2,1)S(1)}, u32[]{:S(2)}, u32[]{:S(2)}) collective-permute-start(bf16[256,384]{1,0:T(8,128)(2,1)S(1)} %copy-done.11), channel_id=1, source_target_pairs={{0,3},{1,2},{2,1},{3,0},{4,7},{5,6},{6,5},{7,4},{8,11},{9,10},{10,... | collective-permute-start | bytes 589832 | tf_op jit(solution)/shard_map/ppermute | solution.py:284
  101.1 2.1 %copy-start.2 = (bf16[16,3,320,128]{3,2,1,0:T(8,128)(2,1)S(1)}, bf16[16,3,320,128]{3,2,1,0:T(8,128)(2,1)}, u32[]{:S(2)}) copy-start(bf16[16,3,320,128]{3,2,1,0:T(8,128)(2,1)} %copy-done) | copy-start | bytes 11796484
  116.1 0.6 copy-start.6
  118.6 0.8 copy-start.9
  121.2 14.5 %collective-permute-start.12 = (bf16[64,1024]{1,0:T(8,128)(2,1)}, bf16[64,1024]{1,0:T(8,128)(2,1)S(1)}, u32[]{:S(2)}, u32[]{:S(2)}) collective-permute-start(bf16[64,1024]{1,0:T(8,128)(2,1)} %get-tuple-element.40), channel_id=1, source_target_pairs={{0,32},{16,48},{32,0},{48,16},{64,96},{80,112},{96,64},{112,80},{1... | collective-permute-start | bytes 393224 | tf_op jit(solution)/shard_map/ppermute | solution.py:284
  122.0 13.8 %collective-permute-start.13 = (bf16[64,1024]{1,0:T(8,128)(2,1)}, bf16[64,1024]{1,0:T(8,128)(2,1)S(1)}, u32[]{:S(2)}, u32[]{:S(2)}) collective-permute-start(bf16[64,1024]{1,0:T(8,128)(2,1)} %get-tuple-element.40), channel_id=1, source_target_pairs={{0,64},{16,80},{32,96},{48,112},{64,0},{80,16},{96,32},{112,48},{1... | collective-permute-start | bytes 393224 | tf_op jit(solution)/shard_map/ppermute | solution.py:284
  124.5 11.3 %collective-permute-start.14 = (bf16[64,1024]{1,0:T(8,128)(2,1)}, bf16[64,1024]{1,0:T(8,128)(2,1)S(1)}, u32[]{:S(2)}, u32[]{:S(2)}) collective-permute-start(bf16[64,1024]{1,0:T(8,128)(2,1)} %get-tuple-element.40), channel_id=1, source_target_pairs={{0,96},{16,112},{32,64},{48,80},{64,32},{80,48},{96,0},{112,16},{1... | collective-permute-start | bytes 393224 | tf_op jit(solution)/shard_map/ppermute | solution.py:284
  125.1 2.1 %copy-start.3 = (bf16[16,3,320,128]{3,2,1,0:T(8,128)(2,1)S(1)}, bf16[16,3,320,128]{3,2,1,0:T(8,128)(2,1)}, u32[]{:S(2)}) copy-start(bf16[16,3,320,128]{3,2,1,0:T(8,128)(2,1)} %copy-done) | copy-start | bytes 11796484
  127.2 0.7 copy-start.7
  127.9 7.9 %copy-start.13 = (bf16[64,1024]{1,0:T(8,128)(2,1)S(1)}, bf16[64,1024]{1,0:T(8,128)(2,1)}, u32[]{:S(2)}) copy-start(bf16[64,1024]{1,0:T(8,128)(2,1)} %get-tuple-element.40) | copy-start | bytes 393220
  135.7 10.2 %copy-start.4 = (bf16[4,256,384]{2,1,0:T(8,128)(2,1)S(1)}, bf16[4,256,384]{2,1,0:T(8,128)(2,1)}, u32[]{:S(2)}) copy-start(bf16[4,256,384]{2,1,0:T(8,128)(2,1)} %pad_maximum_fusion.1) | copy-start | bytes 2359300
  135.8 10.2 %copy-start.5 = (bf16[4,8,16,384]{3,2,0,1:T(8,128)(2,1)S(1)}, bf16[4,8,16,384]{3,2,0,1:T(8,128)(2,1)}, u32[]{:S(2)}) copy-start(bf16[4,8,16,384]{3,2,0,1:T(8,128)(2,1)} %pad_maximum_fusion.3) | copy-start | bytes 1179652
  135.9 26.4 %all-to-all-start.2 = ((bf16[16,288,128]{2,1,0:T(8,128)(2,1)}), bf16[16,288,128]{2,1,0:T(8,128)(2,1)S(1)}, u32[]{:S(2)}, u32[]{:S(2)}) async-start(bf16[16,288,128]{2,1,0:T(8,128)(2,1)} %get-tuple-element.46), calls=%async_computation.2 | async-start | bytes 2359296 | tf_op jit(solution)/shard_map/all_to_all | solution.py:381
  140.4 5.4 %collective-permute-start.15 = (bf16[4,64,1024]{2,1,0:T(8,128)(2,1)S(1)}, bf16[4,64,1024]{2,1,0:T(8,128)(2,1)S(1)}, u32[]{:S(2)}, u32[]{:S(2)}) collective-permute-start(bf16[4,64,1024]{2,1,0:T(8,128)(2,1)S(1)} %pad_maximum_fusion.2), channel_id=1, source_target_pairs={{0,16},{16,0},{32,48},{48,32},{64,80},{80,64},{96,112},{112,96},{1... | collective-permute-start | bytes 1572872 | tf_op jit(solution)/shard_map/ppermute | solution.py:284
  147.2 10.2 %collective-permute-start.16 = (bf16[8,16,384]{2,1,0:T(8,128)(2,1)S(1)}, bf16[8,16,384]{2,1,0:T(8,128)(2,1)S(1)}, u32[]{:S(2)}, u32[]{:S(2)}) collective-permute-start(bf16[8,16,384]{2,1,0:T(8,128)(2,1)S(1)} %get-tuple-element.43), channel_id=1, source_target_pairs={{0,4},{1,5},{2,6},{3,7},{4,0},{5,1},{6,2},{7,3},{8,12},{9,13},{10,... | collective-permute-start | bytes 294920 | tf_op jit(solution)/shard_map/ppermute | solution.py:284
  148.9 11.7 %collective-permute-start.17 = (bf16[8,16,384]{2,1,0:T(8,128)(2,1)S(1)}, bf16[8,16,384]{2,1,0:T(8,128)(2,1)S(1)}, u32[]{:S(2)}, u32[]{:S(2)}) collective-permute-start(bf16[8,16,384]{2,1,0:T(8,128)(2,1)S(1)} %get-tuple-element.44), channel_id=1, source_target_pairs={{0,8},{1,9},{2,10},{3,11},{4,12},{5,13},{6,14},{7,15},{8,0},{9,1},... | collective-permute-start | bytes 294920 | tf_op jit(solution)/shard_map/ppermute | solution.py:284
  151.3 10.9 %collective-permute-start.18 = (bf16[8,16,384]{2,1,0:T(8,128)(2,1)S(1)}, bf16[8,16,384]{2,1,0:T(8,128)(2,1)S(1)}, u32[]{:S(2)}, u32[]{:S(2)}) collective-permute-start(bf16[8,16,384]{2,1,0:T(8,128)(2,1)S(1)} %get-tuple-element.45), channel_id=1, source_target_pairs={{0,12},{1,13},{2,14},{3,15},{4,8},{5,9},{6,10},{7,11},{8,4},{9,5},... | collective-permute-start | bytes 294920 | tf_op jit(solution)/shard_map/ppermute | solution.py:284
  151.4 15.6 %collective-permute-start.23 = (bf16[256,384]{1,0:T(8,128)(2,1)S(1)}, bf16[256,384]{1,0:T(8,128)(2,1)S(1)}, u32[]{:S(2)}, u32[]{:S(2)}) collective-permute-start(bf16[256,384]{1,0:T(8,128)(2,1)S(1)} %get-tuple-element.50), channel_id=1, source_target_pairs={{0,1},{1,0},{2,3},{3,2},{4,5},{5,4},{6,7},{7,6},{8,9},{9,8},{10,11... | collective-permute-start | bytes 589832 | tf_op jit(solution)/shard_map/ppermute | solution.py:284
  152.7 14.2 %collective-permute-start.24 = (bf16[256,384]{1,0:T(8,128)(2,1)S(1)}, bf16[256,384]{1,0:T(8,128)(2,1)S(1)}, u32[]{:S(2)}, u32[]{:S(2)}) collective-permute-start(bf16[256,384]{1,0:T(8,128)(2,1)S(1)} %get-tuple-element.51), channel_id=1, source_target_pairs={{0,2},{1,3},{2,0},{3,1},{4,6},{5,7},{6,4},{7,5},{8,10},{9,11},{10,... | collective-permute-start | bytes 589832 | tf_op jit(solution)/shard_map/ppermute | solution.py:284
  157.4 10.5 %collective-permute-start.25 = (bf16[256,384]{1,0:T(8,128)(2,1)S(1)}, bf16[256,384]{1,0:T(8,128)(2,1)S(1)}, u32[]{:S(2)}, u32[]{:S(2)}) collective-permute-start(bf16[256,384]{1,0:T(8,128)(2,1)S(1)} %get-tuple-element.52), channel_id=1, source_target_pairs={{0,3},{1,2},{2,1},{3,0},{4,7},{5,6},{6,5},{7,4},{8,11},{9,10},{10,... | collective-permute-start | bytes 589832 | tf_op jit(solution)/shard_map/ppermute | solution.py:284
  162.2 12.5 %copy-start.8 = (bf16[16,288,128]{2,1,0:T(8,128)(2,1)}, bf16[16,288,128]{2,1,0:T(8,128)(2,1)S(1)}, u32[]{:S(2)}) copy-start(bf16[16,288,128]{2,1,0:T(8,128)(2,1)S(1)} %all-to-all-done.2.got) | copy-start | bytes 3538948
  162.3 4.5 %collective-permute-start.20 = (bf16[1,4,16,384]{3,2,1,0:T(8,128)(2,1)S(1)}, bf16[1,4,16,384]{3,2,1,0:T(8,128)(2,1)S(1)}, u32[]{:S(2)}, u32[]{:S(2)}) collective-permute-start(bf16[1,4,16,384]{3,2,1,0:T(8,128)(2,1)S(1)} %get-tuple-element.58), channel_id=1, source_target_pairs={{0,64},{16,80},{32,96},{48,112},{64,0},{80,16},{96,32},{112,48},{1... | collective-permute-start | bytes 147464 | tf_op jit(solution)/shard_map/ppermute | solution.py:284
  166.8 3.0 %collective-permute-start.21 = (bf16[2,2,16,384]{3,2,1,0:T(8,128)(2,1)S(1)}, bf16[2,2,16,384]{3,2,1,0:T(8,128)(2,1)S(1)}, u32[]{:S(2)}, u32[]{:S(2)}) collective-permute-start(bf16[2,2,16,384]{3,2,1,0:T(8,128)(2,1)S(1)} %get-tuple-element.56), channel_id=1, source_target_pairs={{0,32},{16,48},{32,0},{48,16},{64,96},{80,112},{96,64},{112,80},{1... | collective-permute-start | bytes 147464 | tf_op jit(solution)/shard_map/ppermute | solution.py:284
  169.9 4.0 %collective-permute-start.22 = (bf16[4,1,16,384]{3,2,0,1:T(8,128)(2,1)S(1)}, bf16[4,1,16,384]{3,2,0,1:T(8,128)(2,1)S(1)}, u32[]{:S(2)}, u32[]{:S(2)}) collective-permute-start(bf16[4,1,16,384]{3,2,0,1:T(8,128)(2,1)S(1)} %get-tuple-element.54), channel_id=1, source_target_pairs={{0,16},{16,0},{32,48},{48,32},{64,80},{80,64},{96,112},{112,96},{1... | collective-permute-start | bytes 147464 | tf_op jit(solution)/shard_map/ppermute | solution.py:284
  173.0 1.7 collective-permute-start.19
  174.7 0.7 copy-start.12

commit v3 on v2

--- a/solution.py
+++ b/solution.py
@@ -222,8 +222,19 @@
     video_blocks(4, 4 * HALF, load, store, keys, values, bias_c[...], scores, tops)
 
 
-def slot_text_kernel(ranks, core, seat, got, _t, _w, _c, out, token):
+def list_ranks(live, ranks):
+    def body(h, count):
+        alive = live[h] > 0
+        ranks[h] = jnp.where(alive, count, -1)
+        return count + jnp.where(alive, 1, 0)
+
+    lax.fori_loop(0, SLOTS, body, jnp.int32(0))
+
+
+def slot_text_kernel(live, core, seat, got, *rest):
+    out, token, ranks = rest[-3:]
     token[...] = jnp.zeros_like(token)
+    list_ranks(live, ranks)
     y, x = seat[0] // 4, seat[0] % 4
     for k in range(8):
         rank = ranks[8 * y + k]
@@ -235,8 +246,19 @@
             out[j * TT:(j + 1) * TT, cols] = jnp.where(rank >= 0, block, jnp.zeros_like(block))
 
 
-def project_kernel(rows, weight, cot, p0, p1, p2, p3, g0, g1, g2, g3):
-    part = jnp.dot(rows[...], weight[...], preferred_element_type=F32).reshape(8, 4, TT, 384)
+def project_kernel(near, far, w0, w1, w2, w3, c0, c1, c2, c3, p0, p1, p2, p3, g0, g1, g2, g3, rows, cot):
+    for z in range(4):
+        rows[z * 128:z * 128 + 64, :] = near[z]
+        rows[z * 128 + 64:(z + 1) * 128, :] = far[z]
+    for w in range(8):
+        for j, ref in enumerate((c0, c1, c2, c3)):
+            at = (w * 4 + j) * TT
+            cot[at:at + TT, :] = ref[w * TT:(w + 1) * TT, :]
+    part = None
+    for j, ref in enumerate((w0, w1, w2, w3)):
+        term = jnp.dot(rows[:, j * 256:(j + 1) * 256], ref[...], preferred_element_type=F32)
+        part = term if part is None else part + term
+    part = part.reshape(8, 4, TT, 384)
     for j, ref in enumerate((p0, p1, p2, p3)):
         ref[...] = part[:, j].astype(ref.dtype)
     for j, ref in enumerate((g0, g1, g2, g3)):
@@ -298,7 +320,7 @@
 
 
 def direct4(x, axis, low):
-    return jnp.stack([x] + [trade(x, axis, j * low) for j in (1, 2, 3)])
+    return [x] + [trade(x, axis, j * low) for j in (1, 2, 3)]
 
 
 def exchange_round(x, b):
@@ -306,12 +328,6 @@
     parts = x.reshape((8 >> (b + 1), 2, 1 << b) + rest)
     got = trade(parts[:, 1], "dp", 1 << b)
     return jnp.stack([parts[:, 0], got], axis=1).reshape((8,) + rest)
-
-
-def exchange_dp(x):
-    for b in (2, 1, 0):
-        x = exchange_round(x, b)
-    return x
 
 
 def on_device(video_projected, text_projected, head_live, text_valid, text_weight, text_cotangent):
@@ -322,10 +338,6 @@
     core_bit = dp % 2
     core = core_bit.astype(jnp.int32).reshape(1)
     seat = seq.astype(jnp.int32).reshape(1)
-
-    heads = jnp.arange(SLOTS, dtype=jnp.int32)
-    before = jnp.sum(jnp.where(heads[None, :] < heads[:, None], head_live[None, :], 0), axis=1)
-    ranks = jnp.where(head_live > 0, before, -1).astype(jnp.int32)
 
     slots_scratch = pltpu.SMEM((SLOTS,), jnp.int32)
     give = pl.pallas_call(
@@ -340,13 +352,15 @@
         out_specs=VMEM, scratch_shapes=[slots_scratch, pltpu.SemaphoreType.DMA((4,))], name="pack",
         cost_estimate=pl.CostEstimate(flops=0, bytes_accessed=7 << 20, transcendentals=0),
     )(head_live, core, video, text)
+    cot = by_xor(text_cotangent[0].reshape(TT, 8, 384).transpose(1, 0, 2), dp)
+    cot = exchange_round(exchange_round(cot, 2), 1)
+    buf, cot = lax.optimization_barrier((buf, cot))
+    cot = exchange_round(cot, 0).reshape(8 * TT, 384)
     buf = pl.pallas_call(
         fill_kernel, out_shape=shape(SEQ, 3, ROWS, HD), in_specs=[SMEM, VMEM, ANY],
         out_specs=ANY, scratch_shapes=[pltpu.SemaphoreType.DMA], name="fill",
         input_output_aliases={2: 0},
     )(core, got, buf)
-    cot = by_xor(text_cotangent[0].reshape(TT, 8, 384).transpose(1, 0, 2), dp)
-    cot = exchange_dp(cot).reshape(8 * TT, 384)
     buf, valid_other, cot = lax.optimization_barrier((buf, valid_other, cot))
     recv = lax.all_to_all(buf, "seq", split_axis=0, concat_axis=0, tiled=True)
     other = swap(recv[:, 1:3, VT + TT:VT + TT + HALF, :])
@@ -359,9 +373,8 @@
         text_kernel, "text_attention", 2 * TXT, TXT, 2, shape(SEQ, 8 * TT, HD), [VMEM] * 4,
     )(bias_a, bias_c, recv, other)
     text_out, weight, cot = lax.optimization_barrier((text_out, text_weight, cot))
-    weight_x = direct4(weight, "seq", 1).reshape(4 * 256, 384)
-    cot = direct4(cot, "seq", 4)
-    cot_y = cot.reshape(4, 8, TT, 384).transpose(1, 0, 2, 3).reshape(8 * 4 * TT, 384)
+    weight_x = direct4(weight, "seq", 1)
+    cot_y = direct4(cot, "seq", 4)
     text_got = lax.all_to_all(text_out, "seq", split_axis=0, concat_axis=0, tiled=True)
 
     out_a, token = attention_call(
@@ -369,25 +382,26 @@
     )(bias_a, recv, token)
     text_rows, token = pl.pallas_call(
         slot_text_kernel, out_shape=[shape(4 * TT, 8 * HD), shape(8, HD, dtype=F32)],
-        in_specs=[SMEM, SMEM, SMEM, VMEM, VMEM, ANY, ANY], out_specs=[VMEM, VMEM],
+        in_specs=[SMEM, SMEM, SMEM, VMEM, VMEM] + [ANY] * 6, out_specs=[VMEM, VMEM],
+        scratch_shapes=[slots_scratch],
         name="slot_text",
-    )(ranks, core, seat, text_got, token, weight_x, cot_y)
+    )(head_live, core, seat, text_got, token, *weight_x[1:], *cot_y[1:])
     out_c, _ = attention_call(
         c_kernel, "video_attention_c", VID // 2, 4 * HALF, 1, shape(SEQ, VT + HALF, HD),
         [VMEM] * 5,
     )(bias_c, recv, other, out_a, token)
-    rows_near = direct4(text_rows, "dp", 2)
+    rows_near = jnp.stack(direct4(text_rows, "dp", 2))
     out_c, rows_near = lax.optimization_barrier((out_c, rows_near))
     back = lax.all_to_all(out_c, "seq", split_axis=0, concat_axis=0, tiled=True)
     rows_far = swap(rows_near)
-    rows_all = jnp.stack([rows_near, rows_far], axis=1).reshape(8 * 4 * TT, 8 * HD)
     sums = pl.pallas_call(
         project_kernel,
         out_shape=[shape(8, TT, 384, dtype=F32)] + [shape(8, TT, 384)] * 3
         + [shape(256, 384, dtype=F32)] + [shape(256, 384)] * 3,
-        in_specs=[VMEM] * 3, out_specs=[VMEM] * 8, name="project",
+        in_specs=[VMEM] * 10, out_specs=[VMEM] * 8, name="project",
+        scratch_shapes=[pltpu.VMEM((512, 8 * HD), BF16), pltpu.VMEM((512, 384), BF16)],
         compiler_params=pltpu.CompilerParams(vmem_limit_bytes=20 << 20),
-    )(rows_all, weight_x, cot_y)
+    )(rows_near, rows_far, *weight_x, *cot_y)
     projected = sums[0]
     for j in (1, 2, 3):
         projected = projected + trade(sums[j], "seq", 4 * j).astype(F32)
@@ -402,7 +416,8 @@
         out_specs=VMEM, scratch_shapes=[slots_scratch], name="slot_video",
     )(head_live, core, back, halves)
 
-    projected = by_xor(exchange_dp(projected), dp)
+    projected = exchange_round(projected, 2)
+    projected = by_xor(exchange_round(exchange_round(projected, 1), 0), dp)
     text_output = projected.transpose(1, 0, 2).reshape(TT, 8 * 384)
     return (video_attended[None], text_output[None], gradient)
 

time: 179 us -> 175 us (0.978)
  waiting for transfers between devices: 17.1 us -> 14.1 us
  other arithmetic: 3.72 us -> 1.17 us
    ppermute x26, waiting for transfers between devices: 17.1 us -> 14.1 us  [trade(): return lax.ppermute(x, axis, [(i, i ^ mask) for i in range(count)])]
    another operation x4 -> x1, other arithmetic: 2 us -> 0.07 us  [on_device(): rows_near = jnp.stack(direct4(text_rows, 'dp', 2))]
    unnamed x33 -> x50, local copies, waits for them, and re-layouts: 12.7 us -> 12.9 us
  transfers between devices with their start and end apart: 28 -> 28, of which waited for: 10 -> 10; matrix products, arithmetic and copies ran while one was open for 2% -> 2% of each run, Pallas kernels for 18% -> 19%
where the time goes in v3:
time: 175 us; the launch traced here: 174 us
  blocking collectives  54.4 us (31%)
  starting transfers between devices  47 us (27%)
  Pallas kernels  41.4 us (24%)
  local copies, waits for them, and re-layouts  14.8 us (8%)
  waiting for transfers between devices  14.1 us (8%)
    all_to_all x1, blocking collectives, on_device(): recv = lax.all_to_all(buf, 'seq', split_axis=0, concat_axis=0, tiled=True)  54.4 us
    ppermute x26, starting transfers between devices, trade(): return lax.ppermute(x, axis, [(i, i ^ mask) for i in range(count)])  37.9 us
    ppermute x26, waiting for transfers between devices, trade(): return lax.ppermute(x, axis, [(i, i ^ mask) for i in range(count)])  14.1 us
    pallas_call x1, Pallas kernels, on_device(): attention_call(a_kernel, 'video_attention_a', VID, 2 * VT, 1, shape(SEQ,...  12.9 us
    unnamed x50, local copies, waits for them, and re-layouts  12.9 us
    pallas_call x1, Pallas kernels, on_device(): attention_call(c_kernel, 'video_attention_c', VID // 2, 4 * HALF, 1, shap...  7.88 us
    pallas_call x1, Pallas kernels, on_device(): pl.pallas_call(pack_kernel, out_shape=shape(SEQ, 3, ROWS, HD), in_specs=[...  5.17 us
    all_to_all x1, starting transfers between devices, on_device(): back = lax.all_to_all(out_c, 'seq', split_axis=0, concat_axis=0, tiled=True)  4.97 us
  transfers between devices with their start and end apart: 28, of which 10 were waited for; matrix products, arithmetic and copies ran while one was open for 2% of the time, Pallas kernels for 19%

profile of v3, /device:TPU:1, one launch (start us, length us, event | category | flops | bytes accessed | tf_op | source)
XLA Modules:
  0.0 174.0 jit_solution(17807003995777400307)
XLA Ops:
  0.6 0.9 copy.26
  1.7 4.5 %collective-permute-start.1 = (bf16[1,4,16,384]{3,2,1,0:T(8,128)(2,1)S(1)}, bf16[1,4,16,384]{3,2,1,0:T(8,128)(2,1)S(1)}, u32[]{:S(2)}, u32[]{:S(2)}) collective-permute-start(bf16[1,4,16,384]{3,2,1,0:T(8,128)(2,1)S(1)} %get-tuple-element.68), channel_id=1, source_target_pairs={{0,64},{16,80},{32,96},{48,112},{64,0},{80,16},{96,32},{112,48},{1... | collective-permute-start | bytes 147464 | tf_op jit(solution)/shard_map/ppermute | solution.py:306
  6.2 3.2 %give.1 = bf16[8,3,112,128]{3,2,1,0:T(8,128)(2,1)} custom-call(s32[32]{0:T(128)} %live.7, s32[1]{0:T(128)} %bitcast.core, bf16[3,192,4096]{2,1,0:T(8,128)(2,1)} %bitcast.69, bf16[3,16,4096]{2,1,0:T(8,128)(2,1)} %bitcast.71), custom_call_target="tpu_custom_call" | custom-call | bytes 2097152 | tf_op jit(solution)/shard_map/give/pallas_call | solution.py:343
  9.4 1.0 collective-permute-start
  10.5 0.8 collective-permute-start.2
  11.3 5.2 %pack.1._ = bf16[16,3,320,128]{3,2,1,0:T(8,128)(2,1)} custom-call(s32[32]{0:T(128)} %live.7, s32[1]{0:T(128)} %bitcast.core, bf16[3,192,4096]{2,1,0:T(8,128)(2,1)} %bitcast.70, bf16[3,16,4096]{2,1,0:T(8,128)(2,1)} %bitcast.72), custom_call_target="tpu_custom_call" | custom-call | bytes 7340032 | tf_op jit(solution)/shard_map/pack/pallas_call | solution.py:350
  17.1 0.7 collective-permute-done.4
  17.9 0.8 copy-done.20
  18.7 2.0 %fill.1 = bf16[16,3,320,128]{3,2,1,0:T(8,128)(2,1)} custom-call(s32[1]{0:T(128)} %bitcast.core, bf16[8,3,112,128]{3,2,1,0:T(8,128)(2,1)} %copy-done.20, bf16[16,3,320,128]{3,2,1,0:T(8,128)(2,1)} %pack.1._), custom_call_target="tpu_custom_call", output_to_operand_aliasing={{}: (2, {})} | custom-call | tf_op jit(solution)/shard_map/fill/pallas_call | solution.py:359
  20.8 54.4 %all_to_all.15.recv = bf16[16,3,320,128]{3,2,1,0:T(8,128)(2,1)S(1)} all-to-all(bf16[16,3,320,128]{3,2,1,0:T(8,128)(2,1)} %fill.1), channel_id=1, replica_groups=mesh['dp'=8,'seq'=16] {'seq'}, dimensions={0} | all-to-all | bytes 7864320 | tf_op jit(solution)/shard_map/all_to_all | solution.py:365
  75.3 1.9 %copy-done = bf16[16,3,320,128]{3,2,1,0:T(8,128)(2,1)} copy-done((bf16[16,3,320,128]{3,2,1,0:T(8,128)(2,1)}, bf16[16,3,320,128]{3,2,1,0:T(8,128)(2,1)S(1)}, u32[]{:S(2)}) %copy-start) | copy-done | bytes 3932184
  77.2 1.4 collective-permute-start.5
  78.5 1.9 %collective-permute-done.5.other = bf16[16,2,96,128]{3,2,1,0:T(8,128)(2,1)S(1)} collective-permute-done((bf16[16,2,96,128]{3,2,1,0:T(8,128)(2,1)S(1)}, bf16[16,2,96,128]{3,2,1,0:T(8,128)(2,1)S(1)}, u32[]{:S(2)}, u32[]{:S(2)}) %collective-permute-start.5) | collective-permute-done | bytes 786464 | tf_op jit(solution)/shard_map/ppermute | solution.py:306
  80.4 2.1 %copy-done.1 = bf16[16,3,320,128]{3,2,1,0:T(8,128)(2,1)S(1)} copy-done((bf16[16,3,320,128]{3,2,1,0:T(8,128)(2,1)S(1)}, bf16[16,3,320,128]{3,2,1,0:T(8,128)(2,1)}, u32[]{:S(2)}) %copy-start.1) | copy-done | bytes 3932184
  82.5 3.5 %text_attention.1 = (bf16[16,128,128]{2,1,0:T(8,128)(2,1)}, f32[8,128]{1,0:T(8,128)S(1)}) custom-call(f32[1,256]{1,0:T(1,128)S(1)} %get-tuple-element.69.bias_a, f32[1,256]{1,0:T(1,128)S(1)} %get-tuple-element.70.bias_c, bf16[16,3,320,128]{3,2,1,0:T(8,128)(2,1)S(1)} %copy-done.1, bf16[16,2,96,128]{3,2,1,0:T(8,128)(2,1)S(1)} %collective-permute-done.5.other), custom_call_target="tpu_custom_call" | custom-call | flops 872415232 | bytes 8388608 | tf_op jit(solution)/shard_map/text_attention/pallas_call | solution.py:372
  86.6 4.2 %all-to-all-start.1 = ((bf16[16,128,128]{2,1,0:T(8,128)(2,1)}), bf16[16,128,128]{2,1,0:T(8,128)(2,1)S(1)}, u32[]{:S(2)}, u32[]{:S(2)}) async-start(bf16[16,128,128]{2,1,0:T(8,128)(2,1)} %get-tuple-element.38), calls=%async_computation.1 | async-start | bytes 1048576 | tf_op jit(solution)/shard_map/all_to_all | solution.py:378
  90.8 1.4 collective-permute-start.6
  92.2 2.4 %collective-permute-start.7 = (bf16[256,384]{1,0:T(8,128)(2,1)S(1)}, bf16[256,384]{1,0:T(8,128)(2,1)S(1)}, u32[]{:S(2)}, u32[]{:S(2)}) collective-permute-start(bf16[256,384]{1,0:T(8,128)(2,1)S(1)} %copy-done.16), channel_id=1, source_target_pairs={{0,2},{1,3},{2,0},{3,1},{4,6},{5,7},{6,4},{7,5},{8,10},{9,11},{10,... | collective-permute-start | bytes 589832 | tf_op jit(solution)/shard_map/ppermute | solution.py:306
  94.7 2.6 %collective-permute-start.11 = (bf16[128,384]{1,0:T(8,128)(2,1)S(1)}, bf16[128,384]{1,0:T(8,128)(2,1)S(1)}, u32[]{:S(2)}, u32[]{:S(2)}) collective-permute-start(bf16[128,384]{1,0:T(8,128)(2,1)S(1)} %bitcast.66), channel_id=1, source_target_pairs={{0,12},{1,13},{2,14},{3,15},{4,8},{5,9},{6,10},{7,11},{8,4},{9,5},... | collective-permute-start | bytes 294920 | tf_op jit(solution)/shard_map/ppermute | solution.py:306
  97.3 2.1 %copy-done.2 = bf16[16,3,320,128]{3,2,1,0:T(8,128)(2,1)S(1)} copy-done((bf16[16,3,320,128]{3,2,1,0:T(8,128)(2,1)S(1)}, bf16[16,3,320,128]{3,2,1,0:T(8,128)(2,1)}, u32[]{:S(2)}) %copy-start.2) | copy-done | bytes 3932184
  99.5 12.9 %video_attention_a.1 = (bf16[16,192,128]{2,1,0:T(8,128)(2,1)S(1)}, f32[8,128]{1,0:T(8,128)S(1)}) custom-call(f32[1,256]{1,0:T(1,128)S(1)} %get-tuple-element.69.bias_a, bf16[16,3,320,128]{3,2,1,0:T(8,128)(2,1)S(1)} %copy-done.2, f32[8,128]{1,0:T(8,128)S(1)} %get-tuple-element.34._), custom_call_target="tpu_custom_call" | custom-call | flops 5234491392 | bytes 8388608 | tf_op jit(solution)/shard_map/video_attention_a/pallas_call | solution.py:380
  114.1 2.1 %slot_text.1 = (bf16[64,1024]{1,0:T(8,128)(2,1)}, f32[8,128]{1,0:T(8,128)}) custom-call(s32[32]{0:T(128)} %live.7, s32[1]{0:T(128)} %bitcast.core, s32[1]{0:T(128)} %bitcast.22.seat, bf16[16,128,128]{2,1,0:T(8,128)(2,1)} %copy-done.19, f32[8,128]{1,0:T(8,128)} %copy-done.17, bf16[256,384]{1,0:T(8,128)(2,1)} %copy-done.4, bf16[256,384]{1,0:T(8,128)(2,1)} %copy-done.6, ...), custom_call_target="tpu_custom_call" | custom-call | tf_op jit(solution)/shard_map/slot_text/pallas_call | solution.py:383
  116.1 0.7 collective-permute-start.12
  116.8 2.0 %collective-permute-start.13 = (bf16[64,1024]{1,0:T(8,128)(2,1)}, bf16[64,1024]{1,0:T(8,128)(2,1)S(1)}, u32[]{:S(2)}, u32[]{:S(2)}) collective-permute-start(bf16[64,1024]{1,0:T(8,128)(2,1)} %get-tuple-element.44), channel_id=1, source_target_pairs={{0,64},{16,80},{32,96},{48,112},{64,0},{80,16},{96,32},{112,48},{1... | collective-permute-start | bytes 393224 | tf_op jit(solution)/shard_map/ppermute | solution.py:306
  118.8 1.2 collective-permute-start.14
  120.0 2.1 %copy-done.3 = bf16[16,3,320,128]{3,2,1,0:T(8,128)(2,1)S(1)} copy-done((bf16[16,3,320,128]{3,2,1,0:T(8,128)(2,1)S(1)}, bf16[16,3,320,128]{3,2,1,0:T(8,128)(2,1)}, u32[]{:S(2)}) %copy-start.3) | copy-done | bytes 3932184
  122.1 0.7 copy-done.18
  122.8 7.9 %video_attention_c.1 = (bf16[16,288,128]{2,1,0:T(8,128)(2,1)}, f32[8,128]{1,0:T(8,128)}) custom-call(f32[1,256]{1,0:T(1,128)S(1)} %get-tuple-element.70.bias_c, bf16[16,3,320,128]{3,2,1,0:T(8,128)(2,1)S(1)} %copy-done.3, bf16[16,2,96,128]{3,2,1,0:T(8,128)(2,1)S(1)} %collective-permute-done.5.other, bf16[16,192,128]{2,1,0:T(8,128)(2,1)S(1)} %get-tuple-element.35.out_a, ...), custom_call_target="tpu_custom_call" | custom-call | flops 2617245696 | bytes 8388608 | tf_op jit(solution)/shard_map/video_attention_c/pallas_call | solution.py:389
  130.8 5.0 %all-to-all-start.2 = ((bf16[16,288,128]{2,1,0:T(8,128)(2,1)}), bf16[16,288,128]{2,1,0:T(8,128)(2,1)}, u32[]{:S(2)}, u32[]{:S(2)}) async-start(bf16[16,288,128]{2,1,0:T(8,128)(2,1)} %get-tuple-element.50), calls=%async_computation.2 | async-start | bytes 2359296 | tf_op jit(solution)/shard_map/all_to_all | solution.py:395
  135.8 3.8 %collective-permute-start.15 = (bf16[4,64,1024]{2,1,0:T(8,128)(2,1)S(1)}, bf16[4,64,1024]{2,1,0:T(8,128)(2,1)S(1)}, u32[]{:S(2)}, u32[]{:S(2)}) collective-permute-start(bf16[4,64,1024]{2,1,0:T(8,128)(2,1)S(1)} %pad_maximum_fusion.near), channel_id=1, source_target_pairs={{0,16},{16,0},{32,48},{48,32},{64,80},{80,64},{96,112},{112,96},{1... | collective-permute-start | bytes 1572872 | tf_op jit(solution)/shard_map/ppermute | solution.py:306
  139.6 1.5 collective-permute-done.15.far
  141.2 1.3 project.1
  142.4 1.6 collective-permute-start.16
  144.0 2.4 %collective-permute-start.17 = (bf16[8,16,384]{2,1,0:T(8,128)(2,1)S(1)}, bf16[8,16,384]{2,1,0:T(8,128)(2,1)S(1)}, u32[]{:S(2)}, u32[]{:S(2)}) collective-permute-start(bf16[8,16,384]{2,1,0:T(8,128)(2,1)S(1)} %get-tuple-element.48), channel_id=1, source_target_pairs={{0,8},{1,9},{2,10},{3,11},{4,12},{5,13},{6,14},{7,15},{8,0},{9,1},... | collective-permute-start | bytes 294920 | tf_op jit(solution)/shard_map/ppermute | solution.py:306
  146.5 1.4 collective-permute-start.23
  147.9 2.4 %collective-permute-start.24 = (bf16[256,384]{1,0:T(8,128)(2,1)S(1)}, bf16[256,384]{1,0:T(8,128)(2,1)S(1)}, u32[]{:S(2)}, u32[]{:S(2)}) collective-permute-start(bf16[256,384]{1,0:T(8,128)(2,1)S(1)} %get-tuple-element.55), channel_id=1, source_target_pairs={{0,2},{1,3},{2,0},{3,1},{4,6},{5,7},{6,4},{7,5},{8,10},{9,11},{10,... | collective-permute-start | bytes 589832 | tf_op jit(solution)/shard_map/ppermute | solution.py:306
  150.3 2.6 %collective-permute-done.16 = bf16[8,16,384]{2,1,0:T(8,128)(2,1)S(1)} collective-permute-done((bf16[8,16,384]{2,1,0:T(8,128)(2,1)S(1)}, bf16[8,16,384]{2,1,0:T(8,128)(2,1)S(1)}, u32[]{:S(2)}, u32[]{:S(2)}) %collective-permute-start.16) | collective-permute-done | bytes 98336 | tf_op jit(solution)/shard_map/ppermute | solution.py:306
  152.9 2.4 %collective-permute-start.25 = (bf16[256,384]{1,0:T(8,128)(2,1)S(1)}, bf16[256,384]{1,0:T(8,128)(2,1)S(1)}, u32[]{:S(2)}, u32[]{:S(2)}) collective-permute-start(bf16[256,384]{1,0:T(8,128)(2,1)S(1)} %get-tuple-element.56), channel_id=1, source_target_pairs={{0,3},{1,2},{2,1},{3,0},{4,7},{5,6},{6,5},{7,4},{8,11},{9,10},{10,... | collective-permute-start | bytes 589832 | tf_op jit(solution)/shard_map/ppermute | solution.py:306
  155.9 1.7 collective-permute-done.18
  157.7 1.4 collective-permute-start.20
  159.1 3.2 %collective-permute-done.20 = bf16[1,4,16,384]{3,2,1,0:T(8,128)(2,1)S(1)} collective-permute-done((bf16[1,4,16,384]{3,2,1,0:T(8,128)(2,1)S(1)}, bf16[1,4,16,384]{3,2,1,0:T(8,128)(2,1)S(1)}, u32[]{:S(2)}, u32[]{:S(2)}) %collective-permute-start.20) | collective-permute-done | bytes 49184 | tf_op jit(solution)/shard_map/ppermute | solution.py:306
  162.4 0.9 collective-permute-done.25
  163.3 0.8 convert_add_fusion
  164.2 1.0 slice.63
  165.3 3.0 %collective-permute-start.22 = (bf16[4,1,16,384]{3,2,0,1:T(8,128)(2,1)S(1)}, bf16[4,1,16,384]{3,2,0,1:T(8,128)(2,1)S(1)}, u32[]{:S(2)}, u32[]{:S(2)}) collective-permute-start(bf16[4,1,16,384]{3,2,0,1:T(8,128)(2,1)S(1)} %get-tuple-element.58), channel_id=1, source_target_pairs={{0,16},{16,0},{32,48},{48,32},{64,80},{80,64},{96,112},{112,96},{1... | collective-permute-start | bytes 147464 | tf_op jit(solution)/shard_map/ppermute | solution.py:306
  168.5 0.8 collective-permute-done.22
  169.4 0.7 broadcast_in_dim_reshape.3
  170.7 3.3 %slot_video.1 = bf16[192,4096]{1,0:T(8,128)(2,1)} custom-call(s32[32]{0:T(128)} %live.7, s32[1]{0:T(128)} %bitcast.core, bf16[16,288,128]{2,1,0:T(8,128)(2,1)} %all-to-all-done.2.got, bf16[8,96,128]{2,1,0:T(8,128)(2,1)} %copy-done.21), custom_call_target="tpu_custom_call" | custom-call | tf_op jit(solution)/shard_map/slot_video/pallas_call | solution.py:414
  (94 shorter events, 5.1 us)
Async XLA Ops:
  1.7 8.8 %collective-permute-start.1 = (bf16[1,4,16,384]{3,2,1,0:T(8,128)(2,1)S(1)}, bf16[1,4,16,384]{3,2,1,0:T(8,128)(2,1)S(1)}, u32[]{:S(2)}, u32[]{:S(2)}) collective-permute-start(bf16[1,4,16,384]{3,2,1,0:T(8,128)(2,1)S(1)} %get-tuple-element.68), channel_id=1, source_target_pairs={{0,64},{16,80},{32,96},{48,112},{64,0},{80,16},{96,32},{112,48},{1... | collective-permute-start | bytes 147464 | tf_op jit(solution)/shard_map/ppermute | solution.py:306
  9.4 8.5 %collective-permute-start = (bf16[8,3,112,128]{3,2,1,0:T(8,128)(2,1)}, bf16[8,3,112,128]{3,2,1,0:T(8,128)(2,1)S(1)}, u32[]{:S(2)}, u32[]{:S(2)}) collective-permute-start(bf16[8,3,112,128]{3,2,1,0:T(8,128)(2,1)} %give.1), channel_id=1, source_target_pairs={{0,16},{16,0},{32,48},{48,32},{64,80},{80,64},{96,112},{112,96},{1... | collective-permute-start | bytes 2064392 | tf_op jit(solution)/shard_map/ppermute | solution.py:306
  10.5 6.4 %copy-start.23 = (s32[1,256]{1,0:T(1,128)S(1)}, s32[1,256]{1,0:T(1,128)}, u32[]{:S(2)}) copy-start(s32[1,256]{1,0:T(1,128)} %param.9) | copy-start | bytes 3076
  10.5 6.0 %collective-permute-start.2 = (bf16[2,2,16,384]{3,2,1,0:T(8,128)(2,1)S(1)}, bf16[2,2,16,384]{3,2,1,0:T(8,128)(2,1)S(1)}, u32[]{:S(2)}, u32[]{:S(2)}) collective-permute-start(bf16[2,2,16,384]{3,2,1,0:T(8,128)(2,1)S(1)} %get-tuple-element.66), channel_id=1, source_target_pairs={{0,32},{16,48},{32,0},{48,16},{64,96},{80,112},{96,64},{112,80},{1... | collective-permute-start | bytes 147464 | tf_op jit(solution)/shard_map/ppermute | solution.py:306
  16.5 1.3 collective-permute-start.4
  16.9 3.9 %collective-permute-start.3 = (s32[1,256]{1,0:T(1,128)S(1)}, s32[1,256]{1,0:T(1,128)S(1)}, u32[]{:S(2)}, u32[]{:S(2)}) collective-permute-start(s32[1,256]{1,0:T(1,128)S(1)} %copy-done.23), channel_id=1, source_target_pairs={{0,16},{16,0},{32,48},{48,32},{64,80},{80,64},{96,112},{112,96},{1... | collective-permute-start | bytes 3080 | tf_op jit(solution)/shard_map/ppermute | solution.py:306
  17.9 0.8 copy-start.20
  75.2 15.6 %copy-start.16 = (bf16[256,384]{1,0:T(8,128)(2,1)S(1)}, bf16[256,384]{1,0:T(8,128)(2,1)}, u32[]{:S(2)}) copy-start(bf16[256,384]{1,0:T(8,128)(2,1)} %w0) | copy-start | bytes 589828
  75.3 1.9 %copy-start = (bf16[16,3,320,128]{3,2,1,0:T(8,128)(2,1)}, bf16[16,3,320,128]{3,2,1,0:T(8,128)(2,1)S(1)}, u32[]{:S(2)}) copy-start(bf16[16,3,320,128]{3,2,1,0:T(8,128)(2,1)S(1)} %all_to_all.15.recv) | copy-start | bytes 11796484
  77.2 3.3 %collective-permute-start.5 = (bf16[16,2,96,128]{3,2,1,0:T(8,128)(2,1)S(1)}, bf16[16,2,96,128]{3,2,1,0:T(8,128)(2,1)S(1)}, u32[]{:S(2)}, u32[]{:S(2)}) collective-permute-start(bf16[16,2,96,128]{3,2,1,0:T(8,128)(2,1)S(1)} %slice.62), channel_id=1, source_target_pairs={{0,16},{16,0},{32,48},{48,32},{64,80},{80,64},{96,112},{112,96},{1... | collective-permute-start | bytes 2359304 | tf_op jit(solution)/shard_map/ppermute | solution.py:306
  80.4 2.1 %copy-start.1 = (bf16[16,3,320,128]{3,2,1,0:T(8,128)(2,1)S(1)}, bf16[16,3,320,128]{3,2,1,0:T(8,128)(2,1)}, u32[]{:S(2)}) copy-start(bf16[16,3,320,128]{3,2,1,0:T(8,128)(2,1)} %copy-done) | copy-start | bytes 11796484
  86.0 11.3 %collective-permute-start.10 = (bf16[128,384]{1,0:T(8,128)(2,1)S(1)}, bf16[128,384]{1,0:T(8,128)(2,1)S(1)}, u32[]{:S(2)}, u32[]{:S(2)}) collective-permute-start(bf16[128,384]{1,0:T(8,128)(2,1)S(1)} %bitcast.65), channel_id=1, source_target_pairs={{0,8},{1,9},{2,10},{3,11},{4,12},{5,13},{6,14},{7,15},{8,0},{9,1},... | collective-permute-start | bytes 294920 | tf_op jit(solution)/shard_map/ppermute | solution.py:306
  86.6 26.5 %all-to-all-start.1 = ((bf16[16,128,128]{2,1,0:T(8,128)(2,1)}), bf16[16,128,128]{2,1,0:T(8,128)(2,1)S(1)}, u32[]{:S(2)}, u32[]{:S(2)}) async-start(bf16[16,128,128]{2,1,0:T(8,128)(2,1)} %get-tuple-element.38), calls=%async_computation.1 | async-start | bytes 1048576 | tf_op jit(solution)/shard_map/all_to_all | solution.py:378
  90.8 22.3 %collective-permute-start.6 = (bf16[256,384]{1,0:T(8,128)(2,1)S(1)}, bf16[256,384]{1,0:T(8,128)(2,1)S(1)}, u32[]{:S(2)}, u32[]{:S(2)}) collective-permute-start(bf16[256,384]{1,0:T(8,128)(2,1)S(1)} %copy-done.16), channel_id=1, source_target_pairs={{0,1},{1,0},{2,3},{3,2},{4,5},{5,4},{6,7},{7,6},{8,9},{9,8},{10,11... | collective-permute-start | bytes 589832 | tf_op jit(solution)/shard_map/ppermute | solution.py:306
  92.2 20.8 %collective-permute-start.7 = (bf16[256,384]{1,0:T(8,128)(2,1)S(1)}, bf16[256,384]{1,0:T(8,128)(2,1)S(1)}, u32[]{:S(2)}, u32[]{:S(2)}) collective-permute-start(bf16[256,384]{1,0:T(8,128)(2,1)S(1)} %copy-done.16), channel_id=1, source_target_pairs={{0,2},{1,3},{2,0},{3,1},{4,6},{5,7},{6,4},{7,5},{8,10},{9,11},{10,... | collective-permute-start | bytes 589832 | tf_op jit(solution)/shard_map/ppermute | solution.py:306
  94.6 18.5 %collective-permute-start.8 = (bf16[256,384]{1,0:T(8,128)(2,1)S(1)}, bf16[256,384]{1,0:T(8,128)(2,1)S(1)}, u32[]{:S(2)}, u32[]{:S(2)}) collective-permute-start(bf16[256,384]{1,0:T(8,128)(2,1)S(1)} %copy-done.16), channel_id=1, source_target_pairs={{0,3},{1,2},{2,1},{3,0},{4,7},{5,6},{6,5},{7,4},{8,11},{9,10},{10,... | collective-permute-start | bytes 589832 | tf_op jit(solution)/shard_map/ppermute | solution.py:306
  94.7 18.3 %collective-permute-start.11 = (bf16[128,384]{1,0:T(8,128)(2,1)S(1)}, bf16[128,384]{1,0:T(8,128)(2,1)S(1)}, u32[]{:S(2)}, u32[]{:S(2)}) collective-permute-start(bf16[128,384]{1,0:T(8,128)(2,1)S(1)} %bitcast.66), channel_id=1, source_target_pairs={{0,12},{1,13},{2,14},{3,15},{4,8},{5,9},{6,10},{7,11},{8,4},{9,5},... | collective-permute-start | bytes 294920 | tf_op jit(solution)/shard_map/ppermute | solution.py:306
  97.3 15.1 %copy-start.10 = (bf16[128,384]{1,0:T(8,128)(2,1)}, bf16[128,384]{1,0:T(8,128)(2,1)S(1)}, u32[]{:S(2)}) copy-start(bf16[128,384]{1,0:T(8,128)(2,1)S(1)} %collective-permute-done.10.rest_5_.c2) | copy-start | bytes 294916
  97.3 15.7 %collective-permute-start.9 = (bf16[128,384]{1,0:T(8,128)(2,1)S(1)}, bf16[128,384]{1,0:T(8,128)(2,1)S(1)}, u32[]{:S(2)}, u32[]{:S(2)}) collective-permute-start(bf16[128,384]{1,0:T(8,128)(2,1)S(1)} %bitcast.67), channel_id=1, source_target_pairs={{0,4},{1,5},{2,6},{3,7},{4,0},{5,1},{6,2},{7,3},{8,12},{9,13},{10,... | collective-permute-start | bytes 294920 | tf_op jit(solution)/shard_map/ppermute | solution.py:306
  97.3 2.2 %copy-start.2 = (bf16[16,3,320,128]{3,2,1,0:T(8,128)(2,1)S(1)}, bf16[16,3,320,128]{3,2,1,0:T(8,128)(2,1)}, u32[]{:S(2)}) copy-start(bf16[16,3,320,128]{3,2,1,0:T(8,128)(2,1)} %copy-done) | copy-start | bytes 11796484
  113.1 0.7 copy-start.4
  113.1 0.8 copy-start.6
  113.1 0.8 copy-start.8
  113.1 1.0 copy-start.19
  116.1 14.6 %collective-permute-start.12 = (bf16[64,1024]{1,0:T(8,128)(2,1)}, bf16[64,1024]{1,0:T(8,128)(2,1)S(1)}, u32[]{:S(2)}, u32[]{:S(2)}) collective-permute-start(bf16[64,1024]{1,0:T(8,128)(2,1)} %get-tuple-element.44), channel_id=1, source_target_pairs={{0,32},{16,48},{32,0},{48,16},{64,96},{80,112},{96,64},{112,80},{1... | collective-permute-start | bytes 393224 | tf_op jit(solution)/shard_map/ppermute | solution.py:306
  116.8 13.9 %collective-permute-start.13 = (bf16[64,1024]{1,0:T(8,128)(2,1)}, bf16[64,1024]{1,0:T(8,128)(2,1)S(1)}, u32[]{:S(2)}, u32[]{:S(2)}) collective-permute-start(bf16[64,1024]{1,0:T(8,128)(2,1)} %get-tuple-element.44), channel_id=1, source_target_pairs={{0,64},{16,80},{32,96},{48,112},{64,0},{80,16},{96,32},{112,48},{1... | collective-permute-start | bytes 393224 | tf_op jit(solution)/shard_map/ppermute | solution.py:306
  118.8 11.9 %collective-permute-start.14 = (bf16[64,1024]{1,0:T(8,128)(2,1)}, bf16[64,1024]{1,0:T(8,128)(2,1)S(1)}, u32[]{:S(2)}, u32[]{:S(2)}) collective-permute-start(bf16[64,1024]{1,0:T(8,128)(2,1)} %get-tuple-element.44), channel_id=1, source_target_pairs={{0,96},{16,112},{32,64},{48,80},{64,32},{80,48},{96,0},{112,16},{1... | collective-permute-start | bytes 393224 | tf_op jit(solution)/shard_map/ppermute | solution.py:306
  120.0 2.1 %copy-start.3 = (bf16[16,3,320,128]{3,2,1,0:T(8,128)(2,1)S(1)}, bf16[16,3,320,128]{3,2,1,0:T(8,128)(2,1)}, u32[]{:S(2)}) copy-start(bf16[16,3,320,128]{3,2,1,0:T(8,128)(2,1)} %copy-done) | copy-start | bytes 11796484
  122.1 0.7 copy-start.18
  122.8 7.9 %copy-start.22 = (bf16[64,1024]{1,0:T(8,128)(2,1)S(1)}, bf16[64,1024]{1,0:T(8,128)(2,1)}, u32[]{:S(2)}) copy-start(bf16[64,1024]{1,0:T(8,128)(2,1)} %get-tuple-element.44) | copy-start | bytes 393220
  122.8 18.3 %copy-start.5 = (bf16[256,384]{1,0:T(8,128)(2,1)S(1)}, bf16[256,384]{1,0:T(8,128)(2,1)}, u32[]{:S(2)}) copy-start(bf16[256,384]{1,0:T(8,128)(2,1)} %copy-done.4) | copy-start | bytes 589828
  122.8 18.3 %copy-start.7 = (bf16[256,384]{1,0:T(8,128)(2,1)S(1)}, bf16[256,384]{1,0:T(8,128)(2,1)}, u32[]{:S(2)}) copy-start(bf16[256,384]{1,0:T(8,128)(2,1)} %copy-done.6) | copy-start | bytes 589828
  122.8 18.3 %copy-start.9 = (bf16[256,384]{1,0:T(8,128)(2,1)S(1)}, bf16[256,384]{1,0:T(8,128)(2,1)}, u32[]{:S(2)}) copy-start(bf16[256,384]{1,0:T(8,128)(2,1)} %copy-done.8) | copy-start | bytes 589828
  122.8 18.3 %copy-start.11 = (bf16[128,384]{1,0:T(8,128)(2,1)S(1)}, bf16[128,384]{1,0:T(8,128)(2,1)}, u32[]{:S(2)}) copy-start(bf16[128,384]{1,0:T(8,128)(2,1)} %copy-done.10) | copy-start | bytes 294916
  122.8 18.3 %copy-start.13 = (bf16[128,384]{1,0:T(8,128)(2,1)S(1)}, bf16[128,384]{1,0:T(8,128)(2,1)}, u32[]{:S(2)}) copy-start(bf16[128,384]{1,0:T(8,128)(2,1)} %copy-done.12) | copy-start | bytes 294916
  122.8 18.3 %copy-start.15 = (bf16[128,384]{1,0:T(8,128)(2,1)S(1)}, bf16[128,384]{1,0:T(8,128)(2,1)}, u32[]{:S(2)}) copy-start(bf16[128,384]{1,0:T(8,128)(2,1)} %copy-done.14) | copy-start | bytes 294916
  130.8 26.9 %all-to-all-start.2 = ((bf16[16,288,128]{2,1,0:T(8,128)(2,1)}), bf16[16,288,128]{2,1,0:T(8,128)(2,1)}, u32[]{:S(2)}, u32[]{:S(2)}) async-start(bf16[16,288,128]{2,1,0:T(8,128)(2,1)} %get-tuple-element.50), calls=%async_computation.2 | async-start | bytes 2359296 | tf_op jit(solution)/shard_map/all_to_all | solution.py:395
  135.8 5.3 %collective-permute-start.15 = (bf16[4,64,1024]{2,1,0:T(8,128)(2,1)S(1)}, bf16[4,64,1024]{2,1,0:T(8,128)(2,1)S(1)}, u32[]{:S(2)}, u32[]{:S(2)}) collective-permute-start(bf16[4,64,1024]{2,1,0:T(8,128)(2,1)S(1)} %pad_maximum_fusion.near), channel_id=1, source_target_pairs={{0,16},{16,0},{32,48},{48,32},{64,80},{80,64},{96,112},{112,96},{1... | collective-permute-start | bytes 1572872 | tf_op jit(solution)/shard_map/ppermute | solution.py:306
  142.4 10.4 %collective-permute-start.16 = (bf16[8,16,384]{2,1,0:T(8,128)(2,1)S(1)}, bf16[8,16,384]{2,1,0:T(8,128)(2,1)S(1)}, u32[]{:S(2)}, u32[]{:S(2)}) collective-permute-start(bf16[8,16,384]{2,1,0:T(8,128)(2,1)S(1)} %get-tuple-element.47), channel_id=1, source_target_pairs={{0,4},{1,5},{2,6},{3,7},{4,0},{5,1},{6,2},{7,3},{8,12},{9,13},{10,... | collective-permute-start | bytes 294920 | tf_op jit(solution)/shard_map/ppermute | solution.py:306
  144.0 11.9 %collective-permute-start.17 = (bf16[8,16,384]{2,1,0:T(8,128)(2,1)S(1)}, bf16[8,16,384]{2,1,0:T(8,128)(2,1)S(1)}, u32[]{:S(2)}, u32[]{:S(2)}) collective-permute-start(bf16[8,16,384]{2,1,0:T(8,128)(2,1)S(1)} %get-tuple-element.48), channel_id=1, source_target_pairs={{0,8},{1,9},{2,10},{3,11},{4,12},{5,13},{6,14},{7,15},{8,0},{9,1},... | collective-permute-start | bytes 294920 | tf_op jit(solution)/shard_map/ppermute | solution.py:306
  146.4 11.2 %collective-permute-start.18 = (bf16[8,16,384]{2,1,0:T(8,128)(2,1)S(1)}, bf16[8,16,384]{2,1,0:T(8,128)(2,1)S(1)}, u32[]{:S(2)}, u32[]{:S(2)}) collective-permute-start(bf16[8,16,384]{2,1,0:T(8,128)(2,1)S(1)} %get-tuple-element.49), channel_id=1, source_target_pairs={{0,12},{1,13},{2,14},{3,15},{4,8},{5,9},{6,10},{7,11},{8,4},{9,5},... | collective-permute-start | bytes 294920 | tf_op jit(solution)/shard_map/ppermute | solution.py:306
  146.5 15.9 %collective-permute-start.23 = (bf16[256,384]{1,0:T(8,128)(2,1)S(1)}, bf16[256,384]{1,0:T(8,128)(2,1)S(1)}, u32[]{:S(2)}, u32[]{:S(2)}) collective-permute-start(bf16[256,384]{1,0:T(8,128)(2,1)S(1)} %get-tuple-element.54), channel_id=1, source_target_pairs={{0,1},{1,0},{2,3},{3,2},{4,5},{5,4},{6,7},{7,6},{8,9},{9,8},{10,11... | collective-permute-start | bytes 589832 | tf_op jit(solution)/shard_map/ppermute | solution.py:306
  147.9 14.5 %collective-permute-start.24 = (bf16[256,384]{1,0:T(8,128)(2,1)S(1)}, bf16[256,384]{1,0:T(8,128)(2,1)S(1)}, u32[]{:S(2)}, u32[]{:S(2)}) collective-permute-start(bf16[256,384]{1,0:T(8,128)(2,1)S(1)} %get-tuple-element.55), channel_id=1, source_target_pairs={{0,2},{1,3},{2,0},{3,1},{4,6},{5,7},{6,4},{7,5},{8,10},{9,11},{10,... | collective-permute-start | bytes 589832 | tf_op jit(solution)/shard_map/ppermute | solution.py:306
  152.9 10.5 %collective-permute-start.25 = (bf16[256,384]{1,0:T(8,128)(2,1)S(1)}, bf16[256,384]{1,0:T(8,128)(2,1)S(1)}, u32[]{:S(2)}, u32[]{:S(2)}) collective-permute-start(bf16[256,384]{1,0:T(8,128)(2,1)S(1)} %get-tuple-element.56), channel_id=1, source_target_pairs={{0,3},{1,2},{2,1},{3,0},{4,7},{5,6},{6,5},{7,4},{8,11},{9,10},{10,... | collective-permute-start | bytes 589832 | tf_op jit(solution)/shard_map/ppermute | solution.py:306
  157.7 4.5 %collective-permute-start.20 = (bf16[1,4,16,384]{3,2,1,0:T(8,128)(2,1)S(1)}, bf16[1,4,16,384]{3,2,1,0:T(8,128)(2,1)S(1)}, u32[]{:S(2)}, u32[]{:S(2)}) collective-permute-start(bf16[1,4,16,384]{3,2,1,0:T(8,128)(2,1)S(1)} %get-tuple-element.62), channel_id=1, source_target_pairs={{0,64},{16,80},{32,96},{48,112},{64,0},{80,16},{96,32},{112,48},{1... | collective-permute-start | bytes 147464 | tf_op jit(solution)/shard_map/ppermute | solution.py:306
  162.3 3.0 %collective-permute-start.21 = (bf16[2,2,16,384]{3,2,1,0:T(8,128)(2,1)S(1)}, bf16[2,2,16,384]{3,2,1,0:T(8,128)(2,1)S(1)}, u32[]{:S(2)}, u32[]{:S(2)}) collective-permute-start(bf16[2,2,16,384]{3,2,1,0:T(8,128)(2,1)S(1)} %get-tuple-element.60), channel_id=1, source_target_pairs={{0,32},{16,48},{32,0},{48,16},{64,96},{80,112},{96,64},{112,80},{1... | collective-permute-start | bytes 147464 | tf_op jit(solution)/shard_map/ppermute | solution.py:306
  165.3 3.9 %collective-permute-start.22 = (bf16[4,1,16,384]{3,2,0,1:T(8,128)(2,1)S(1)}, bf16[4,1,16,384]{3,2,0,1:T(8,128)(2,1)S(1)}, u32[]{:S(2)}, u32[]{:S(2)}) collective-permute-start(bf16[4,1,16,384]{3,2,0,1:T(8,128)(2,1)S(1)} %get-tuple-element.58), channel_id=1, source_target_pairs={{0,16},{16,0},{32,48},{48,32},{64,80},{80,64},{96,112},{112,96},{1... | collective-permute-start | bytes 147464 | tf_op jit(solution)/shard_map/ppermute | solution.py:306
  168.4 1.7 collective-permute-start.19
  (4 other events, 2.6 us)

commit v4 on v3

--- a/solution.py
+++ b/solution.py
@@ -348,9 +348,10 @@
     got = swap(give)
     valid_other = swap(text_valid)
     buf = pl.pallas_call(
-        pack_kernel, out_shape=shape(SEQ, 3, ROWS, HD), in_specs=[SMEM, SMEM, ANY, ANY],
+        pack_kernel, out_shape=shape(SEQ, 3, ROWS, HD), in_specs=[SMEM, SMEM, VMEM, VMEM],
         out_specs=VMEM, scratch_shapes=[slots_scratch, pltpu.SemaphoreType.DMA((4,))], name="pack",
         cost_estimate=pl.CostEstimate(flops=0, bytes_accessed=7 << 20, transcendentals=0),
+        compiler_params=pltpu.CompilerParams(vmem_limit_bytes=24 << 20),
     )(head_live, core, video, text)
     cot = by_xor(text_cotangent[0].reshape(TT, 8, 384).transpose(1, 0, 2), dp)
     cot = exchange_round(exchange_round(cot, 2), 1)

time: 175 us -> 176 us (level)
  local copies, waits for them, and re-layouts: 14.8 us -> 18.9 us
  Pallas kernels: 41.4 us -> 38.2 us
    unnamed x50 -> x56, local copies, waits for them, and re-layouts: 12.9 us -> 17.1 us
    pallas_call x1, Pallas kernels: 5.17 us -> 2.05 us  [on_device(): pl.pallas_call(pack_kernel, out_shape=shape(SEQ, 3, ROWS, HD), in_specs=[...]
  transfers between devices with their start and end apart: 28 -> 28, of which waited for: 10 -> 10; matrix products, arithmetic and copies ran while one was open for 2% -> 2% of each run, Pallas kernels for 19% -> 17%
where the time goes in v4:
time: 176 us; the launch traced here: 175 us
  blocking collectives  54.3 us (31%)
  starting transfers between devices  47.2 us (27%)
  Pallas kernels  38.2 us (22%)
  local copies, waits for them, and re-layouts  18.9 us (11%)
  waiting for transfers between devices  14 us (8%)
    all_to_all x1, blocking collectives, on_device(): recv = lax.all_to_all(buf, 'seq', split_axis=0, concat_axis=0, tiled=True)  54.3 us
    ppermute x26, starting transfers between devices, trade(): return lax.ppermute(x, axis, [(i, i ^ mask) for i in range(count)])  38 us
    unnamed x56, local copies, waits for them, and re-layouts  17.1 us
    ppermute x26, waiting for transfers between devices, trade(): return lax.ppermute(x, axis, [(i, i ^ mask) for i in range(count)])  13.9 us
    pallas_call x1, Pallas kernels, on_device(): attention_call(a_kernel, 'video_attention_a', VID, 2 * VT, 1, shape(SEQ,...  12.9 us
    pallas_call x1, Pallas kernels, on_device(): attention_call(c_kernel, 'video_attention_c', VID // 2, 4 * HALF, 1, shap...  7.88 us
    all_to_all x1, starting transfers between devices, on_device(): back = lax.all_to_all(out_c, 'seq', split_axis=0, concat_axis=0, tiled=True)  4.97 us
    all_to_all x1, starting transfers between devices, on_device(): lax.all_to_all(text_out, 'seq', split_axis=0, concat_axis=0, tiled=True)  4.24 us
  transfers between devices with their start and end apart: 28, of which 10 were waited for; matrix products, arithmetic and copies ran while one was open for 2% of the time, Pallas kernels for 17%

profile of v4, /device:TPU:1, one launch (start us, length us, event | category | flops | bytes accessed | tf_op | source)
XLA Modules:
  0.0 174.9 jit_solution(8913046318820458468)
XLA Ops:
  0.7 1.0 copy.26
  1.8 4.5 %collective-permute-start.1 = (bf16[1,4,16,384]{3,2,1,0:T(8,128)(2,1)S(1)}, bf16[1,4,16,384]{3,2,1,0:T(8,128)(2,1)S(1)}, u32[]{:S(2)}, u32[]{:S(2)}) collective-permute-start(bf16[1,4,16,384]{3,2,1,0:T(8,128)(2,1)S(1)} %get-tuple-element.68), channel_id=1, source_target_pairs={{0,64},{16,80},{32,96},{48,112},{64,0},{80,16},{96,32},{112,48},{1... | collective-permute-start | bytes 147464 | tf_op jit(solution)/shard_map/ppermute | solution.py:306
  6.3 3.2 %give.1 = bf16[8,3,112,128]{3,2,1,0:T(8,128)(2,1)} custom-call(s32[32]{0:T(128)} %live.7, s32[1]{0:T(128)} %bitcast.core, bf16[3,192,4096]{2,1,0:T(8,128)(2,1)} %bitcast.65, bf16[3,16,4096]{2,1,0:T(8,128)(2,1)} %bitcast.67), custom_call_target="tpu_custom_call" | custom-call | bytes 2097152 | tf_op jit(solution)/shard_map/give/pallas_call | solution.py:343
  9.5 1.0 collective-permute-start
  10.5 0.8 collective-permute-start.2
  11.4 2.3 %copy-done.5 = bf16[1,192,3,4096]{3,1,2,0:T(8,128)(2,1)S(1)} copy-done((bf16[1,192,3,4096]{3,1,2,0:T(8,128)(2,1)S(1)}, bf16[1,192,3,4096]{3,1,2,0:T(8,128)(2,1)}, u32[]{:S(2)}) %copy-start.5) | copy-done | bytes 4718616
  13.7 2.0 %pack.1._ = bf16[16,3,320,128]{3,2,1,0:T(8,128)(2,1)S(1)} custom-call(s32[32]{0:T(128)S(1)} %copy-done.20, s32[1]{0:T(128)} %bitcast.core, bf16[3,192,4096]{2,1,0:T(8,128)(2,1)S(1)} %bitcast.66, bf16[3,16,4096]{2,1,0:T(8,128)(2,1)S(1)} %bitcast.68), custom_call_target="tpu_custom_call" | custom-call | bytes 7340032 | tf_op jit(solution)/shard_map/pack/pallas_call | solution.py:350
  15.8 1.9 %copy-done = bf16[16,3,320,128]{3,2,1,0:T(8,128)(2,1)} copy-done((bf16[16,3,320,128]{3,2,1,0:T(8,128)(2,1)}, bf16[16,3,320,128]{3,2,1,0:T(8,128)(2,1)S(1)}, u32[]{:S(2)}) %copy-start) | copy-done | bytes 3932184
  18.3 0.7 collective-permute-done.4
  19.1 0.8 copy-done.23
  19.9 2.0 %fill.1 = bf16[16,3,320,128]{3,2,1,0:T(8,128)(2,1)} custom-call(s32[1]{0:T(128)} %bitcast.core, bf16[8,3,112,128]{3,2,1,0:T(8,128)(2,1)} %copy-done.23, bf16[16,3,320,128]{3,2,1,0:T(8,128)(2,1)} %copy-done), custom_call_target="tpu_custom_call", output_to_operand_aliasing={{}: (2, {})} | custom-call | tf_op jit(solution)/shard_map/fill/pallas_call | solution.py:360
  21.9 54.3 %all_to_all.15.recv = bf16[16,3,320,128]{3,2,1,0:T(8,128)(2,1)S(1)} all-to-all(bf16[16,3,320,128]{3,2,1,0:T(8,128)(2,1)} %fill.1), channel_id=1, replica_groups=mesh['dp'=8,'seq'=16] {'seq'}, dimensions={0} | all-to-all | bytes 7864320 | tf_op jit(solution)/shard_map/all_to_all | solution.py:366
  76.3 1.9 %copy-done.1 = bf16[16,3,320,128]{3,2,1,0:T(8,128)(2,1)} copy-done((bf16[16,3,320,128]{3,2,1,0:T(8,128)(2,1)}, bf16[16,3,320,128]{3,2,1,0:T(8,128)(2,1)S(1)}, u32[]{:S(2)}) %copy-start.1) | copy-done | bytes 3932184
  78.2 1.4 collective-permute-start.5
  79.6 1.9 %collective-permute-done.5.other = bf16[16,2,96,128]{3,2,1,0:T(8,128)(2,1)S(1)} collective-permute-done((bf16[16,2,96,128]{3,2,1,0:T(8,128)(2,1)S(1)}, bf16[16,2,96,128]{3,2,1,0:T(8,128)(2,1)S(1)}, u32[]{:S(2)}, u32[]{:S(2)}) %collective-permute-start.5) | collective-permute-done | bytes 786464 | tf_op jit(solution)/shard_map/ppermute | solution.py:306
  81.5 2.1 %copy-done.2 = bf16[16,3,320,128]{3,2,1,0:T(8,128)(2,1)S(1)} copy-done((bf16[16,3,320,128]{3,2,1,0:T(8,128)(2,1)S(1)}, bf16[16,3,320,128]{3,2,1,0:T(8,128)(2,1)}, u32[]{:S(2)}) %copy-start.2) | copy-done | bytes 3932184
  83.6 3.5 %text_attention.1 = (bf16[16,128,128]{2,1,0:T(8,128)(2,1)}, f32[8,128]{1,0:T(8,128)S(1)}) custom-call(f32[1,256]{1,0:T(1,128)S(1)} %get-tuple-element.69.bias_a, f32[1,256]{1,0:T(1,128)S(1)} %get-tuple-element.70.bias_c, bf16[16,3,320,128]{3,2,1,0:T(8,128)(2,1)S(1)} %copy-done.2, bf16[16,2,96,128]{3,2,1,0:T(8,128)(2,1)S(1)} %collective-permute-done.5.other), custom_call_target="tpu_custom_call" | custom-call | flops 872415232 | bytes 8388608 | tf_op jit(solution)/shard_map/text_attention/pallas_call | solution.py:373
  87.7 4.2 %all-to-all-start.1 = ((bf16[16,128,128]{2,1,0:T(8,128)(2,1)}), bf16[16,128,128]{2,1,0:T(8,128)(2,1)}, u32[]{:S(2)}, u32[]{:S(2)}) async-start(bf16[16,128,128]{2,1,0:T(8,128)(2,1)} %get-tuple-element.38), calls=%async_computation.1 | async-start | bytes 1048576 | tf_op jit(solution)/shard_map/all_to_all | solution.py:379
  92.0 1.3 collective-permute-start.6
  93.3 2.4 %collective-permute-start.7 = (bf16[256,384]{1,0:T(8,128)(2,1)S(1)}, bf16[256,384]{1,0:T(8,128)(2,1)S(1)}, u32[]{:S(2)}, u32[]{:S(2)}) collective-permute-start(bf16[256,384]{1,0:T(8,128)(2,1)S(1)} %copy-done.19), channel_id=1, source_target_pairs={{0,2},{1,3},{2,0},{3,1},{4,6},{5,7},{6,4},{7,5},{8,10},{9,11},{10,... | collective-permute-start | bytes 589832 | tf_op jit(solution)/shard_map/ppermute | solution.py:306
  95.9 2.5 %collective-permute-start.11 = (bf16[128,384]{1,0:T(8,128)(2,1)S(1)}, bf16[128,384]{1,0:T(8,128)(2,1)S(1)}, u32[]{:S(2)}, u32[]{:S(2)}) collective-permute-start(bf16[128,384]{1,0:T(8,128)(2,1)S(1)} %bitcast.70), channel_id=1, source_target_pairs={{0,12},{1,13},{2,14},{3,15},{4,8},{5,9},{6,10},{7,11},{8,4},{9,5},... | collective-permute-start | bytes 294920 | tf_op jit(solution)/shard_map/ppermute | solution.py:306
  98.4 2.1 %copy-done.3 = bf16[16,3,320,128]{3,2,1,0:T(8,128)(2,1)S(1)} copy-done((bf16[16,3,320,128]{3,2,1,0:T(8,128)(2,1)S(1)}, bf16[16,3,320,128]{3,2,1,0:T(8,128)(2,1)}, u32[]{:S(2)}) %copy-start.3) | copy-done | bytes 3932184
  100.6 12.9 %video_attention_a.1 = (bf16[16,192,128]{2,1,0:T(8,128)(2,1)S(1)}, f32[8,128]{1,0:T(8,128)S(1)}) custom-call(f32[1,256]{1,0:T(1,128)S(1)} %get-tuple-element.69.bias_a, bf16[16,3,320,128]{3,2,1,0:T(8,128)(2,1)S(1)} %copy-done.3, f32[8,128]{1,0:T(8,128)S(1)} %get-tuple-element.34._), custom_call_target="tpu_custom_call" | custom-call | flops 5234491392 | bytes 8388608 | tf_op jit(solution)/shard_map/video_attention_a/pallas_call | solution.py:381
  115.0 2.1 %slot_text.1 = (bf16[64,1024]{1,0:T(8,128)(2,1)}, f32[8,128]{1,0:T(8,128)}) custom-call(s32[32]{0:T(128)} %live.7, s32[1]{0:T(128)} %bitcast.core, s32[1]{0:T(128)} %bitcast.22.seat, bf16[16,128,128]{2,1,0:T(8,128)(2,1)} %all-to-all-done.1.got, f32[8,128]{1,0:T(8,128)} %copy-done.21, bf16[256,384]{1,0:T(8,128)(2,1)} %copy-done.7, ...), custom_call_target="tpu_custom_call" | custom-call | tf_op jit(solution)/shard_map/slot_text/pallas_call | solution.py:384
  117.1 0.7 collective-permute-start.12
  117.8 1.9 %collective-permute-start.13 = (bf16[64,1024]{1,0:T(8,128)(2,1)}, bf16[64,1024]{1,0:T(8,128)(2,1)S(1)}, u32[]{:S(2)}, u32[]{:S(2)}) collective-permute-start(bf16[64,1024]{1,0:T(8,128)(2,1)} %get-tuple-element.44), channel_id=1, source_target_pairs={{0,64},{16,80},{32,96},{48,112},{64,0},{80,16},{96,32},{112,48},{1... | collective-permute-start | bytes 393224 | tf_op jit(solution)/shard_map/ppermute | solution.py:306
  119.7 1.2 collective-permute-start.14
  120.9 2.1 %copy-done.4 = bf16[16,3,320,128]{3,2,1,0:T(8,128)(2,1)S(1)} copy-done((bf16[16,3,320,128]{3,2,1,0:T(8,128)(2,1)S(1)}, bf16[16,3,320,128]{3,2,1,0:T(8,128)(2,1)}, u32[]{:S(2)}) %copy-start.4) | copy-done | bytes 3932184
  123.8 7.9 %video_attention_c.1 = (bf16[16,288,128]{2,1,0:T(8,128)(2,1)}, f32[8,128]{1,0:T(8,128)}) custom-call(f32[1,256]{1,0:T(1,128)S(1)} %get-tuple-element.70.bias_c, bf16[16,3,320,128]{3,2,1,0:T(8,128)(2,1)S(1)} %copy-done.4, bf16[16,2,96,128]{3,2,1,0:T(8,128)(2,1)S(1)} %collective-permute-done.5.other, bf16[16,192,128]{2,1,0:T(8,128)(2,1)S(1)} %get-tuple-element.35.out_a, ...), custom_call_target="tpu_custom_call" | custom-call | flops 2617245696 | bytes 8388608 | tf_op jit(solution)/shard_map/video_attention_c/pallas_call | solution.py:390
  131.7 5.0 %all-to-all-start.2 = ((bf16[16,288,128]{2,1,0:T(8,128)(2,1)}), bf16[16,288,128]{2,1,0:T(8,128)(2,1)}, u32[]{:S(2)}, u32[]{:S(2)}) async-start(bf16[16,288,128]{2,1,0:T(8,128)(2,1)} %get-tuple-element.50), calls=%async_computation.2 | async-start | bytes 2359296 | tf_op jit(solution)/shard_map/all_to_all | solution.py:396
  136.7 3.8 %collective-permute-start.15 = (bf16[4,64,1024]{2,1,0:T(8,128)(2,1)S(1)}, bf16[4,64,1024]{2,1,0:T(8,128)(2,1)S(1)}, u32[]{:S(2)}, u32[]{:S(2)}) collective-permute-start(bf16[4,64,1024]{2,1,0:T(8,128)(2,1)S(1)} %pad_maximum_fusion.near), channel_id=1, source_target_pairs={{0,16},{16,0},{32,48},{48,32},{64,80},{80,64},{96,112},{112,96},{1... | collective-permute-start | bytes 1572872 | tf_op jit(solution)/shard_map/ppermute | solution.py:306
  140.5 1.5 collective-permute-done.15.far
  142.1 1.3 project.1
  143.4 1.6 collective-permute-start.16
  145.0 2.4 %collective-permute-start.17 = (bf16[8,16,384]{2,1,0:T(8,128)(2,1)S(1)}, bf16[8,16,384]{2,1,0:T(8,128)(2,1)S(1)}, u32[]{:S(2)}, u32[]{:S(2)}) collective-permute-start(bf16[8,16,384]{2,1,0:T(8,128)(2,1)S(1)} %get-tuple-element.48), channel_id=1, source_target_pairs={{0,8},{1,9},{2,10},{3,11},{4,12},{5,13},{6,14},{7,15},{8,0},{9,1},... | collective-permute-start | bytes 294920 | tf_op jit(solution)/shard_map/ppermute | solution.py:306
  147.5 1.4 collective-permute-start.23
  148.9 2.4 %collective-permute-start.24 = (bf16[256,384]{1,0:T(8,128)(2,1)S(1)}, bf16[256,384]{1,0:T(8,128)(2,1)S(1)}, u32[]{:S(2)}, u32[]{:S(2)}) collective-permute-start(bf16[256,384]{1,0:T(8,128)(2,1)S(1)} %get-tuple-element.55), channel_id=1, source_target_pairs={{0,2},{1,3},{2,0},{3,1},{4,6},{5,7},{6,4},{7,5},{8,10},{9,11},{10,... | collective-permute-start | bytes 589832 | tf_op jit(solution)/shard_map/ppermute | solution.py:306
  151.3 2.5 %collective-permute-done.16 = bf16[8,16,384]{2,1,0:T(8,128)(2,1)S(1)} collective-permute-done((bf16[8,16,384]{2,1,0:T(8,128)(2,1)S(1)}, bf16[8,16,384]{2,1,0:T(8,128)(2,1)S(1)}, u32[]{:S(2)}, u32[]{:S(2)}) %collective-permute-start.16) | collective-permute-done | bytes 98336 | tf_op jit(solution)/shard_map/ppermute | solution.py:306
  153.8 2.4 %collective-permute-start.25 = (bf16[256,384]{1,0:T(8,128)(2,1)S(1)}, bf16[256,384]{1,0:T(8,128)(2,1)S(1)}, u32[]{:S(2)}, u32[]{:S(2)}) collective-permute-start(bf16[256,384]{1,0:T(8,128)(2,1)S(1)} %get-tuple-element.56), channel_id=1, source_target_pairs={{0,3},{1,2},{2,1},{3,0},{4,7},{5,6},{6,5},{7,4},{8,11},{9,10},{10,... | collective-permute-start | bytes 589832 | tf_op jit(solution)/shard_map/ppermute | solution.py:306
  156.9 1.6 collective-permute-done.18
  158.6 1.4 collective-permute-start.20
  160.0 3.1 %collective-permute-done.20 = bf16[1,4,16,384]{3,2,1,0:T(8,128)(2,1)S(1)} collective-permute-done((bf16[1,4,16,384]{3,2,1,0:T(8,128)(2,1)S(1)}, bf16[1,4,16,384]{3,2,1,0:T(8,128)(2,1)S(1)}, u32[]{:S(2)}, u32[]{:S(2)}) %collective-permute-start.20) | collective-permute-done | bytes 49184 | tf_op jit(solution)/shard_map/ppermute | solution.py:306
  163.3 1.0 collective-permute-done.25
  164.3 0.8 convert_add_fusion
  165.1 1.0 slice.63
  166.2 3.1 %collective-permute-start.22 = (bf16[4,1,16,384]{3,2,0,1:T(8,128)(2,1)S(1)}, bf16[4,1,16,384]{3,2,0,1:T(8,128)(2,1)S(1)}, u32[]{:S(2)}, u32[]{:S(2)}) collective-permute-start(bf16[4,1,16,384]{3,2,0,1:T(8,128)(2,1)S(1)} %get-tuple-element.58), channel_id=1, source_target_pairs={{0,16},{16,0},{32,48},{48,32},{64,80},{80,64},{96,112},{112,96},{1... | collective-permute-start | bytes 147464 | tf_op jit(solution)/shard_map/ppermute | solution.py:306
  169.4 0.8 collective-permute-done.22
  171.7 3.3 %slot_video.1 = bf16[192,4096]{1,0:T(8,128)(2,1)} custom-call(s32[32]{0:T(128)} %live.7, s32[1]{0:T(128)} %bitcast.core, bf16[16,288,128]{2,1,0:T(8,128)(2,1)} %all-to-all-done.2.got, bf16[8,96,128]{2,1,0:T(8,128)(2,1)} %copy-done.24), custom_call_target="tpu_custom_call" | custom-call | tf_op jit(solution)/shard_map/slot_video/pallas_call | solution.py:415
  (100 shorter events, 6.5 us)
Async XLA Ops:
  0.6 10.7 %copy-start.6 = (bf16[1,16,3,4096]{3,1,2,0:T(8,128)(2,1)S(1)}, bf16[1,16,3,4096]{3,1,2,0:T(8,128)(2,1)}, u32[]{:S(2)}) copy-start(bf16[1,16,3,4096]{3,1,2,0:T(8,128)(2,1)} %param.7) | copy-start | bytes 1179652
  0.6 10.7 %copy-start.20 = (s32[32]{0:T(128)S(1)}, s32[32]{0:T(128)}, u32[]{:S(2)}) copy-start(s32[32]{0:T(128)} %live.7) | copy-start | bytes 388
  1.8 8.8 %collective-permute-start.1 = (bf16[1,4,16,384]{3,2,1,0:T(8,128)(2,1)S(1)}, bf16[1,4,16,384]{3,2,1,0:T(8,128)(2,1)S(1)}, u32[]{:S(2)}, u32[]{:S(2)}) collective-permute-start(bf16[1,4,16,384]{3,2,1,0:T(8,128)(2,1)S(1)} %get-tuple-element.68), channel_id=1, source_target_pairs={{0,64},{16,80},{32,96},{48,112},{64,0},{80,16},{96,32},{112,48},{1... | collective-permute-start | bytes 147464 | tf_op jit(solution)/shard_map/ppermute | solution.py:306
  9.5 9.6 %collective-permute-start = (bf16[8,3,112,128]{3,2,1,0:T(8,128)(2,1)}, bf16[8,3,112,128]{3,2,1,0:T(8,128)(2,1)S(1)}, u32[]{:S(2)}, u32[]{:S(2)}) collective-permute-start(bf16[8,3,112,128]{3,2,1,0:T(8,128)(2,1)} %give.1), channel_id=1, source_target_pairs={{0,16},{16,0},{32,48},{48,32},{64,80},{80,64},{96,112},{112,96},{1... | collective-permute-start | bytes 2064392 | tf_op jit(solution)/shard_map/ppermute | solution.py:306
  10.5 7.1 %collective-permute-start.2 = (bf16[2,2,16,384]{3,2,1,0:T(8,128)(2,1)S(1)}, bf16[2,2,16,384]{3,2,1,0:T(8,128)(2,1)S(1)}, u32[]{:S(2)}, u32[]{:S(2)}) collective-permute-start(bf16[2,2,16,384]{3,2,1,0:T(8,128)(2,1)S(1)} %get-tuple-element.66), channel_id=1, source_target_pairs={{0,32},{16,48},{32,0},{48,16},{64,96},{80,112},{96,64},{112,80},{1... | collective-permute-start | bytes 147464 | tf_op jit(solution)/shard_map/ppermute | solution.py:306
  11.4 2.3 %copy-start.5 = (bf16[1,192,3,4096]{3,1,2,0:T(8,128)(2,1)S(1)}, bf16[1,192,3,4096]{3,1,2,0:T(8,128)(2,1)}, u32[]{:S(2)}) copy-start(bf16[1,192,3,4096]{3,1,2,0:T(8,128)(2,1)} %param.6) | copy-start | bytes 14155780
  13.7 4.4 %copy-start.26 = (s32[1,256]{1,0:T(1,128)S(1)}, s32[1,256]{1,0:T(1,128)}, u32[]{:S(2)}) copy-start(s32[1,256]{1,0:T(1,128)} %param.9) | copy-start | bytes 3076
  15.8 1.9 %copy-start = (bf16[16,3,320,128]{3,2,1,0:T(8,128)(2,1)}, bf16[16,3,320,128]{3,2,1,0:T(8,128)(2,1)S(1)}, u32[]{:S(2)}) copy-start(bf16[16,3,320,128]{3,2,1,0:T(8,128)(2,1)S(1)} %pack.1._) | copy-start | bytes 11796484
  17.7 1.3 collective-permute-start.4
  18.1 3.8 %collective-permute-start.3 = (s32[1,256]{1,0:T(1,128)S(1)}, s32[1,256]{1,0:T(1,128)S(1)}, u32[]{:S(2)}, u32[]{:S(2)}) collective-permute-start(s32[1,256]{1,0:T(1,128)S(1)} %copy-done.26), channel_id=1, source_target_pairs={{0,16},{16,0},{32,48},{48,32},{64,80},{80,64},{96,112},{112,96},{1... | collective-permute-start | bytes 3080 | tf_op jit(solution)/shard_map/ppermute | solution.py:306
  19.1 0.8 copy-start.23
  76.2 15.7 %copy-start.19 = (bf16[256,384]{1,0:T(8,128)(2,1)S(1)}, bf16[256,384]{1,0:T(8,128)(2,1)}, u32[]{:S(2)}) copy-start(bf16[256,384]{1,0:T(8,128)(2,1)} %w0) | copy-start | bytes 589828
  76.3 1.9 %copy-start.1 = (bf16[16,3,320,128]{3,2,1,0:T(8,128)(2,1)}, bf16[16,3,320,128]{3,2,1,0:T(8,128)(2,1)S(1)}, u32[]{:S(2)}) copy-start(bf16[16,3,320,128]{3,2,1,0:T(8,128)(2,1)S(1)} %all_to_all.15.recv) | copy-start | bytes 11796484
  78.2 3.3 %collective-permute-start.5 = (bf16[16,2,96,128]{3,2,1,0:T(8,128)(2,1)S(1)}, bf16[16,2,96,128]{3,2,1,0:T(8,128)(2,1)S(1)}, u32[]{:S(2)}, u32[]{:S(2)}) collective-permute-start(bf16[16,2,96,128]{3,2,1,0:T(8,128)(2,1)S(1)} %slice.62), channel_id=1, source_target_pairs={{0,16},{16,0},{32,48},{48,32},{64,80},{80,64},{96,112},{112,96},{1... | collective-permute-start | bytes 2359304 | tf_op jit(solution)/shard_map/ppermute | solution.py:306
  81.5 2.1 %copy-start.2 = (bf16[16,3,320,128]{3,2,1,0:T(8,128)(2,1)S(1)}, bf16[16,3,320,128]{3,2,1,0:T(8,128)(2,1)}, u32[]{:S(2)}) copy-start(bf16[16,3,320,128]{3,2,1,0:T(8,128)(2,1)} %copy-done.1) | copy-start | bytes 11796484
  87.1 11.3 %collective-permute-start.10 = (bf16[128,384]{1,0:T(8,128)(2,1)S(1)}, bf16[128,384]{1,0:T(8,128)(2,1)S(1)}, u32[]{:S(2)}, u32[]{:S(2)}) collective-permute-start(bf16[128,384]{1,0:T(8,128)(2,1)S(1)} %bitcast.69), channel_id=1, source_target_pairs={{0,8},{1,9},{2,10},{3,11},{4,12},{5,13},{6,14},{7,15},{8,0},{9,1},... | collective-permute-start | bytes 294920 | tf_op jit(solution)/shard_map/ppermute | solution.py:306
  87.7 26.5 %all-to-all-start.1 = ((bf16[16,128,128]{2,1,0:T(8,128)(2,1)}), bf16[16,128,128]{2,1,0:T(8,128)(2,1)}, u32[]{:S(2)}, u32[]{:S(2)}) async-start(bf16[16,128,128]{2,1,0:T(8,128)(2,1)} %get-tuple-element.38), calls=%async_computation.1 | async-start | bytes 1048576 | tf_op jit(solution)/shard_map/all_to_all | solution.py:379
  92.0 22.2 %collective-permute-start.6 = (bf16[256,384]{1,0:T(8,128)(2,1)S(1)}, bf16[256,384]{1,0:T(8,128)(2,1)S(1)}, u32[]{:S(2)}, u32[]{:S(2)}) collective-permute-start(bf16[256,384]{1,0:T(8,128)(2,1)S(1)} %copy-done.19), channel_id=1, source_target_pairs={{0,1},{1,0},{2,3},{3,2},{4,5},{5,4},{6,7},{7,6},{8,9},{9,8},{10,11... | collective-permute-start | bytes 589832 | tf_op jit(solution)/shard_map/ppermute | solution.py:306
  93.3 20.8 %collective-permute-start.7 = (bf16[256,384]{1,0:T(8,128)(2,1)S(1)}, bf16[256,384]{1,0:T(8,128)(2,1)S(1)}, u32[]{:S(2)}, u32[]{:S(2)}) collective-permute-start(bf16[256,384]{1,0:T(8,128)(2,1)S(1)} %copy-done.19), channel_id=1, source_target_pairs={{0,2},{1,3},{2,0},{3,1},{4,6},{5,7},{6,4},{7,5},{8,10},{9,11},{10,... | collective-permute-start | bytes 589832 | tf_op jit(solution)/shard_map/ppermute | solution.py:306
  95.7 18.5 %collective-permute-start.8 = (bf16[256,384]{1,0:T(8,128)(2,1)S(1)}, bf16[256,384]{1,0:T(8,128)(2,1)S(1)}, u32[]{:S(2)}, u32[]{:S(2)}) collective-permute-start(bf16[256,384]{1,0:T(8,128)(2,1)S(1)} %copy-done.19), channel_id=1, source_target_pairs={{0,3},{1,2},{2,1},{3,0},{4,7},{5,6},{6,5},{7,4},{8,11},{9,10},{10,... | collective-permute-start | bytes 589832 | tf_op jit(solution)/shard_map/ppermute | solution.py:306
  95.9 18.2 %collective-permute-start.11 = (bf16[128,384]{1,0:T(8,128)(2,1)S(1)}, bf16[128,384]{1,0:T(8,128)(2,1)S(1)}, u32[]{:S(2)}, u32[]{:S(2)}) collective-permute-start(bf16[128,384]{1,0:T(8,128)(2,1)S(1)} %bitcast.70), channel_id=1, source_target_pairs={{0,12},{1,13},{2,14},{3,15},{4,8},{5,9},{6,10},{7,11},{8,4},{9,5},... | collective-permute-start | bytes 294920 | tf_op jit(solution)/shard_map/ppermute | solution.py:306
  98.4 15.1 %copy-start.13 = (bf16[128,384]{1,0:T(8,128)(2,1)}, bf16[128,384]{1,0:T(8,128)(2,1)S(1)}, u32[]{:S(2)}) copy-start(bf16[128,384]{1,0:T(8,128)(2,1)S(1)} %collective-permute-done.10.rest_5_.c2) | copy-start | bytes 294916
  98.4 15.7 %collective-permute-start.9 = (bf16[128,384]{1,0:T(8,128)(2,1)S(1)}, bf16[128,384]{1,0:T(8,128)(2,1)S(1)}, u32[]{:S(2)}, u32[]{:S(2)}) collective-permute-start(bf16[128,384]{1,0:T(8,128)(2,1)S(1)} %bitcast.71), channel_id=1, source_target_pairs={{0,4},{1,5},{2,6},{3,7},{4,0},{5,1},{6,2},{7,3},{8,12},{9,13},{10,... | collective-permute-start | bytes 294920 | tf_op jit(solution)/shard_map/ppermute | solution.py:306
  98.4 2.2 %copy-start.3 = (bf16[16,3,320,128]{3,2,1,0:T(8,128)(2,1)S(1)}, bf16[16,3,320,128]{3,2,1,0:T(8,128)(2,1)}, u32[]{:S(2)}) copy-start(bf16[16,3,320,128]{3,2,1,0:T(8,128)(2,1)} %copy-done.1) | copy-start | bytes 11796484
  114.2 0.8 copy-start.11
  117.1 14.6 %collective-permute-start.12 = (bf16[64,1024]{1,0:T(8,128)(2,1)}, bf16[64,1024]{1,0:T(8,128)(2,1)S(1)}, u32[]{:S(2)}, u32[]{:S(2)}) collective-permute-start(bf16[64,1024]{1,0:T(8,128)(2,1)} %get-tuple-element.44), channel_id=1, source_target_pairs={{0,32},{16,48},{32,0},{48,16},{64,96},{80,112},{96,64},{112,80},{1... | collective-permute-start | bytes 393224 | tf_op jit(solution)/shard_map/ppermute | solution.py:306
  117.8 13.9 %collective-permute-start.13 = (bf16[64,1024]{1,0:T(8,128)(2,1)}, bf16[64,1024]{1,0:T(8,128)(2,1)S(1)}, u32[]{:S(2)}, u32[]{:S(2)}) collective-permute-start(bf16[64,1024]{1,0:T(8,128)(2,1)} %get-tuple-element.44), channel_id=1, source_target_pairs={{0,64},{16,80},{32,96},{48,112},{64,0},{80,16},{96,32},{112,48},{1... | collective-permute-start | bytes 393224 | tf_op jit(solution)/shard_map/ppermute | solution.py:306
  119.7 11.9 %collective-permute-start.14 = (bf16[64,1024]{1,0:T(8,128)(2,1)}, bf16[64,1024]{1,0:T(8,128)(2,1)S(1)}, u32[]{:S(2)}, u32[]{:S(2)}) collective-permute-start(bf16[64,1024]{1,0:T(8,128)(2,1)} %get-tuple-element.44), channel_id=1, source_target_pairs={{0,96},{16,112},{32,64},{48,80},{64,32},{80,48},{96,0},{112,16},{1... | collective-permute-start | bytes 393224 | tf_op jit(solution)/shard_map/ppermute | solution.py:306
  120.9 2.1 %copy-start.4 = (bf16[16,3,320,128]{3,2,1,0:T(8,128)(2,1)S(1)}, bf16[16,3,320,128]{3,2,1,0:T(8,128)(2,1)}, u32[]{:S(2)}) copy-start(bf16[16,3,320,128]{3,2,1,0:T(8,128)(2,1)} %copy-done.1) | copy-start | bytes 11796484
  123.7 7.9 %copy-start.25 = (bf16[64,1024]{1,0:T(8,128)(2,1)S(1)}, bf16[64,1024]{1,0:T(8,128)(2,1)}, u32[]{:S(2)}) copy-start(bf16[64,1024]{1,0:T(8,128)(2,1)} %get-tuple-element.44) | copy-start | bytes 393220
  123.7 18.4 %copy-start.8 = (bf16[256,384]{1,0:T(8,128)(2,1)S(1)}, bf16[256,384]{1,0:T(8,128)(2,1)}, u32[]{:S(2)}) copy-start(bf16[256,384]{1,0:T(8,128)(2,1)} %copy-done.7) | copy-start | bytes 589828
  123.7 18.4 %copy-start.10 = (bf16[256,384]{1,0:T(8,128)(2,1)S(1)}, bf16[256,384]{1,0:T(8,128)(2,1)}, u32[]{:S(2)}) copy-start(bf16[256,384]{1,0:T(8,128)(2,1)} %copy-done.9) | copy-start | bytes 589828
  123.7 18.4 %copy-start.12 = (bf16[256,384]{1,0:T(8,128)(2,1)S(1)}, bf16[256,384]{1,0:T(8,128)(2,1)}, u32[]{:S(2)}) copy-start(bf16[256,384]{1,0:T(8,128)(2,1)} %copy-done.11) | copy-start | bytes 589828
  123.7 18.4 %copy-start.14 = (bf16[128,384]{1,0:T(8,128)(2,1)S(1)}, bf16[128,384]{1,0:T(8,128)(2,1)}, u32[]{:S(2)}) copy-start(bf16[128,384]{1,0:T(8,128)(2,1)} %copy-done.13) | copy-start | bytes 294916
  123.7 18.4 %copy-start.16 = (bf16[128,384]{1,0:T(8,128)(2,1)S(1)}, bf16[128,384]{1,0:T(8,128)(2,1)}, u32[]{:S(2)}) copy-start(bf16[128,384]{1,0:T(8,128)(2,1)} %copy-done.15) | copy-start | bytes 294916
  123.8 18.4 %copy-start.18 = (bf16[128,384]{1,0:T(8,128)(2,1)S(1)}, bf16[128,384]{1,0:T(8,128)(2,1)}, u32[]{:S(2)}) copy-start(bf16[128,384]{1,0:T(8,128)(2,1)} %copy-done.17) | copy-start | bytes 294916
  131.7 26.8 %all-to-all-start.2 = ((bf16[16,288,128]{2,1,0:T(8,128)(2,1)}), bf16[16,288,128]{2,1,0:T(8,128)(2,1)}, u32[]{:S(2)}, u32[]{:S(2)}) async-start(bf16[16,288,128]{2,1,0:T(8,128)(2,1)} %get-tuple-element.50), calls=%async_computation.2 | async-start | bytes 2359296 | tf_op jit(solution)/shard_map/all_to_all | solution.py:396
  136.7 5.4 %collective-permute-start.15 = (bf16[4,64,1024]{2,1,0:T(8,128)(2,1)S(1)}, bf16[4,64,1024]{2,1,0:T(8,128)(2,1)S(1)}, u32[]{:S(2)}, u32[]{:S(2)}) collective-permute-start(bf16[4,64,1024]{2,1,0:T(8,128)(2,1)S(1)} %pad_maximum_fusion.near), channel_id=1, source_target_pairs={{0,16},{16,0},{32,48},{48,32},{64,80},{80,64},{96,112},{112,96},{1... | collective-permute-start | bytes 1572872 | tf_op jit(solution)/shard_map/ppermute | solution.py:306
  143.4 10.4 %collective-permute-start.16 = (bf16[8,16,384]{2,1,0:T(8,128)(2,1)S(1)}, bf16[8,16,384]{2,1,0:T(8,128)(2,1)S(1)}, u32[]{:S(2)}, u32[]{:S(2)}) collective-permute-start(bf16[8,16,384]{2,1,0:T(8,128)(2,1)S(1)} %get-tuple-element.47), channel_id=1, source_target_pairs={{0,4},{1,5},{2,6},{3,7},{4,0},{5,1},{6,2},{7,3},{8,12},{9,13},{10,... | collective-permute-start | bytes 294920 | tf_op jit(solution)/shard_map/ppermute | solution.py:306
  145.0 11.9 %collective-permute-start.17 = (bf16[8,16,384]{2,1,0:T(8,128)(2,1)S(1)}, bf16[8,16,384]{2,1,0:T(8,128)(2,1)S(1)}, u32[]{:S(2)}, u32[]{:S(2)}) collective-permute-start(bf16[8,16,384]{2,1,0:T(8,128)(2,1)S(1)} %get-tuple-element.48), channel_id=1, source_target_pairs={{0,8},{1,9},{2,10},{3,11},{4,12},{5,13},{6,14},{7,15},{8,0},{9,1},... | collective-permute-start | bytes 294920 | tf_op jit(solution)/shard_map/ppermute | solution.py:306
  147.4 11.1 %collective-permute-start.18 = (bf16[8,16,384]{2,1,0:T(8,128)(2,1)S(1)}, bf16[8,16,384]{2,1,0:T(8,128)(2,1)S(1)}, u32[]{:S(2)}, u32[]{:S(2)}) collective-permute-start(bf16[8,16,384]{2,1,0:T(8,128)(2,1)S(1)} %get-tuple-element.49), channel_id=1, source_target_pairs={{0,12},{1,13},{2,14},{3,15},{4,8},{5,9},{6,10},{7,11},{8,4},{9,5},... | collective-permute-start | bytes 294920 | tf_op jit(solution)/shard_map/ppermute | solution.py:306
  147.5 15.7 %collective-permute-start.23 = (bf16[256,384]{1,0:T(8,128)(2,1)S(1)}, bf16[256,384]{1,0:T(8,128)(2,1)S(1)}, u32[]{:S(2)}, u32[]{:S(2)}) collective-permute-start(bf16[256,384]{1,0:T(8,128)(2,1)S(1)} %get-tuple-element.54), channel_id=1, source_target_pairs={{0,1},{1,0},{2,3},{3,2},{4,5},{5,4},{6,7},{7,6},{8,9},{9,8},{10,11... | collective-permute-start | bytes 589832 | tf_op jit(solution)/shard_map/ppermute | solution.py:306
  148.9 14.4 %collective-permute-start.24 = (bf16[256,384]{1,0:T(8,128)(2,1)S(1)}, bf16[256,384]{1,0:T(8,128)(2,1)S(1)}, u32[]{:S(2)}, u32[]{:S(2)}) collective-permute-start(bf16[256,384]{1,0:T(8,128)(2,1)S(1)} %get-tuple-element.55), channel_id=1, source_target_pairs={{0,2},{1,3},{2,0},{3,1},{4,6},{5,7},{6,4},{7,5},{8,10},{9,11},{10,... | collective-permute-start | bytes 589832 | tf_op jit(solution)/shard_map/ppermute | solution.py:306
  153.8 10.5 %collective-permute-start.25 = (bf16[256,384]{1,0:T(8,128)(2,1)S(1)}, bf16[256,384]{1,0:T(8,128)(2,1)S(1)}, u32[]{:S(2)}, u32[]{:S(2)}) collective-permute-start(bf16[256,384]{1,0:T(8,128)(2,1)S(1)} %get-tuple-element.56), channel_id=1, source_target_pairs={{0,3},{1,2},{2,1},{3,0},{4,7},{5,6},{6,5},{7,4},{8,11},{9,10},{10,... | collective-permute-start | bytes 589832 | tf_op jit(solution)/shard_map/ppermute | solution.py:306
  158.6 4.5 %collective-permute-start.20 = (bf16[1,4,16,384]{3,2,1,0:T(8,128)(2,1)S(1)}, bf16[1,4,16,384]{3,2,1,0:T(8,128)(2,1)S(1)}, u32[]{:S(2)}, u32[]{:S(2)}) collective-permute-start(bf16[1,4,16,384]{3,2,1,0:T(8,128)(2,1)S(1)} %get-tuple-element.62), channel_id=1, source_target_pairs={{0,64},{16,80},{32,96},{48,112},{64,0},{80,16},{96,32},{112,48},{1... | collective-permute-start | bytes 147464 | tf_op jit(solution)/shard_map/ppermute | solution.py:306
  163.1 3.0 %collective-permute-start.21 = (bf16[2,2,16,384]{3,2,1,0:T(8,128)(2,1)S(1)}, bf16[2,2,16,384]{3,2,1,0:T(8,128)(2,1)S(1)}, u32[]{:S(2)}, u32[]{:S(2)}) collective-permute-start(bf16[2,2,16,384]{3,2,1,0:T(8,128)(2,1)S(1)} %get-tuple-element.60), channel_id=1, source_target_pairs={{0,32},{16,48},{32,0},{48,16},{64,96},{80,112},{96,64},{112,80},{1... | collective-permute-start | bytes 147464 | tf_op jit(solution)/shard_map/ppermute | solution.py:306
  166.2 4.0 %collective-permute-start.22 = (bf16[4,1,16,384]{3,2,0,1:T(8,128)(2,1)S(1)}, bf16[4,1,16,384]{3,2,0,1:T(8,128)(2,1)S(1)}, u32[]{:S(2)}, u32[]{:S(2)}) collective-permute-start(bf16[4,1,16,384]{3,2,0,1:T(8,128)(2,1)S(1)} %get-tuple-element.58), channel_id=1, source_target_pairs={{0,16},{16,0},{32,48},{48,32},{64,80},{80,64},{96,112},{112,96},{1... | collective-permute-start | bytes 147464 | tf_op jit(solution)/shard_map/ppermute | solution.py:306
  169.3 1.7 collective-permute-start.19
  (7 other events, 4.7 us)
